TPU v7x, 256 devices: a whole 4x4x8 slice. The times are simulated.
256 devices in a mesh: grp: 8 (over z), seg: 32 (over x, y, core).
Axes of the slice: x: 4, y: 4, z: 8, core: 2. Of those that a mesh axis runs over, the one named last changes fastest.
Arguments:
- tokens: bfloat16 [98304, 768], P(('grp', 'seg')), may hold values from -6 to 6
- doc_segments: int32 [8, 6], P('grp'), may hold values from 1 to 48, 96 in all within a row
- local_qkv: bfloat16 [768, 2304], P('seg'), may hold values from -0.21875 to 0.21875
- local_out: bfloat16 [768, 768], P('seg'), may hold values from -0.875 to 0.875
- local_up: bfloat16 [768, 3072], P('seg'), may hold values from -0.21875 to 0.21875
- local_down: bfloat16 [3072, 768], P('seg'), may hold values from -0.109375 to 0.109375
- local_bias: bfloat16 [6, 768], P(None, 'seg'), may hold values from -1.5 to 1.5
- local_upbias: bfloat16 [3072], P('seg'), may hold values from -1.5 to 1.5
- local_gains: bfloat16 [2, 768], P(None, 'seg'), may hold values from 0.5 to 1.5
- cross_qkv: bfloat16 [768, 2304], P('seg'), may hold values from -0.21875 to 0.21875
- cross_out: bfloat16 [768, 768], P('seg'), may hold values from -0.625 to 0.625
- cross_up: bfloat16 [768, 3072], P('seg'), may hold values from -0.21875 to 0.21875
- cross_down: bfloat16 [3072, 768], P('seg'), may hold values from -0.109375 to 0.109375
- cross_bias: bfloat16 [6, 768], P(None, 'seg'), may hold values from -1.5 to 1.5
- cross_upbias: bfloat16 [3072], P('seg'), may hold values from -1.5 to 1.5
- cross_gains: bfloat16 [2, 768], P(None, 'seg'), may hold values from 0.5 to 1.5
- pos_table: bfloat16 [64, 768], P('seg'), may hold values from -3 to 3
- cotangent: bfloat16 [98304, 768], P(('grp', 'seg')), may hold values from -6 to 6
Outputs:
- layer_out: bfloat16 [98304, 768], P(('grp', 'seg'))
- tokens_grad: float32 [98304, 768], P(('grp', 'seg'))
- local_qkv_grad: float32 [768, 2304], P('seg')
- local_out_grad: float32 [768, 768], P('seg')
- local_up_grad: float32 [768, 3072], P('seg')
- local_down_grad: float32 [3072, 768], P('seg')
- local_bias_grad: float32 [6, 768], P(None, 'seg')
- local_upbias_grad: float32 [3072], P('seg')
- local_gains_grad: float32 [2, 768], P(None, 'seg')
- cross_qkv_grad: float32 [768, 2304], P('seg')
- cross_out_grad: float32 [768, 768], P('seg')
- cross_up_grad: float32 [768, 3072], P('seg')
- cross_down_grad: float32 [3072, 768], P('seg')
- cross_bias_grad: float32 [6, 768], P(None, 'seg')
- cross_upbias_grad: float32 [3072], P('seg')
- cross_gains_grad: float32 [2, 768], P(None, 'seg')
- pos_table_grad: float32 [64, 768], P('seg')
Inputs may be any that keep to these rules, and one draw needn't show every extreme that they name: `doc_segments`: each row lists the segment counts of a group's 6 documents in document order; a row sums to 96 and its largest count is exactly 48.
All inputs are finite; a program needn't handle non-finite values.
Results may differ from a plain program's by a relative error of at most 0.029.
Values may be sent and summed in bfloat16 or wider, within the bound.
A program may use at most 128 MiB of HBM per device.

v0:
```python
import math

import jax
import jax.numpy as jnp
from jax import lax
from jax.sharding import PartitionSpec as P

D = 768
H = 12
HD = 64
SEG_LEN = 128
POSN = 64


HIGHEST = lax.Precision.HIGHEST


def layer_norm(values, gain_vec, shift_vec):
    center = values - jnp.mean(values, axis=-1, keepdims=True)
    spread = jnp.mean(center * center, axis=-1, keepdims=True)
    return center * lax.rsqrt(spread + 1e-05) * gain_vec + shift_vec


def gelu_exact(values):
    return jax.nn.gelu(values, approximate=False)


def slot_layout(counts, segs_dev, seg_count):
    slot_ids = jnp.arange(segs_dev * seg_count, dtype=jnp.int32)
    doc_order = slot_ids % segs_dev * seg_count + slot_ids // segs_dev
    doc_ends = jnp.cumsum(counts)
    doc_starts = doc_ends - counts
    member_of = (doc_order[:, None] >= doc_starts[None, :]) & (
        doc_order[:, None] < doc_ends[None, :]
    )
    numbers = jnp.arange(counts.shape[0], dtype=jnp.int32)
    doc_ids = jnp.sum(jnp.where(member_of, numbers[None, :], 0), axis=1)
    seg_place = doc_order - jnp.sum(jnp.where(member_of, doc_starts[None, :], 0), axis=1)
    return (doc_ids, seg_place)


def project(inputs_b, weights):
    joined = jnp.dot(inputs_b, weights[0], preferred_element_type=jnp.float32)
    biases = weights[4]
    queries = (joined[:, :D] + biases[0]).astype(jnp.bfloat16)
    key_rows = joined[:, D : 2 * D].astype(jnp.bfloat16)
    value_rows = (joined[:, 2 * D :] + biases[1]).astype(jnp.bfloat16)
    return (queries, key_rows, value_rows)


def attend(queries, key_rows, value_rows, allowed):
    scores = jnp.einsum(
        "bqhe,bkhe->bhqk", queries, key_rows, preferred_element_type=jnp.float32
    ) * (1.0 / math.sqrt(HD))
    if allowed is not None:
        scores = jnp.where(allowed[:, None], scores, -1e30)
    row_max = jnp.max(scores, axis=-1, keepdims=True)
    exp_scores = jnp.exp(scores - row_max)
    row_sum = jnp.sum(exp_scores, axis=-1, keepdims=True)
    weights_b = (exp_scores / row_sum).astype(jnp.bfloat16)
    mixed_rows = jnp.einsum(
        "bhqk,bkhe->bqhe", weights_b, value_rows, preferred_element_type=jnp.float32
    )
    return (mixed_rows.astype(jnp.bfloat16), row_max + jnp.log(row_sum))


def attend_back(queries, key_rows, value_rows, allowed, log_total, grad_mixed):
    scale_f = 1.0 / math.sqrt(HD)
    scores = (
        jnp.einsum("bqhe,bkhe->bhqk", queries, key_rows, preferred_element_type=jnp.float32)
        * scale_f
    )
    if allowed is not None:
        scores = jnp.where(allowed[:, None], scores, -1e30)
    weights_f = jnp.exp(scores - log_total)
    grad_weights = jnp.einsum(
        "bqhe,bkhe->bhqk", grad_mixed, value_rows, preferred_element_type=jnp.float32
    )
    grad_scores = weights_f * (
        grad_weights - jnp.sum(weights_f * grad_weights, axis=-1, keepdims=True)
    )
    grad_scores = grad_scores.astype(jnp.bfloat16)
    grad_queries = (
        jnp.einsum("bhqk,bkhe->bqhe", grad_scores, key_rows, preferred_element_type=jnp.float32)
        * scale_f
    )
    grad_keys = (
        jnp.einsum("bhqk,bqhe->bkhe", grad_scores, queries, preferred_element_type=jnp.float32)
        * scale_f
    )
    grad_values = jnp.einsum(
        "bhqk,bqhe->bkhe",
        weights_f.astype(jnp.bfloat16),
        grad_mixed,
        preferred_element_type=jnp.float32,
    )
    return (grad_queries, grad_keys, grad_values)


def tail_ahead(inputs_f, mixed_rows, weights):
    w_qkv, w_out, w_up, w_down, biases, up_bias, gains = weights
    first_sum = (
        inputs_f + jnp.dot(mixed_rows, w_out, preferred_element_type=jnp.float32) + biases[2]
    )
    first_norm = layer_norm(first_sum, gains[0], biases[3]).astype(jnp.bfloat16)
    up_pre = jnp.dot(first_norm, w_up, preferred_element_type=jnp.float32) + up_bias
    active = gelu_exact(up_pre).astype(jnp.bfloat16)
    second_sum = (
        first_norm.astype(jnp.float32)
        + jnp.dot(active, w_down, preferred_element_type=jnp.float32)
        + biases[4]
    )
    output = layer_norm(second_sum, gains[1], biases[5])
    return (output, (first_sum, first_norm, up_pre, active, second_sum))


def tail_back(grad_out, mixed_rows, weights, saved):
    w_qkv, w_out, w_up, w_down, biases, up_bias, gains = weights
    first_sum, first_norm, up_pre, active, second_sum = saved
    _, second_pull = jax.vjp(
        layer_norm, second_sum, gains[1].astype(jnp.float32), biases[5].astype(jnp.float32)
    )
    grad_second, gain_two, shift_two = second_pull(grad_out)
    down_grad = grad_second.astype(jnp.bfloat16)
    grad_wdown = jnp.einsum("rf,rd->fd", active, down_grad, preferred_element_type=jnp.float32)
    grad_active = jnp.einsum("rd,fd->rf", down_grad, w_down, preferred_element_type=jnp.float32)
    _, gelu_pull = jax.vjp(gelu_exact, up_pre)
    up_grad = gelu_pull(grad_active)[0].astype(jnp.bfloat16)
    grad_wup = jnp.einsum("rd,rf->df", first_norm, up_grad, preferred_element_type=jnp.float32)
    grad_first = (
        jnp.einsum("rf,df->rd", up_grad, w_up, preferred_element_type=jnp.float32) + grad_second
    )
    _, first_pull = jax.vjp(
        layer_norm, first_sum, gains[0].astype(jnp.float32), biases[3].astype(jnp.float32)
    )
    grad_fsum, gain_one, shift_one = first_pull(grad_first)
    attn_grad = grad_fsum.astype(jnp.bfloat16)
    grad_wout = jnp.einsum("re,rd->ed", mixed_rows, attn_grad, preferred_element_type=jnp.float32)
    grad_mixed = jnp.einsum(
        "rd,ed->re", attn_grad, w_out, preferred_element_type=jnp.float32
    ).astype(jnp.bfloat16)
    small_grads = (
        jnp.sum(attn_grad.astype(jnp.float32), axis=0),
        shift_one,
        jnp.sum(down_grad.astype(jnp.float32), axis=0),
        shift_two,
        jnp.sum(up_grad.astype(jnp.float32), axis=0),
        gain_one,
        gain_two,
    )
    return (grad_mixed, grad_fsum, grad_wout, grad_wup, grad_wdown, small_grads)


def head_back(inputs_b, w_qkv, grad_queries, grad_keys, grad_values, grad_resid):
    grad_joined = jnp.concatenate([grad_queries, grad_keys, grad_values], axis=1)
    grad_inputs = (
        jnp.einsum("rc,dc->rd", grad_joined, w_qkv, preferred_element_type=jnp.float32) + grad_resid
    )
    grad_wqkv = jnp.einsum("rd,rc->dc", inputs_b, grad_joined, preferred_element_type=jnp.float32)
    sum_queries = jnp.sum(grad_queries.astype(jnp.float32), axis=0)
    sum_values = jnp.sum(grad_values.astype(jnp.float32), axis=0)
    return (grad_inputs, grad_wqkv, sum_queries, sum_values)


def pack_grads(grad_wqkv, sum_queries, sum_values, tail_parts):
    grad_mixed, grad_fsum, grad_wout, grad_wup, grad_wdown, small_grads = tail_parts
    out_bias, shift_one, down_bias, shift_two, up_bias, gain_one, gain_two = small_grads
    bias_grad = jnp.stack([sum_queries, sum_values, out_bias, shift_one, down_bias, shift_two])
    gains_grad = jnp.stack([gain_one, gain_two])
    return (grad_wqkv, grad_wout, grad_wup, grad_wdown, bias_grad, up_bias, gains_grad)


def local_ahead(tokens, weights):
    queries, key_rows, value_rows = project(tokens, weights)
    four_shape = (-1, SEG_LEN, H, HD)
    queries = queries.reshape(four_shape)
    key_rows = key_rows.reshape(four_shape)
    value_rows = value_rows.reshape(four_shape)
    mixed_rows, log_total = attend(queries, key_rows, value_rows, None)
    mixed_rows = mixed_rows.reshape(-1, D)
    output, saved = tail_ahead(tokens.astype(jnp.float32), mixed_rows, weights)
    return (output, (queries, key_rows, value_rows, mixed_rows, log_total, saved))


def shards(
    tokens,
    doc_segments,
    local_qkv,
    local_out,
    local_up,
    local_down,
    local_bias,
    local_upbias,
    local_gains,
    cross_qkv,
    cross_out,
    cross_up,
    cross_down,
    cross_bias,
    cross_upbias,
    cross_gains,
    pos_table,
    cotangent,
):
    seg_count = lax.axis_size("seg")
    seg_index = lax.axis_index("seg")
    segs_dev = tokens.shape[0] // SEG_LEN
    doc_all, place_all = slot_layout(doc_segments[0], segs_dev, seg_count)
    doc_own = lax.dynamic_slice_in_dim(doc_all, seg_index * segs_dev, segs_dev)
    place_own = lax.dynamic_slice_in_dim(place_all, seg_index * segs_dev, segs_dev)
    local_full = (
        lax.all_gather(local_qkv, "seg", axis=0, tiled=True),
        lax.all_gather(local_out, "seg", axis=0, tiled=True),
        lax.all_gather(local_up, "seg", axis=0, tiled=True),
        lax.all_gather(local_down, "seg", axis=0, tiled=True),
        lax.all_gather(local_bias, "seg", axis=1, tiled=True),
        lax.all_gather(local_upbias, "seg", axis=0, tiled=True),
        lax.all_gather(local_gains, "seg", axis=1, tiled=True),
    )
    cross_full = (
        lax.all_gather(cross_qkv, "seg", axis=0, tiled=True),
        lax.all_gather(cross_out, "seg", axis=0, tiled=True),
        lax.all_gather(cross_up, "seg", axis=0, tiled=True),
        lax.all_gather(cross_down, "seg", axis=0, tiled=True),
        lax.all_gather(cross_bias, "seg", axis=1, tiled=True),
        lax.all_gather(cross_upbias, "seg", axis=0, tiled=True),
        lax.all_gather(cross_gains, "seg", axis=1, tiled=True),
        lax.all_gather(pos_table, "seg", axis=0, tiled=True),
    )
    cross_set = cross_full[:7]
    local_result, _ = local_ahead(tokens, local_full)
    layer_rows = local_result.reshape(segs_dev, SEG_LEN, D)
    onehot = (place_own[:, None] == jnp.arange(POSN, dtype=jnp.int32)[None, :]).astype(jnp.bfloat16)
    cross_in = layer_rows[:, 0, :] + jnp.dot(
        onehot, cross_full[7], preferred_element_type=jnp.float32
    )
    cross_in = cross_in.astype(jnp.bfloat16)
    cross_w = cross_set[0]
    cross_b = cross_set[4]
    queries = (
        jnp.dot(cross_in, cross_w[:, :D], preferred_element_type=jnp.float32) + cross_b[0]
    ).astype(jnp.bfloat16)
    rows_all = lax.all_gather(cross_in, "seg", axis=0, tiled=True)
    key_value = jnp.dot(rows_all, cross_w[:, D:], preferred_element_type=jnp.float32)
    keys_all = key_value[:, :D].astype(jnp.bfloat16)
    values_all = (key_value[:, D:] + cross_b[1]).astype(jnp.bfloat16)
    allowed = (doc_own[:, None] == doc_all[None, :])[None]
    query_four = queries.reshape(1, segs_dev, H, HD)
    key_four = keys_all.reshape(1, -1, H, HD)
    value_four = values_all.reshape(1, -1, H, HD)
    cross_mixed, cross_total = attend(query_four, key_four, value_four, allowed)
    cross_mixed = cross_mixed.reshape(segs_dev, D)
    cross_result, cross_saved = tail_ahead(cross_in.astype(jnp.float32), cross_mixed, cross_set)
    layer_rows = layer_rows.at[:, 0, :].set(cross_result)
    layer_out = layer_rows.reshape(-1, D).astype(jnp.bfloat16)
    cross_back = (
        lax.all_gather(cross_qkv, "seg", axis=0, tiled=True),
        lax.all_gather(cross_out, "seg", axis=0, tiled=True),
        lax.all_gather(cross_up, "seg", axis=0, tiled=True),
        lax.all_gather(cross_down, "seg", axis=0, tiled=True),
        lax.all_gather(cross_bias, "seg", axis=1, tiled=True),
        lax.all_gather(cross_upbias, "seg", axis=0, tiled=True),
        lax.all_gather(cross_gains, "seg", axis=1, tiled=True),
    )
    grad_layer = cotangent.astype(jnp.float32).reshape(segs_dev, SEG_LEN, D)
    cross_tail = tail_back(grad_layer[:, 0, :], cross_mixed, cross_back, cross_saved)
    grad_q, grad_k_part, grad_v_part = attend_back(
        query_four,
        key_four,
        value_four,
        allowed,
        cross_total,
        cross_tail[0].reshape(1, segs_dev, H, HD),
    )
    grad_k, grad_v = (
        lax.psum_scatter(
            grad_k_part.reshape(-1, D).astype(jnp.bfloat16), "seg", scatter_dimension=0, tiled=True
        ).astype(jnp.float32),
        lax.psum_scatter(
            grad_v_part.reshape(-1, D).astype(jnp.bfloat16), "seg", scatter_dimension=0, tiled=True
        ).astype(jnp.float32),
    )
    grad_cross_in, cross_wqkv, cross_sum_q, cross_sum_v = head_back(
        cross_in,
        cross_back[0],
        grad_q.reshape(segs_dev, D).astype(jnp.bfloat16),
        grad_k.astype(jnp.bfloat16),
        grad_v.astype(jnp.bfloat16),
        cross_tail[1],
    )
    grad_pos = jnp.einsum("rp,rd->pd", onehot.astype(jnp.float32), grad_cross_in, precision=HIGHEST)
    cross_grads = pack_grads(cross_wqkv, cross_sum_q, cross_sum_v, cross_tail)
    cross_share = (
        lax.psum_scatter(
            cross_grads[0].astype(jnp.bfloat16), "seg", scatter_dimension=0, tiled=True
        ).astype(jnp.float32),
        lax.psum_scatter(
            cross_grads[1].astype(jnp.bfloat16), "seg", scatter_dimension=0, tiled=True
        ).astype(jnp.float32),
        lax.psum_scatter(
            cross_grads[2].astype(jnp.bfloat16), "seg", scatter_dimension=0, tiled=True
        ).astype(jnp.float32),
        lax.psum_scatter(
            cross_grads[3].astype(jnp.bfloat16), "seg", scatter_dimension=0, tiled=True
        ).astype(jnp.float32),
        lax.psum_scatter(
            cross_grads[4].astype(jnp.bfloat16), "seg", scatter_dimension=1, tiled=True
        ).astype(jnp.float32),
        lax.psum_scatter(
            cross_grads[5].astype(jnp.bfloat16), "seg", scatter_dimension=0, tiled=True
        ).astype(jnp.float32),
        lax.psum_scatter(
            cross_grads[6].astype(jnp.bfloat16), "seg", scatter_dimension=1, tiled=True
        ).astype(jnp.float32),
        lax.psum_scatter(
            grad_pos.astype(jnp.bfloat16), "seg", scatter_dimension=0, tiled=True
        ).astype(jnp.float32),
    )
    grad_layer = grad_layer.at[:, 0, :].set(grad_cross_in)
    local_back = (
        lax.all_gather(local_qkv, "seg", axis=0, tiled=True),
        lax.all_gather(local_out, "seg", axis=0, tiled=True),
        lax.all_gather(local_up, "seg", axis=0, tiled=True),
        lax.all_gather(local_down, "seg", axis=0, tiled=True),
        lax.all_gather(local_bias, "seg", axis=1, tiled=True),
        lax.all_gather(local_upbias, "seg", axis=0, tiled=True),
        lax.all_gather(local_gains, "seg", axis=1, tiled=True),
    )
    _, local_saved = local_ahead(tokens, local_back)
    seg_queries, seg_keys, seg_values, seg_mixed, seg_total, seg_saved = local_saved
    local_tail = tail_back(grad_layer.reshape(-1, D), seg_mixed, local_back, seg_saved)
    grad_sq, grad_sk, grad_sv = attend_back(
        seg_queries,
        seg_keys,
        seg_values,
        None,
        seg_total,
        local_tail[0].reshape(-1, SEG_LEN, H, HD),
    )
    grad_tokens, local_wqkv, local_sum_q, local_sum_v = head_back(
        tokens,
        local_back[0],
        grad_sq.reshape(-1, D).astype(jnp.bfloat16),
        grad_sk.reshape(-1, D).astype(jnp.bfloat16),
        grad_sv.reshape(-1, D).astype(jnp.bfloat16),
        local_tail[1],
    )
    local_grads = pack_grads(local_wqkv, local_sum_q, local_sum_v, local_tail)
    local_share = (
        lax.psum_scatter(
            local_grads[0].astype(jnp.bfloat16), "seg", scatter_dimension=0, tiled=True
        ).astype(jnp.float32),
        lax.psum_scatter(
            local_grads[1].astype(jnp.bfloat16), "seg", scatter_dimension=0, tiled=True
        ).astype(jnp.float32),
        lax.psum_scatter(
            local_grads[2].astype(jnp.bfloat16), "seg", scatter_dimension=0, tiled=True
        ).astype(jnp.float32),
        lax.psum_scatter(
            local_grads[3].astype(jnp.bfloat16), "seg", scatter_dimension=0, tiled=True
        ).astype(jnp.float32),
        lax.psum_scatter(
            local_grads[4].astype(jnp.bfloat16), "seg", scatter_dimension=1, tiled=True
        ).astype(jnp.float32),
        lax.psum_scatter(
            local_grads[5].astype(jnp.bfloat16), "seg", scatter_dimension=0, tiled=True
        ).astype(jnp.float32),
        lax.psum_scatter(
            local_grads[6].astype(jnp.bfloat16), "seg", scatter_dimension=1, tiled=True
        ).astype(jnp.float32),
    )
    totals = (
        lax.psum(local_share[0].astype(jnp.bfloat16), "grp").astype(jnp.float32),
        lax.psum(local_share[1].astype(jnp.bfloat16), "grp").astype(jnp.float32),
        lax.psum(local_share[2].astype(jnp.bfloat16), "grp").astype(jnp.float32),
        lax.psum(local_share[3].astype(jnp.bfloat16), "grp").astype(jnp.float32),
        lax.psum(local_share[4].astype(jnp.bfloat16), "grp").astype(jnp.float32),
        lax.psum(local_share[5].astype(jnp.bfloat16), "grp").astype(jnp.float32),
        lax.psum(local_share[6].astype(jnp.bfloat16), "grp").astype(jnp.float32),
        lax.psum(cross_share[0].astype(jnp.bfloat16), "grp").astype(jnp.float32),
        lax.psum(cross_share[1].astype(jnp.bfloat16), "grp").astype(jnp.float32),
        lax.psum(cross_share[2].astype(jnp.bfloat16), "grp").astype(jnp.float32),
        lax.psum(cross_share[3].astype(jnp.bfloat16), "grp").astype(jnp.float32),
        lax.psum(cross_share[4].astype(jnp.bfloat16), "grp").astype(jnp.float32),
        lax.psum(cross_share[5].astype(jnp.bfloat16), "grp").astype(jnp.float32),
        lax.psum(cross_share[6].astype(jnp.bfloat16), "grp").astype(jnp.float32),
        lax.psum(cross_share[7].astype(jnp.bfloat16), "grp").astype(jnp.float32),
    )
    return (
        layer_out,
        grad_tokens,
        totals[0],
        totals[1],
        totals[2],
        totals[3],
        totals[4],
        totals[5],
        totals[6],
        totals[7],
        totals[8],
        totals[9],
        totals[10],
        totals[11],
        totals[12],
        totals[13],
        totals[14],
    )


def solution(mesh):
    in_specs = (
        P(("grp", "seg"), None),
        P("grp", None),
        P("seg", None),
        P("seg", None),
        P("seg", None),
        P("seg", None),
        P(None, "seg"),
        P("seg"),
        P(None, "seg"),
        P("seg", None),
        P("seg", None),
        P("seg", None),
        P("seg", None),
        P(None, "seg"),
        P("seg"),
        P(None, "seg"),
        P("seg", None),
        P(("grp", "seg"), None),
    )
    out_specs = (
        P(("grp", "seg"), None),
        P(("grp", "seg"), None),
        P("seg", None),
        P("seg", None),
        P("seg", None),
        P("seg", None),
        P(None, "seg"),
        P("seg"),
        P(None, "seg"),
        P("seg", None),
        P("seg", None),
        P("seg", None),
        P("seg", None),
        P(None, "seg"),
        P("seg"),
        P(None, "seg"),
        P("seg", None),
    )
    return jax.shard_map(shards, mesh=mesh, in_specs=in_specs, out_specs=out_specs, check_vma=False)
```

profile of v0, /device:TPU:1, one launch (start us, length us, event | category | flops | bytes accessed | tf_op | source)
XLA Modules:
  0.0 1588.9 jit_solution(4809915738664884276)
XLA Ops:
  15.4 25.8 %all-gather = bf16[32,24,6]{1,2,0:T(8,128)(2,1)S(1)} all-gather(bf16[1,24,6]{1,2,0:T(8,128)(2,1)S(1)} %bitcast.221), channel_id=1, replica_groups=mesh['grp'=8,'seg'=32] {'seg'}, dimensions={0}, use_global_device_ids=true | all-gather | bytes 9504 | tf_op jit(solution)/shard_map/all_gather | solution.py:216
  43.7 121.6 %all-reduce.12 = (bf16[3072]{0:T(1024)(128)(2,1)S(1)}, bf16[3072]{0:T(1024)(128)(2,1)S(1)}) all-reduce(bf16[3072]{0:T(1024)(128)(2,1)S(1)} %dynamic-update-slice.6, bf16[3072]{0:T(1024)(128)(2,1)S(1)} %dynamic-update-slice.7), channel_id=1, replica_groups=mesh['grp'=8,'seg'=32] {'seg'}, use_global_device_ids=true, to_apply=%add | all-reduce | flops 6144 | bytes 24576
  165.9 22.7 %all-gather.1 = bf16[32,24,2]{1,2,0:T(2,128)(2,1)S(1)} all-gather(bf16[1,24,2]{1,2,0:T(2,128)(2,1)S(1)} %bitcast.223), channel_id=1, replica_groups=mesh['grp'=8,'seg'=32] {'seg'}, dimensions={0}, use_global_device_ids=true | all-gather | bytes 3168 | tf_op jit(solution)/shard_map/all_gather | solution.py:218
  189.6 25.1 %all-gather.2 = bf16[32,2,768]{2,1,0:T(2,128)(2,1)S(1)} all-gather(bf16[1,2,768]{2,1,0:T(2,128)(2,1)S(1)} %bitcast.220), channel_id=1, replica_groups=mesh['grp'=8,'seg'=32] {'seg'}, dimensions={0}, use_global_device_ids=true | all-gather | bytes 101376 | tf_op jit(solution)/shard_map/all_gather | solution.py:228
  215.4 21.4 %all-gather.4 = bf16[32,24,6]{1,2,0:T(8,128)(2,1)S(1)} all-gather(bf16[1,24,6]{1,2,0:T(8,128)(2,1)S(1)} %bitcast.222), channel_id=1, replica_groups=mesh['grp'=8,'seg'=32] {'seg'}, dimensions={0}, use_global_device_ids=true | all-gather | bytes 9504 | tf_op jit(solution)/shard_map/all_gather | solution.py:225
  238.8 21.5 %all-gather.5 = bf16[32,24,2]{1,2,0:T(2,128)(2,1)S(1)} all-gather(bf16[1,24,2]{1,2,0:T(2,128)(2,1)S(1)} %bitcast.224), channel_id=1, replica_groups=mesh['grp'=8,'seg'=32] {'seg'}, dimensions={0}, use_global_device_ids=true | all-gather | bytes 3168 | tf_op jit(solution)/shard_map/all_gather | solution.py:227
  263.0 3.6 fusion.112
  268.5 1.9 reshape.538
  270.4 1.7 copy.141
  272.1 1.9 reshape.539
  274.1 1.7 copy.142
  276.8 1.7 copy.143
  278.5 1.9 multiply_reduce_fusion.1
  283.1 2.4 fusion.104
  288.0 16.0 %multiply_convert_fusion = (bf16[384,3072]{1,0:T(8,128)(2,1)}, f32[384,3072]{1,0:T(8,128)}, f32[384,3072]{1,0:T(8,128)}) fusion(f32[3072]{0:T(1024)} %convert_element_type.394, bf16[768,3072]{1,0:T(8,128)(2,1)} %all-gather.19.cloned.1.call-done, f32[384,768]{1,0:T(8,128)} %copy-done.10, f32[768]{0:T(1024)} %get-tuple-element.127, ...), kind=kOutput, calls=%fused_computation.9 | convolution fusion | flops 1891270656 | bytes 17716224 | tf_op jit(solution)/shard_map/dot_general | solution.py:106
  304.1 5.5 fusion.105
  312.2 24.2 %all-gather.3 = bf16[32,3,768]{2,1,0:T(4,128)(2,1)} all-gather(bf16[1,3,768]{2,1,0:T(4,128)(2,1)S(1)} %bitcast.214), channel_id=1, replica_groups=mesh['grp'=8,'seg'=32] {'seg'}, dimensions={0}, use_global_device_ids=true | all-gather | bytes 152064 | tf_op jit(solution)/shard_map/all_gather | solution.py:243
  336.4 1.7 reshape.509
  338.1 2.3 fusion.7
  341.9 1.7 copy.150
  343.6 2.1 fusion.35
  348.2 1.7 copy.149
  360.0 19.8 %all-gather.27.cloned.1.call-done = bf16[768,3072]{1,0:T(8,128)(2,1)} async-done(((bf16[24,3072]{1,0:T(8,128)(2,1)}), bf16[768,3072]{1,0:T(8,128)(2,1)}) %all-gather.27.cloned.1.call-update) | async-done | bytes 4718608 | tf_op jit(solution)/shard_map/all_gather | solution.py:223
  379.8 3.8 multiply_convert_fusion.2
  383.6 50.1 %all-gather.29.cloned.1.call-done = bf16[3072,768]{1,0:T(8,128)(2,1)} async-done(((bf16[96,768]{1,0:T(8,128)(2,1)}), bf16[3072,768]{1,0:T(8,128)(2,1)}) %all-gather.29.cloned.1.call-update) | async-done | bytes 4718608 | tf_op jit(solution)/shard_map/all_gather | solution.py:224
  433.6 3.3 fusion.108
  440.8 1.9 fusion.90
  443.1 2.1 multiply_reduce_fusion.8
  450.3 1.7 convolution_convert_fusion.11
  454.5 1.7 copy.159
  456.2 1.7 copy.161
  458.0 1.8 fusion.111
  460.5 107.4 %all-reduce.23.cloned.1.call-done = (bf16[96,768]{1,0:T(8,128)(2,1)}, bf16[96,768]{1,0:T(8,128)(2,1)}) async-done(((bf16[96,768]{1,0:T(8,128)(2,1)}, bf16[96,768]{1,0:T(8,128)(2,1)}), (bf16[96,768]{1,0:T(8,128)(2,1)}, bf16[96,768]{1,0:T(8,128)(2,1)})) %all-reduce.23.cloned.1.call-update) | async-done | bytes 294928
  569.9 3.0 convolution_add_fusion.10
  574.6 2.3 convolution_convert_fusion.7
  578.4 2.4 fusion.22
  582.2 8.9 fusion.94
  591.1 2.9 multiply_reduce_fusion.2
  598.7 2.8 reshape.540
  601.5 2.6 copy.164
  604.1 3.1 convolution_convert_fusion.6
  607.2 2.0 multiply_reduce_fusion
  609.2 1.8 multiply_convert_fusion.1
  611.5 2.2 fusion.110
  618.4 3.8 fusion.6
  622.2 5.8 copy.180
  628.7 3.0 convolution_convert_fusion.5
  632.5 3.6 convolution_convert_fusion
  636.8 3.6 convolution_convert_fusion.1
  641.6 6.3 convolution_convert_fusion.3
  649.0 6.5 convolution_convert_fusion.2
  669.1 120.7 %all-reduce.11 = (bf16[6,768]{1,0:T(8,128)(2,1)S(1)}, bf16[3072]{0:T(1024)(128)(2,1)S(1)}, bf16[2,768]{1,0:T(2,128)(2,1)S(1)}, bf16[6,768]{1,0:T(8,128)(2,1)S(1)...) all-reduce(bf16[6,768]{1,0:T(8,128)(2,1)S(1)} %stack.68, ...), channel_id=8, replica_groups=mesh['grp'=8,'seg'=32] {'seg'}, use_global_device_ids=true, to_apply=%region_41.42.clone | all-reduce | flops 18432 | bytes 73728
  794.7 60.4 %reduce-scatter.15.cloned.1.call-done = bf16[24,768]{1,0:T(8,128)(2,1)} async-done(((bf16[768,768]{1,0:T(8,128)(2,1)}), bf16[24,768]{1,0:T(8,128)(2,1)}) %reduce-scatter.15.cloned.1.call-update) | async-done | bytes 36880 | tf_op jit(solution)/shard_map/reduce_scatter | solution.py:353
  855.2 92.0 %reduce-scatter.29.cloned.1.call-done = bf16[24,2304]{1,0:T(8,128)(2,1)} async-done(((bf16[768,2304]{1,0:T(8,128)(2,1)}), bf16[24,2304]{1,0:T(8,128)(2,1)}) %reduce-scatter.29.cloned.1.call-update) | async-done | bytes 110608
  947.2 2.0 copy.181
  949.2 89.9 %reduce-scatter.21.cloned.1.call-done = bf16[24,2304]{1,0:T(8,128)(2,1)} async-done(((bf16[768,2304]{1,0:T(8,128)(2,1)}), bf16[24,2304]{1,0:T(8,128)(2,1)}) %reduce-scatter.21.cloned.1.call-update) | async-done | bytes 110608 | tf_op jit(solution)/shard_map/reduce_scatter | solution.py:294
  1039.1 95.0 %reduce-scatter.27.cloned.1.call-done = bf16[96,768]{1,0:T(8,128)(2,1)} async-done(((bf16[3072,768]{1,0:T(8,128)(2,1)}), bf16[96,768]{1,0:T(8,128)(2,1)}) %reduce-scatter.27.cloned.1.call-update) | async-done | bytes 147472 | tf_op jit(solution)/shard_map/reduce_scatter | solution.py:303
  1134.1 94.6 %reduce-scatter.25.cloned.1.call-done = bf16[24,3072]{1,0:T(8,128)(2,1)} async-done(((bf16[768,3072]{1,0:T(8,128)(2,1)}), bf16[24,3072]{1,0:T(8,128)(2,1)}) %reduce-scatter.25.cloned.1.call-update) | async-done | bytes 147472 | tf_op jit(solution)/shard_map/reduce_scatter | solution.py:300
  1228.7 95.1 %reduce-scatter.17.cloned.1.call-done = bf16[24,3072]{1,0:T(8,128)(2,1)} async-done(((bf16[768,3072]{1,0:T(8,128)(2,1)}), bf16[24,3072]{1,0:T(8,128)(2,1)}) %reduce-scatter.17.cloned.1.call-update) | async-done | bytes 147472 | tf_op jit(solution)/shard_map/reduce_scatter | solution.py:356
  1323.8 94.5 %reduce-scatter.19.cloned.1.call-done = bf16[96,768]{1,0:T(8,128)(2,1)} async-done(((bf16[3072,768]{1,0:T(8,128)(2,1)}), bf16[96,768]{1,0:T(8,128)(2,1)}) %reduce-scatter.19.cloned.1.call-update) | async-done | bytes 147472 | tf_op jit(solution)/shard_map/reduce_scatter | solution.py:359
  1419.4 5.1 convolution_add_fusion.5
  1424.5 67.5 %all-reduce.25.cloned.1.call-done = (bf16[24,768]{1,0:T(8,128)(2,1)}, bf16[6,24]{1,0:T(8,128)(2,1)}, bf16[96]{0:T(256)(128)(2,1)}, bf16[2,24]{1,0:T(2,128)(2,1)}...) async-done(((bf16[24,768]{1,0:T(8,128)(2,1)}, bf16[6,24]{1,0:T(8,128)(2,1)}, ...) | async-done | bytes 77968 | tf_op jit(solution)/shard_map/psum | solution.py:374
  1503.3 69.4 %all-reduce.27.cloned.1.call-done = (bf16[24,2304]{0,1:T(8,128)(2,1)}, bf16[24,3072]{1,0:T(8,128)(2,1)}, bf16[96,768]{1,0:T(8,128)(2,1)}, bf16[24,2304]{1,0:T(8,...) async-done(((bf16[24,2304]{0,1:T(8,128)(2,1)}, bf16[24,3072]{1,0:T(8,128)(2,1)}, bf16[96,768]{1,0:T(8,128)(2,1)}, bf16[24,2304]{1,0:T(8,128)(2,1)}, ...) | async-done | bytes 811024 | tf_op jit(solution)/shard_map/psum | solution.py:373
  1572.7 1.7 convert_element_type.449
  (403 shorter events, 109.8 us)
Async XLA Ops:
  7.2 34.8 %copy-start.89 = (u32[256]{0:T(256)S(1)}, u32[256]{0:T(256)}, u32[]{:S(2)}) copy-start(u32[256]{0:T(256)} %constant.234) | copy-start | bytes 3076
  7.2 8.2 copy-start.85
  7.2 36.0 %copy-start.98 = (bf16[96]{0:T(256)(128)(2,1)S(1)}, bf16[96]{0:T(256)(128)(2,1)}, u32[]{:S(2)}) copy-start(bf16[96]{0:T(256)(128)(2,1)} %param.29) | copy-start | bytes 580
  7.2 36.2 %copy-start.99 = (bf16[96]{0:T(256)(128)(2,1)S(1)}, bf16[96]{0:T(256)(128)(2,1)}, u32[]{:S(2)}) copy-start(bf16[96]{0:T(256)(128)(2,1)} %param.36) | copy-start | bytes 580
  7.2 158.6 %copy-start.91 = (bf16[2,24]{1,0:T(2,128)(2,1)S(1)}, bf16[2,24]{1,0:T(2,128)(2,1)}, u32[]{:S(2)}) copy-start(bf16[2,24]{1,0:T(2,128)(2,1)} %param.30) | copy-start | bytes 292
  7.2 182.1 %copy-start.100 = (s32[1,6]{1,0:T(1,128)S(1)}, s32[1,6]{1,0:T(1,128)}, u32[]{:S(2)}) copy-start(s32[1,6]{1,0:T(1,128)} %param.23) | copy-start | bytes 76
  7.3 182.4 %copy-start.84 = (bf16[2,768]{1,0:T(2,128)(2,1)S(1)}, bf16[2,768]{1,0:T(2,128)(2,1)}, u32[]{:S(2)}) copy-start(bf16[2,768]{1,0:T(2,128)(2,1)} %param.38) | copy-start | bytes 9220
  7.3 208.1 %copy-start.86 = (bf16[6,24]{1,0:T(8,128)(2,1)S(1)}, bf16[6,24]{1,0:T(8,128)(2,1)}, u32[]{:S(2)}) copy-start(bf16[6,24]{1,0:T(8,128)(2,1)} %param.35) | copy-start | bytes 868
  7.3 231.6 %copy-start.92 = (bf16[2,24]{1,0:T(2,128)(2,1)S(1)}, bf16[2,24]{1,0:T(2,128)(2,1)}, u32[]{:S(2)}) copy-start(bf16[2,24]{1,0:T(2,128)(2,1)} %param.37) | copy-start | bytes 292
  7.3 255.7 %copy-start.96 = (bf16[384,768]{1,0:T(8,128)(2,1)S(1)}, bf16[384,768]{1,0:T(8,128)(2,1)}, u32[]{:S(2)}) copy-start(bf16[384,768]{1,0:T(8,128)(2,1)} %param.22) | copy-start | bytes 1769476
  7.3 255.6 %all-gather.15.cloned.1.call-start = ((), (), s32[]{:S(2)}) async-start(), calls=%async_computation.8 | async-start | bytes 3649536 | tf_op jit(solution)/shard_map/all_gather | solution.py:212
  8.0 275.0 %all-gather.17.cloned.1.call-start = ((), (), s32[]{:S(2)}) async-start(), calls=%async_computation.9 | async-start | bytes 1216512 | tf_op jit(solution)/shard_map/all_gather | solution.py:213
  8.8 279.2 %all-gather.19.cloned.1.call-start = ((), (), s32[]{:S(2)}) async-start(), calls=%async_computation.10 | async-start | bytes 4866048 | tf_op jit(solution)/shard_map/all_gather | solution.py:214
  9.5 294.6 %all-gather.21.cloned.1.call-start = ((), (), s32[]{:S(2)}) async-start(), calls=%async_computation.11 | async-start | bytes 4866048 | tf_op jit(solution)/shard_map/all_gather | solution.py:215
  10.1 328.0 %all-gather.23.cloned.1.call-start = ((), (), s32[]{:S(2)}) async-start(), calls=%async_computation.12 | async-start | bytes 3649536 | tf_op jit(solution)/shard_map/all_gather | solution.py:221
  10.7 344.2 %all-gather.25.cloned.1.call-start = ((), (), s32[]{:S(2)}) async-start(), calls=%async_computation.13 | async-start | bytes 1216512 | tf_op jit(solution)/shard_map/all_gather | solution.py:222
  11.3 368.5 %all-gather.27.cloned.1.call-start = ((), (), s32[]{:S(2)}) async-start(), calls=%async_computation.14 | async-start | bytes 4866048 | tf_op jit(solution)/shard_map/all_gather | solution.py:223
  12.0 421.6 %all-gather.29.cloned.1.call-start = ((), (), s32[]{:S(2)}) async-start(), calls=%async_computation.15 | async-start | bytes 4866048 | tf_op jit(solution)/shard_map/all_gather | solution.py:224
  12.8 555.1 %all-reduce.23.cloned.1.call-start = ((), (), s32[]{:S(2)}) async-start(), calls=%async_computation.25 | async-start | bytes 589824
  189.3 121.3 %copy-start.40 = (f32[768]{0:T(1024)}, f32[768]{0:T(1024)S(1)}, u32[]{:S(2)}) copy-start(f32[768]{0:T(1024)S(1)} %get-tuple-element.133) | copy-start | bytes 9220
  283.1 4.3 copy-start.27
  283.1 4.3 copy-start.36
  285.5 18.6 %copy-start.57 = (f32[384]{0:T(512)}, f32[384]{0:T(512)S(1)}, u32[]{:S(2)}) copy-start(f32[384]{0:T(512)S(1)} %broadcast_multiply_fusion.1) | copy-start | bytes 4612
  286.8 17.3 %copy-start.59 = (f32[384]{0:T(512)}, f32[384]{0:T(512)S(1)}, u32[]{:S(2)}) copy-start(f32[384]{0:T(512)S(1)} %multiply_reduce_fusion.6) | copy-start | bytes 4612
  304.1 6.6 copy-start.64
  309.9 30.5 %copy-start.54 = (f32[384]{0:T(512)}, f32[384]{0:T(512)S(1)}, u32[]{:S(2)}) copy-start(f32[384]{0:T(512)S(1)} %fusion.79) | copy-start | bytes 4612
  312.2 31.4 %copy-start.33 = (bf16[3,768]{1,0:T(4,128)(2,1)}, bf16[3,768]{1,0:T(4,128)(2,1)S(1)}, u32[]{:S(2)}) copy-start(bf16[3,768]{1,0:T(4,128)(2,1)S(1)} %fusion.34) | copy-start | bytes 13828
  346.6 8.4 copy-start.32
  433.6 4.9 copy-start.53
  433.6 7.1 copy-start.1
  433.6 7.1 copy-start.28
  433.6 7.1 copy-start.29
  458.0 335.5 %all-reduce.21.cloned.1.call-start = ((), (), s32[]{:S(2)}) async-start(), calls=%async_computation.24 | async-start | bytes 196608
  569.9 8.5 copy-start.41
  574.6 220.1 %reduce-scatter.23.cloned.1.call-start = ((), (), s32[]{:S(2)}) async-start(), calls=%async_computation.20 | async-start | bytes 1216512 | tf_op jit(solution)/shard_map/reduce_scatter | solution.py:297
  576.9 278.2 %reduce-scatter.15.cloned.1.call-start = ((), (), s32[]{:S(2)}) async-start(), calls=%async_computation.16 | async-start | bytes 1216512 | tf_op jit(solution)/shard_map/reduce_scatter | solution.py:353
  580.9 10.2 slice-start
  582.1 8.9 copy-start.17
  582.1 8.9 copy-start.11
  582.1 8.9 copy-start.58
  582.1 8.9 copy-start.65
  582.1 8.9 copy-start.70
  582.1 9.0 slice-start.1
  611.0 336.2 %reduce-scatter.29.cloned.1.call-start = ((), (), s32[]{:S(2)}) async-start(), calls=%async_computation.23 | async-start | bytes 3649536
  628.0 411.1 %reduce-scatter.21.cloned.1.call-start = ((), (), s32[]{:S(2)}) async-start(), calls=%async_computation.19 | async-start | bytes 3649536 | tf_op jit(solution)/shard_map/reduce_scatter | solution.py:294
  631.7 502.4 %reduce-scatter.27.cloned.1.call-start = ((), (), s32[]{:S(2)}) async-start(), calls=%async_computation.22 | async-start | bytes 4866048 | tf_op jit(solution)/shard_map/reduce_scatter | solution.py:303
  636.0 592.6 %reduce-scatter.25.cloned.1.call-start = ((), (), s32[]{:S(2)}) async-start(), calls=%async_computation.21 | async-start | bytes 4866048 | tf_op jit(solution)/shard_map/reduce_scatter | solution.py:300
  640.4 683.4 %reduce-scatter.17.cloned.1.call-start = ((), (), s32[]{:S(2)}) async-start(), calls=%async_computation.17 | async-start | bytes 4866048 | tf_op jit(solution)/shard_map/reduce_scatter | solution.py:356
  647.9 770.4 %reduce-scatter.19.cloned.1.call-start = ((), (), s32[]{:S(2)}) async-start(), calls=%async_computation.18 | async-start | bytes 4866048 | tf_op jit(solution)/shard_map/reduce_scatter | solution.py:359
  655.4 4.5 copy-start.67
  655.5 5.0 copy-start.77
  655.5 5.6 copy-start.66
  655.5 5.6 copy-start.75
  655.5 6.2 copy-start.79
  655.5 7.5 copy-start.74
  655.5 8.1 copy-start.88
  655.5 8.7 copy-start.73
  655.5 762.8 %copy-start.52 = (f32[3,1,768]{2,0,1:T(4,128)S(1)}, f32[3,1,768]{2,0,1:T(4,128)}, u32[]{:S(2)}) copy-start(f32[3,1,768]{2,0,1:T(4,128)} %get-tuple-element.190) | copy-start | bytes 27652
  655.6 762.8 %copy-start.8 = (f32[384,768]{1,0:T(8,128)S(1)}, f32[384,768]{1,0:T(8,128)}, u32[]{:S(2)}) copy-start(f32[384,768]{1,0:T(8,128)} %copy-done.7) | copy-start | bytes 3538948
  655.6 836.4 %all-reduce.25.cloned.1.call-start = ((), (), s32[]{:S(2)}) async-start(), calls=%async_computation.26 | async-start | bytes 165888 | tf_op jit(solution)/shard_map/psum | solution.py:374
  664.8 754.6 %copy-start.14 = (f32[384,768]{1,0:T(8,128)S(1)}, f32[384,768]{1,0:T(8,128)}, u32[]{:S(2)}) copy-start(f32[384,768]{1,0:T(8,128)} %copy-done.13) | copy-start | bytes 3538948
  665.5 753.9 %copy-start.72 = (f32[384]{0:T(512)S(1)}, f32[384]{0:T(512)}, u32[]{:S(2)}) copy-start(f32[384]{0:T(512)} %copy-done.71) | copy-start | bytes 4612
  855.2 717.6 %all-reduce.27.cloned.1.call-start = ((), (), s32[]{:S(2)}) async-start(), calls=%async_computation.27 | async-start | bytes 2580480 | tf_op jit(solution)/shard_map/psum | solution.py:373
  1572.7 8.2 copy-start.20
  (60 other events, 104.2 us)
Sparse Core Ops, SparseCore 0:
  10.7 54.6 all-gather.14
  68.0 47.7 all-gather.16
  118.4 51.2 all-gather.18
  172.0 51.3 all-gather.20
  225.8 50.1 all-gather.22
  278.5 47.4 all-gather.24
  328.5 51.1 all-gather.26
  382.3 51.2 all-gather.28
  458.1 109.7 all-reduce.22
  574.7 107.3 all-reduce.20
  686.4 81.4 reduce-scatter.22
  772.2 82.9 reduce-scatter.14
  859.7 87.4 reduce-scatter.28
  951.6 87.4 reduce-scatter.20
  1043.5 90.5 reduce-scatter.26
  1138.0 90.6 reduce-scatter.24
  1233.1 90.6 reduce-scatter.16
  1327.6 90.6 reduce-scatter.18
  1423.4 68.5 all-reduce.24
  1494.7 77.9 all-reduce.26
where the time goes:
time: 1600 us; the launch traced here: 1590 us
  waiting for transfers between devices  941 us (59%)
  blocking collectives  383 us (24%)
  matrix products  118 us (7%)
  local copies, waits for them, and re-layouts  76.6 us (5%)
  other arithmetic  49.8 us (3%)
  between operations  18.9 us (1%)
    unnamed x2, blocking collectives  242 us
    unnamed x23, waiting for transfers between devices  205 us
    reduce_scatter x1, waiting for transfers between devices, shards(): lax.psum_scatter(local_grads[2].astype(jnp.bfloat16), 'seg', scatter_dime...  95.1 us
    reduce_scatter x1, waiting for transfers between devices, shards(): lax.psum_scatter(cross_grads[3].astype(jnp.bfloat16), 'seg', scatter_dime...  95 us
    reduce_scatter x1, waiting for transfers between devices, shards(): lax.psum_scatter(cross_grads[2].astype(jnp.bfloat16), 'seg', scatter_dime...  94.6 us
    reduce_scatter x1, waiting for transfers between devices, shards(): lax.psum_scatter(local_grads[3].astype(jnp.bfloat16), 'seg', scatter_dime...  94.5 us
    reduce_scatter x1, waiting for transfers between devices, shards(): lax.psum_scatter(cross_grads[0].astype(jnp.bfloat16), 'seg', scatter_dime...  89.9 us
    psum x1, waiting for transfers between devices, shards(): lax.psum(local_share[0].astype(jnp.bfloat16), 'grp').astype(jnp.float32)  69.4 us
  transfers between devices with their start and end apart: 20, of which 12 were waited for; matrix products, arithmetic and copies ran while one was open for 12% of the time, Pallas kernels for 0%

commit v1 on v0

v1 whole, which is shorter than its diff:
```python
import functools
import math
import types

import jax
import jax.numpy as jnp
from jax import lax
from jax.experimental import pallas as pl
from jax.experimental.pallas import tpu as pltpu
from jax.sharding import PartitionSpec as P

D = 768
FF = 3072
ROWS = 384
SEG_LEN = 128
W = 384
F32, BF16 = jnp.float32, jnp.bfloat16
MESH = pl.DeviceIdType.MESH
DMA = pltpu.SemaphoreType.DMA
RSQ2 = 1.0 / math.sqrt(2.0)
RS2PI = 1.0 / math.sqrt(2.0 * math.pi)
VM = pltpu.VMEM


def dot(a, b):
    return lax.dot_general(a, b, (((1,), (0,)), ((), ())), preferred_element_type=F32)


def dot_bt(a, b):
    return lax.dot_general(a, b, (((1,), (1,)), ((), ())), preferred_element_type=F32)


def dot_at(a, b):
    return lax.dot_general(a, b, (((0,), (0,)), ((), ())), preferred_element_type=F32)


def rcopy(src, dst, ssem, rsem, seg):
    return pltpu.make_async_remote_copy(
        src_ref=src, dst_ref=dst, send_sem=ssem, recv_sem=rsem, device_id={"seg": seg}, device_id_type=MESH
    )


def zcopy(src, dst, ssem, rsem, z, seg):
    return pltpu.make_async_remote_copy(
        src_ref=src, dst_ref=dst, send_sem=ssem, recv_sem=rsem, device_id={"grp": z, "seg": seg}, device_id_type=MESH
    )


def take(ref, sem):
    pltpu.make_async_copy(ref, ref, sem).wait()


def send_to(me, target, src, dst, ssem, rsem):
    @pl.when(target != me)
    def _():
        rcopy(src, dst, ssem, rsem, target).start()

    @pl.when(target == me)
    def _():
        pltpu.make_async_copy(src, dst, rsem).start()


def loop(n, fn, first=0):
    def body(i, _):
        fn(i)
        return 0

    lax.fori_loop(first, n, body, 0)


def col(u, width=W):
    return pl.ds(pl.multiple_of(u * width, 128), width)


def norm(v):
    center = v - jnp.mean(v, axis=-1, keepdims=True)
    rstd = lax.rsqrt(jnp.mean(center * center, axis=-1, keepdims=True) + 1e-05)
    return center * rstd, rstd


def norm_back(grad, n, rstd, gain):
    dn = grad * gain
    return rstd * (dn - jnp.mean(dn, axis=-1, keepdims=True) - n * jnp.mean(dn * n, axis=-1, keepdims=True))


def gelu_both(u):
    e = jnp.exp(-0.5 * u * u)
    t = 1.0 / (1.0 + (0.3275911 * RSQ2) * jnp.abs(u))
    poly = t * (0.127414796 + t * (-0.142248368 + t * (0.7107068705 + t * (-0.7265760135 + t * 0.5307027145))))
    tail = poly * e
    cdf = jnp.where(u < 0.0, tail, 1.0 - tail)
    return u * cdf, cdf + u * (RS2PI * e)


def two_heads(v):
    lane = lax.broadcasted_iota(jnp.int32, v.shape, 1)
    none = jnp.zeros_like(v)
    return jnp.concatenate([jnp.where(lane < 64, v, none), jnp.where(lane >= 64, v, none)], axis=0)


def side_by_side(v):
    n = v.shape[0] // 2
    lane = lax.broadcasted_iota(jnp.int32, (n, 128), 1)
    return jnp.where(lane < 64, v[:n], v[n:])


def softmax(s):
    e = jnp.exp(s - jnp.max(s, axis=-1, keepdims=True))
    return e / jnp.sum(e, axis=-1, keepdims=True)


def softmax_back(w, dw):
    return w * (dw - jnp.sum(w * dw, axis=-1, keepdims=True))


def rows8(value):
    return value.reshape(value.shape[0] // 8, 8, value.shape[1])


def flat8(value):
    v = value.astype(F32)
    return v.reshape(v.shape[0] * v.shape[1], v.shape[2])


def sum0(v):
    return jnp.sum(v, axis=0, keepdims=True)


def owner_seg(k):
    return 2 * k


def pair_seg(p):
    return 4 * p + 1


def pair_first(p):
    return 5 * (p % 3) + 16 * (p // 3)


def fields(spec, refs):
    return types.SimpleNamespace(**dict(zip(spec, refs)))


CROSS = dict(
    pup=VM((32, 24, 128), BF16),
    xup=VM((32, 24, 128), BF16),
    xqkv=VM((32, 3, 24, 128), BF16),
    xout=VM((6, 24, D), BF16),
    wup=VM((D, 128), BF16),
    wqkv=VM((D, 384), BF16),
    wout=VM((128, D), BF16),
    wout_f=VM((144, D), F32),
    wdn=VM((128, D), BF16),
    msg=VM((8, D), BF16),
    x1=VM((32, 8, D), BF16),
    own=VM((8, 8, D), F32),
    rst=VM((8, 128), F32),
    xall=VM((96, D), BF16),
    q=VM((3, 96, 128), BF16),
    o=VM((96, 128), BF16),
    af=VM((192, 96), F32),
    p2=VM((12, 8, D), BF16),
    g2=VM((6, 8, D), BF16),
    p3=VM((8, D), BF16),
    g3=VM((12, 8, D), BF16),
    p4=VM((12, 8, D), BF16),
    g46=VM((64, 8, D), BF16),
    p5=VM((2, 8, D), BF16),
    g5=VM((12, 2, 8, D), BF16),
    p6=VM((12, 8, D), BF16),
    p7=VM((8, D), BF16),
    g7=VM((12, 8, D), BF16),
    p7f=VM((8, D), F32),
    g7f=VM((2, 8, D), F32),
    p8=VM((12, 8, D), BF16),
    g8=VM((6, 2, 8, D), BF16),
    gp=VM((96, 128), F32),
    gact=VM((96, 128), BF16),
    fall=VM((96, D), BF16),
    dd=VM((96, D), BF16),
    du=VM((96, 128), BF16),
    dq=VM((96, 384), BF16),
    de=VM((96, D), BF16),
    po_f=VM((144, D), F32),
    cs=DMA((16,)),
    cr=DMA((16,)),
    c7=DMA((32,)),
)


def slot_layout(doc, shape, slots):
    pos = (slots % 3) * 32 + slots // 3
    number = jnp.zeros(shape, jnp.int32)
    begin = jnp.zeros(shape, jnp.int32)
    end = jnp.int32(0)
    for d in range(6):
        begin = jnp.where(pos >= end, end, begin)
        number = jnp.where(pos >= end, d, number)
        end = end + doc[0, d]
    return number, pos - begin


class Cross:
    def __init__(self, r, a):
        self.r, self.a = r, a
        self.me = lax.axis_index("seg")
        self.is_owner = (self.me % 2 == 0) & (self.me < 24)
        self.k = self.me // 2
        self.is_pair = (self.me % 4 == 1) & (self.me < 24)
        self.p = self.me // 4

    def sem(self, e):
        return self.r.cs.at[e], self.r.cr.at[e]

    def seams(self):
        m = self.me % 16
        seam = (m == 5) | (m == 10)
        p0 = 3 * (self.me // 16) + jnp.where(m > 10, 2, jnp.where(m > 5, 1, 0))
        return seam, p0

    def reshard(self):
        r, a, me = self.r, self.a, self.me
        s0, r0 = self.sem(0)
        s1, r1 = self.sem(1)
        s2, r2 = self.sem(2)
        r.pup[...] = jnp.zeros((32, 24, 128), BF16)
        up = a.cup[...].astype(F32)
        for t in range(32):
            r.pup[t, :, 0:96] = up[:, 96 * t : 96 * t + 96].astype(BF16)
        loop(32, lambda t: send_to(me, t, r.pup.at[t], r.xup.at[me], s0, r0))

        def to_pair(p):
            for j in range(3):
                part = pl.ds(pl.multiple_of(D * j + 128 * p, 128), 128)
                send_to(me, pair_seg(p), a.cqkv.at[:, part], r.xqkv.at[me, j], s1, r1)
            first = pair_first(p)

            @pl.when((me >= first) & (me < first + 6))
            def _():
                send_to(me, pair_seg(p), a.cout, r.xout.at[me - first], s2, r2)

        loop(6, to_pair)
        r.wdn[0:96, :] = a.cdown[...]
        r.wdn[96:128, :] = jnp.zeros((32, D), BF16)

    def reshard_end(self):
        r = self.r
        take(r.xup, r.cr.at[0])
        r.wup[...] = r.xup[...].astype(F32).reshape(D, 128).astype(BF16)

        @pl.when(self.is_pair)
        def _():
            take(r.xqkv, r.cr.at[1])
            for j in range(3):
                r.wqkv[:, 128 * j : 128 * (j + 1)] = r.xqkv[:, j].astype(F32).reshape(D, 128).astype(BF16)
            take(r.xout, r.cr.at[2])
            r.wout_f[...] = r.xout[...].astype(F32).reshape(144, D)
            off = pl.multiple_of(8 * (self.p % 3), 8)
            r.wout[...] = r.wout_f[pl.ds(off, 128), :].astype(BF16)

    def start(self, z0, dy0):
        r, a, me = self.r, self.a, self.me
        row = lax.broadcasted_iota(jnp.int32, (8, 512), 0)
        lane = lax.broadcasted_iota(jnp.int32, (8, 512), 1)
        _, place = slot_layout(a.doc, (8, 512), jnp.minimum(me * 3 + row, 95))
        table = a.smg[...].astype(F32).reshape(512, W)[:, 256:384].astype(BF16)
        parts = []
        for i in range(6):
            hot = (lane == (place // 2) * 16 + (place % 2) * 6 + i) & (row < 3)
            parts.append(dot(hot.astype(BF16), table))
        cross_in = z0 + jnp.concatenate(parts, axis=1)
        rowd = lax.broadcasted_iota(jnp.int32, (8, D), 0)
        both = jnp.where(rowd < 3, cross_in, pltpu.roll(dy0, 3, 0))
        r.msg[...] = jnp.where(rowd < 6, both, 0.0).astype(BF16)
        ss, rs = self.sem(3)
        loop(6, lambda p: send_to(me, pair_seg(p), r.msg, r.x1.at[me], ss, rs))
        loop(12, lambda k: send_to(me, owner_seg(k), r.msg, r.x1.at[me], ss, rs))

    def pick(self, n, first, base):
        row = lax.broadcasted_iota(jnp.int32, (n, 256), 0) + first
        lane = lax.broadcasted_iota(jnp.int32, (n, 256), 1)
        return (lane == (row // 3) * 8 + row % 3 + base).astype(BF16)

    def attention(self):
        r, a, me = self.r, self.a, self.me
        ss, rs = self.sem(4)

        @pl.when(self.is_pair)
        def _():
            take(r.x1, r.cr.at[3])
            msgs = flat8(r.x1[...]).astype(BF16)
            xall = dot(self.pick(96, 0, 0), msgs).astype(BF16)
            r.xall[...] = xall
            part = col(self.p, 128)
            joined = dot(xall, r.wqkv[...])
            q = (joined[:, 0:128] + a.cb[0:1, part]).astype(BF16)
            k = joined[:, 128:256].astype(BF16)
            v = (joined[:, 256:384] + a.cb[1:2, part]).astype(BF16)
            r.q[0], r.q[1], r.q[2] = q, k, v
            line = lax.broadcasted_iota(jnp.int32, (192, 96), 0)
            doc_r, _ = slot_layout(a.doc, (192, 96), jnp.where(line < 96, line, line - 96))
            doc_c, _ = slot_layout(a.doc, (192, 96), lax.broadcasted_iota(jnp.int32, (192, 96), 1))
            w = softmax(jnp.where(doc_r == doc_c, dot_bt(two_heads(q), k) * 0.125, -1e30))
            r.af[...] = w
            o = side_by_side(dot(w.astype(BF16), v)).astype(BF16)
            r.o[...] = o
            r.p2[...] = rows8(dot(o, r.wout[...])).astype(BF16)
            loop(12, lambda k: send_to(me, owner_seg(k), r.p2.at[k], r.g2.at[self.p], ss, rs))

    def first_norm(self):
        r, a, me = self.r, self.a, self.me
        ss, rs = self.sem(5)

        @pl.when(self.is_owner)
        def _():
            take(r.x1, r.cr.at[3])
            msgs = flat8(r.x1[...]).astype(BF16)
            x = dot(self.pick(8, 8 * self.k, 0), msgs)
            r.own[1] = dot(self.pick(8, 8 * self.k, 3), msgs)
            take(r.g2, r.cr.at[4])
            total = jnp.sum(r.g2[...].astype(F32), axis=0)
            n, rstd = norm(x + (total + a.cb[2:3, :]))
            r.own[2] = n
            r.rst[...] = jnp.broadcast_to(rstd, (8, 128))
            r.p3[...] = (n * a.cb[6:7, :] + a.cb[3:4, :]).astype(BF16)
            loop(32, lambda t: send_to(me, t, r.p3, r.g3.at[self.k], ss, rs))

    def mlp(self):
        r, a, me = self.r, self.a, self.me
        ss, rs = self.sem(6)
        take(r.g3, r.cr.at[5])
        f = flat8(r.g3[...]).astype(BF16)
        r.fall[...] = f
        g, gp = gelu_both(dot(f, r.wup[...]) + a.cub[0:1, :])
        r.gp[...] = gp
        g = g.astype(BF16)
        r.gact[...] = g
        r.p4[...] = rows8(dot(g, r.wdn[...])).astype(BF16)
        loop(12, lambda k: send_to(me, owner_seg(k), r.p4.at[k], r.g46.at[me], ss, rs))

    def second_norm(self):
        r, a, me = self.r, self.a, self.me
        ss, rs = self.sem(7)

        @pl.when(self.is_owner)
        def _():
            take(r.g46.at[pl.ds(0, 32)], r.cr.at[6])
            total = jnp.sum(r.g46[0:32].astype(F32), axis=0)
            n, rstd = norm(r.p3[...].astype(F32) + (total + a.cb[4:5, :]))
            y = n * a.cb[7:8, :] + a.cb[5:6, :]
            dr2 = norm_back(r.own[1], n, rstd, a.cb[7:8, :])
            r.own[3] = n
            r.own[4] = dr2
            r.p5[0] = dr2.astype(BF16)
            r.p5[1] = y.astype(BF16)
            loop(32, lambda t: send_to(me, t, r.p5, r.g5.at[self.k], ss, rs))

    def mlp_back(self):
        r, me = self.r, self.me
        ss, rs = self.sem(8)
        take(r.g5, r.cr.at[7])
        dd = flat8(r.g5[:, 0]).astype(BF16)
        r.dd[...] = dd
        du = (dot_bt(dd, r.wdn[...]) * r.gp[...]).astype(BF16)
        r.du[...] = du
        r.p6[...] = rows8(dot_bt(du, r.wup[...])).astype(BF16)
        loop(12, lambda k: send_to(me, owner_seg(k), r.p6.at[k], r.g46.at[32 + me], ss, rs))

    def window(self, seg):
        return jnp.minimum((3 * seg) // 8, 10)

    def first_norm_back(self):
        r, a, me = self.r, self.a, self.me
        ss, rs = self.sem(9)
        fr = r.cr.at[10]

        @pl.when(self.is_owner)
        def _():
            take(r.g46.at[pl.ds(32, 32)], r.cr.at[8])
            df = jnp.sum(r.g46[32:64].astype(F32), axis=0) + r.own[4]
            r.own[5] = df
            dr1 = norm_back(df, r.own[2], r.rst[:, 0:1], a.cb[6:7, :])
            r.p7[...] = dr1.astype(BF16)
            loop(6, lambda p: send_to(me, pair_seg(p), r.p7, r.g7.at[self.k], ss, rs))
            r.p7f[...] = dr1

            def one(t):
                w = self.window(t)

                @pl.when((w == self.k) | (w + 1 == self.k))
                def _():
                    send_to(me, t, r.p7f, r.g7f.at[self.k - w], r.c7.at[t], fr)

            loop(32, one)

    def attention_back(self):
        r, me = self.r, self.me
        ss, rs = self.sem(11)

        @pl.when(self.is_pair)
        def _():
            take(r.g7, r.cr.at[9])
            de = flat8(r.g7[...]).astype(BF16)
            r.de[...] = de
            do = dot_bt(de, r.wout[...]).astype(BF16)
            q, k, v = r.q[0], r.q[1], r.q[2]
            do2, w = two_heads(do), r.af[...]
            ds = softmax_back(w, dot_bt(do2, v)).astype(BF16)
            r.dq[:, 0:128] = (side_by_side(dot(ds, k)) * 0.125).astype(BF16)
            r.dq[:, 128:256] = (dot_at(ds, two_heads(q)) * 0.125).astype(BF16)
            r.dq[:, 256:384] = dot_at(w.astype(BF16), do2).astype(BF16)
            r.p8[...] = rows8(dot_bt(r.dq[...], r.wqkv[...])).astype(BF16)
            loop(32, lambda t: send_to(me, t, r.p8.at[pl.ds(self.window(t), 2)], r.g8.at[self.p], ss, rs))

    def finish(self):
        r = self.r
        take(r.g7f, r.cr.at[10])
        take(r.g8, r.cr.at[11])
        total = r.g7f[...] + jnp.sum(r.g8[...].astype(F32), axis=0)
        shift = 3 * self.me - 8 * self.window(self.me)
        return pltpu.roll(total.reshape(16, D), 16 - shift, 0)[0:8]

    def output_rows(self):
        w = self.window(self.me)
        y = self.r.g5[pl.ds(w, 2), 1].astype(F32).reshape(16, D)
        return pltpu.roll(y, 16 - (3 * self.me - 8 * w), 0)[0:8]

    def grads(self):
        r, a = self.r, self.a
        a.pu[...] = dot_at(r.fall[...], r.du[...]).reshape(32, 24, 128).astype(BF16)
        a.gdn[...] = dot_at(r.gact[...], r.dd[...])[0:96].astype(BF16)

        @pl.when(self.is_pair)
        def _():
            a.pq[...] = dot_at(r.xall[...], r.dq[...]).reshape(32, 24, 384).astype(BF16)
            r.po_f[...] = jnp.zeros((144, D), F32)
            off = pl.multiple_of(8 * (self.p % 3), 8)
            r.po_f[pl.ds(off, 128), :] = dot_at(r.o[...], r.de[...])
            a.po[...] = r.po_f[...].reshape(6, 24, D).astype(BF16)

        a.small[...] = jnp.zeros((8, D), F32)

        @pl.when(self.is_owner)
        def _():
            dr1, df, dr2, dy = r.p7[...].astype(F32), r.own[5], r.own[4], r.own[1]
            dd = r.p5[0].astype(F32)
            for row, v in ((2, dr1), (3, df), (4, dd), (5, dy), (6, df * r.own[2]), (7, dy * r.own[3])):
                a.small[row : row + 1, :] = sum0(v)

        @pl.when(self.is_pair)
        def _():
            part = col(self.p, 128)
            a.small[0:1, part] = sum0(r.dq[:, 0:128].astype(F32))
            a.small[1:2, part] = sum0(r.dq[:, 256:384].astype(F32))

        a.dc[...] = jnp.broadcast_to(sum0(r.du[...].astype(F32)), (8, 128))

    def drain(self):
        r, me = self.r, self.me
        cs = r.cs

        def some(e, ref, count, fewer):
            @pl.when(fewer)
            def _():
                take(ref.at[pl.ds(0, count - 1)], cs.at[e])

            @pl.when(jnp.logical_not(fewer))
            def _():
                take(ref.at[pl.ds(0, count)], cs.at[e])

        take(r.xup.at[pl.ds(0, 31)], cs.at[0])
        some(1, r.xqkv, 6, self.is_pair)
        seam, p0 = self.seams()
        hits = jnp.where(me == pair_seg(p0), 1, 0) + jnp.where(seam & (me == pair_seg(p0 + 1)), 1, 0)
        count = jnp.where(seam, 2, 1) - hits
        for n in (1, 2):

            @pl.when(count == n)
            def _():
                take(r.xout.at[pl.ds(0, n)], cs.at[2])

        some(3, r.g46, 18, self.is_pair | self.is_owner)
        some(6, r.g46, 12, self.is_owner)
        some(8, r.g46, 12, self.is_owner)

        @pl.when(self.is_pair)
        def _():
            take(r.g46.at[pl.ds(0, 12)], cs.at[4])
            take(r.g46.at[pl.ds(0, 62)], cs.at[11])

        @pl.when(self.is_owner)
        def _():
            take(r.g46.at[pl.ds(0, 31)], cs.at[5])
            take(r.g46.at[pl.ds(0, 62)], cs.at[7])
            take(r.g46.at[pl.ds(0, 6)], cs.at[9])

            def one(t):
                w = self.window(t)

                @pl.when(((w == self.k) | (w + 1 == self.k)) & (t != me))
                def _():
                    take(r.p7f, r.c7.at[t])

            loop(32, one)


class CrossGrads(Cross):
    def scatter(self):
        r, a, me = self.r, self.a, self.me
        loop(32, lambda t: send_to(me, t, a.pu.at[t], r.gup.at[me], r.ks.at[0], r.kr.at[0]))

        @pl.when(self.is_pair)
        def _():
            loop(32, lambda t: send_to(me, t, a.pq.at[t], r.gqkv.at[self.p], r.ks.at[1], r.kr.at[1]))
            loop(
                6,
                lambda i: send_to(
                    me, pair_first(self.p) + i, a.po.at[i], r.go.at[self.p % 2], r.ks.at[2], r.kr.at[2]
                ),
            )

    def planes(self, red):
        r, a, me, z = self.r, self.a, self.me, red.z
        take(r.gup, r.kr.at[0])
        take(r.gqkv, r.kr.at[1])
        for i in range(6):
            r.c0[i] = r.gqkv[i]
        seam, p0 = self.seams()

        @pl.when(seam)
        def _():
            take(r.go, r.kr.at[2])
            both = (r.go[0].astype(F32) + r.go[1].astype(F32)).astype(BF16)
            for i in range(2):
                r.c0[6 + i] = both[:, W * i : W * (i + 1)]

        @pl.when(jnp.logical_not(seam))
        def _():
            take(r.go.at[0], r.kr.at[2])
            for i in range(2):
                r.c0[6 + i] = r.go[p0 % 2, :, W * i : W * (i + 1)]

        gdn = a.gdn[...].astype(F32).reshape(4, 24, D)
        for i in range(2):
            for n in range(4):
                r.c0[8 + 4 * i + n] = gdn[n, :, W * i : W * (i + 1)].astype(BF16)

        def out(zz):
            zcopy(r.c0.at[pl.ds(2 * zz, 2)], r.cr.at[z], r.xs.at[1], r.xr.at[1], zz, me).start()
            zcopy(r.gup.at[pl.ds(4 * zz, 4)], r.ur.at[z], r.xs.at[2], r.xr.at[2], zz, me).start()

        red.peers(out)
        pltpu.make_async_copy(r.c0.at[pl.ds(2 * z, 2)], r.cr.at[z], r.xr.at[1]).start()
        pltpu.make_async_copy(r.gup.at[pl.ds(4 * z, 4)], r.ur.at[z], r.xr.at[2]).start()

    def planes_sum(self, red):
        r, me, z = self.r, self.me, red.z
        take(r.cr, r.xr.at[1])
        r.cs[...] = jnp.sum(r.cr[...].astype(F32), axis=0).astype(BF16)
        take(r.ur, r.xr.at[2])
        r.us[...] = jnp.sum(r.ur[...].astype(F32), axis=0).astype(BF16)

        def back(zz):
            zcopy(r.cs, r.cf.at[z], r.xs.at[4], r.xr.at[4], zz, me).start()
            zcopy(r.us, r.uf.at[z], r.xs.at[5], r.xr.at[5], zz, me).start()

        red.peers(back)
        pltpu.make_async_copy(r.cs, r.cf.at[z], r.xr.at[4]).start()
        pltpu.make_async_copy(r.us, r.uf.at[z], r.xr.at[5]).start()

    def end(self):
        r, me = self.r, self.me
        take(r.cf, r.xr.at[4])
        take(r.uf, r.xr.at[5])
        take(r.gup.at[pl.ds(0, 31)], r.ks.at[0])

        @pl.when(self.is_pair)
        def _():
            take(r.pq.at[pl.ds(0, 31)], r.ks.at[1])
            first = pair_first(self.p)
            inside = (me >= first) & (me < first + 6)

            @pl.when(inside)
            def _():
                take(r.po.at[pl.ds(0, 5)], r.ks.at[2])

            @pl.when(jnp.logical_not(inside))
            def _():
                take(r.po, r.ks.at[2])

        for n, buf in ((1, r.cr), (2, r.ur), (4, r.cr), (5, r.ur)):
            take(buf.at[pl.ds(0, 7)], r.xs.at[n])


class Plane:
    def __init__(self):
        self.me = lax.axis_index("seg")
        self.x, self.y, self.c = self.me // 8, (self.me // 2) % 4, self.me % 2
        self.other = self.me + 1 - 2 * self.c

    def seg(self, on_x, step):
        if on_x:
            return (((self.x + step) % 4) * 4 + self.y) * 2 + self.c
        return (self.x * 4 + (self.y + step) % 4) * 2 + self.c

    def ring(self, part, which, step):
        return self.seg((part == 0) == (which == 1), step)

    def pos(self, part, which):
        return self.x if (part == 0) == (which == 1) else self.y

    def by_part(self, k, fn):
        for part in range(2):
            pl.when(k % 2 == part)(functools.partial(fn, part))

    @staticmethod
    def ahead(k):
        return 1 + 2 * ((k // 2) % 2)


class Gather(Plane):
    def __init__(self, r):
        super().__init__()
        self.r = r

    def v1(self, k, part, off):
        mine = self.r.ws.at[self.c, k]
        return mine.at[(self.x + off) % 4, self.y] if part == 0 else mine.at[self.x, (self.y + off) % 4]

    def v2(self, k, part, off):
        mine = self.r.ws.at[self.c, k]
        return mine.at[:, (self.y + off) % 4] if part == 0 else mine.at[(self.x + off) % 4]

    def first(self, k):
        r = self.r

        def go(part):
            own = self.v1(k, part, 0)
            src = r.stage.at[k]
            pltpu.make_async_copy(src, own, r.own_sem.at[k]).start()
            rcopy(src, own, r.s1.at[k, 0], r.r1.at[k, 0], self.ring(part, 1, 1)).start()
            rcopy(src, own, r.s1.at[k, 1], r.r1.at[k, 1], self.ring(part, 1, 3)).start()

        self.by_part(k, go)

    def first_on(self, k):
        r, ahead = self.r, self.ahead(k)

        def go(part):
            block = self.v1(k, part, 4 - ahead)
            take(block, r.r1.at[k, ahead // 2])
            rcopy(block, block, r.s1.at[k, 2], r.r1.at[k, 2], self.ring(part, 1, ahead)).start()

        self.by_part(k, go)

    def second(self, k):
        r, ahead = self.r, self.ahead(k)

        def go(part):
            take(self.v1(k, part, ahead), r.r1.at[k, 1 - ahead // 2])
            take(self.v1(k, part, 2), r.r1.at[k, 2])
            own = self.v1(k, part, 0)
            take(own, r.own_sem.at[k])
            row = self.v2(k, part, 0)
            rcopy(row, row, r.s2.at[k, 0], r.r2.at[k, 0], self.ring(part, 2, 1)).start()
            rcopy(row, row, r.s2.at[k, 1], r.r2.at[k, 1], self.ring(part, 2, 3)).start()
            rcopy(row, row, r.s3.at[k, 0], r.r3.at[k, 0], self.other).start()

        self.by_part(k, go)

    def second_on(self, k):
        r, ahead = self.r, self.ahead(k)

        def go(part):
            row = self.v2(k, part, 4 - ahead)
            take(row, r.r2.at[k, ahead // 2])
            rcopy(row, row, r.s2.at[k, 2], r.r2.at[k, 2], self.ring(part, 2, ahead)).start()
            rcopy(row, row, r.s3.at[k, 1], r.r3.at[k, 1], self.other).start()
            row = self.v2(k, part, ahead)
            take(row, r.r2.at[k, 1 - ahead // 2])
            rcopy(row, row, r.s3.at[k, 2], r.r3.at[k, 2], self.other).start()

        self.by_part(k, go)

    def last(self, k):
        r = self.r

        def go(part):
            row = self.v2(k, part, 2)
            take(row, r.r2.at[k, 2])
            rcopy(row, row, r.s3.at[k, 3], r.r3.at[k, 3], self.other).start()

        self.by_part(k, go)

    def arrived(self, k):
        r = self.r
        for n in range(4):
            take(r.ws.at[1 - self.c, k, 0], r.r3.at[k, n])

    def drain(self):
        r = self.r

        def one(k):
            for n in range(4):
                take(r.ws.at[0, 0, 0], r.s3.at[k, n])
            for n in range(3):
                take(r.ws.at[0, 0, 0, 0], r.s1.at[k, n])
                take(r.ws.at[0, 0, 0], r.s2.at[k, n])

        loop(12, one)


F_IN = list(dict(tok=0, cot=0, qkv=0, out=0, up=0, down=0, bias=0, upbias=0, gains=0, cqkv=0, cout=0, cup=0, cdown=0, cbias=0, cupbias=0, cgains=0, pos=0, doc=0))
F_OUT = dict(
    lo=((ROWS, D), BF16),
    ws_o=((2, 12, 4, 4, 48, W), BF16),
    qkv_o=((3, ROWS, D), BF16),
    mix_o=((ROWS, D), BF16),
    n1_o=((ROWS, D), F32),
    n2_o=((ROWS, D), F32),
    f_o=((ROWS, D), BF16),
    g_o=((ROWS, FF), BF16),
    gp_o=((ROWS, FF), BF16),
    rst_o=((2, ROWS, 128), F32),
    lb=((8, D), F32),
    dx=((8, D), F32),
    aw_o=((3, 6, 256, 128), BF16),
    pu=((32, 24, 128), BF16),
    pq=((32, 24, W), BF16),
    po=((6, 24, D), BF16),
    gdn=((96, D), BF16),
    small=((8, D), F32),
    dc=((8, 128), F32),
)
F_HBM = list(dict(aw_o=0, ws_o=0, qkv_o=0, mix_o=0, n1_o=0, n2_o=0, f_o=0, g_o=0, gp_o=0, rst_o=0))
F_SCR = dict(
    ws=VM((2, 12, 4, 4, 48, W), BF16),
    stage=VM((12, 48, W), BF16),
    sibq=VM((24, 3 * D), BF16),
    sibo=VM((24, D), BF16),
    sibu=VM((24, FF), BF16),
    smf=VM((16, W), F32),
    sm=VM((16, W), BF16),
    smg=VM((32, 16, W), BF16),
    both=VM((16, D), F32),
    lub=VM((1, FF), F32),
    cub=VM((8, 128), F32),
    cb=VM((8, D), F32),
    qkvv=VM((3, ROWS, D), BF16),
    mix=VM((ROWS, D), BF16),
    aw=VM((3, 6, 256, 128), BF16),
    n1=VM((ROWS, D), F32),
    n2=VM((ROWS, D), F32),
    f=VM((ROWS, D), BF16),
    g=VM((ROWS, FF), BF16),
    gpl=VM((ROWS, FF), BF16),
    rstl=VM((2, ROWS, 128), F32),
    sib_s=DMA((3,)),
    sib_r=DMA((3,)),
    sm_s=DMA,
    sm_r=DMA,
    own_sem=DMA((12,)),
    s1=DMA((12, 3)),
    r1=DMA((12, 3)),
    s2=DMA((12, 3)),
    r2=DMA((12, 3)),
    s3=DMA((12, 4)),
    r3=DMA((12, 4)),
    keep=DMA((10,)),
    **CROSS,
)


def forward_kernel(*refs):
    r = fields(F_IN + list(F_OUT) + list(F_SCR), refs)
    ring = Gather(r)
    cross = Cross(r, r)
    me, c = ring.me, ring.c
    bar = pltpu.get_barrier_semaphore()
    loop(31, lambda i: pl.semaphore_signal(bar, inc=1, device_id={"seg": (me + 1 + i) % 32}, device_id_type=MESH))
    r.smf[...] = jnp.zeros((16, W), F32)
    r.smf[0:6, 0:24] = r.bias[...].astype(F32)
    r.smf[6:8, 0:24] = r.gains[...].astype(F32)
    r.smf[8:14, 0:24] = r.cbias[...].astype(F32)
    r.smf[14:16, 0:24] = r.cgains[...].astype(F32)
    r.smf[0:1, 128:224] = r.upbias[...].astype(F32)
    table = r.pos[...].astype(F32)
    for t in range(2):
        for i in range(6):
            r.smf[6 * t + i : 6 * t + i + 1, 256:384] = table[t : t + 1, 128 * i : 128 * (i + 1)]
    r.sm[...] = r.smf[...].astype(BF16)
    r.cub[...] = jnp.zeros((8, 128), F32)
    r.cub[0:1, 0:96] = r.cupbias[...].astype(F32)
    pl.semaphore_wait(bar, 31)

    swaps = [(r.qkv, r.sibq), (r.out, r.sibo), (r.up, r.sibu)]
    for i, (src, dst) in enumerate(swaps):
        rcopy(src, dst, r.sib_s.at[i], r.sib_r.at[i], ring.other).start()
    for j in range(4):
        r.stage[8 + j] = r.down[(j % 2) * 48 : (j % 2) * 48 + 48, (j // 2) * W : (j // 2 + 1) * W]

    def compose(k, src, sib, block):
        own = src[:, col(block)].astype(F32)
        oth = sib[:, col(block)].astype(F32)
        lo, hi = jnp.where(c == 0, own, oth), jnp.where(c == 0, oth, own)
        r.stage[k] = jnp.concatenate([lo, hi], axis=0).astype(BF16)
        ring.first(k)

    def arrive(i):
        take(swaps[i][1], r.sib_r.at[i])

    arrive(0)
    loop(3, lambda k: compose(k, r.qkv, r.sibq, 2 * k + c))
    arrive(1)
    compose(3, r.out, r.sibo, c)
    arrive(2)
    loop(8, lambda k: compose(k, r.up, r.sibu, 2 * (k - 4) + c), 4)
    loop(12, ring.first, 8)
    loop(32, lambda t: send_to(me, t, r.sm, r.smg.at[me], r.sm_s, r.sm_r))
    loop(12, ring.first_on)
    loop(6, ring.second)
    cross.reshard()

    take(r.smg, r.sm_r)
    for t in range(32):
        block = r.smg[t].astype(F32)
        r.both[:, 24 * t : 24 * t + 24] = block[:, 0:24]
        r.lub[:, 96 * t : 96 * t + 96] = block[0:1, 128:224]
    r.lb[...] = r.both[0:8, :]
    r.cb[...] = r.both[8:16, :]

    def tick(k):
        ring.second_on(k)

        @pl.when(k < 6)
        def _():
            ring.second(k + 6)

        @pl.when(k >= 3)
        def _():
            ring.last(k - 3)

    def weight(cc, k):
        return r.ws[cc, k].reshape(D, W)

    loop(5, tick)

    def project(k):
        tick(k)
        i = k - 5
        ring.arrived(i)
        shift = jnp.where(i == 0, r.lb[0:1, :], jnp.where(i == 2, r.lb[1:2, :], 0.0))
        for cc in range(2):
            part = slice(cc * W, (cc + 1) * W)
            r.qkvv[i, :, part] = (dot(r.tok[...], weight(cc, i)) + shift[:, part]).astype(BF16)

    loop(8, project, 5)

    def attend(k):
        tick(k)
        s = k - 8
        rows = pl.ds(pl.multiple_of(s * 128, 128), 128)
        for p in range(6):
            part = slice(128 * p, 128 * (p + 1))
            w = softmax(dot_bt(two_heads(r.qkvv[0, rows, part]), r.qkvv[1, rows, part]) * 0.125).astype(BF16)
            r.aw[s, p] = w
            r.mix[rows, part] = side_by_side(dot(w, r.qkvv[2, rows, part])).astype(BF16)

    loop(11, attend, 8)
    tick(11)
    ring.arrived(3)
    for cc in range(2):
        part = slice(cc * W, (cc + 1) * W)
        r.n1[:, part] = dot(r.mix[...], weight(cc, 3)) + (r.tok[:, part].astype(F32) + r.lb[2:3, part])
    ring.last(9)

    def blocks(fn):
        loop(ROWS // 64, lambda i: fn(pl.ds(pl.multiple_of(i * 64, 64), 64)))

    def norm_one(rows):
        n, rstd = norm(r.n1[rows, :])
        r.n1[rows, :] = n
        r.rstl[0, rows, :] = jnp.broadcast_to(rstd, (64, 128))
        r.f[rows, :] = (n * r.lb[6:7, :] + r.lb[3:4, :]).astype(BF16)

    blocks(norm_one)

    def raise_up(i):
        ring.arrived(i)

        def half(cc):
            part = col(2 * (i - 4) + cc)
            u = dot(r.f[...], weight(cc, i)) + r.lub[0:1, part]
            g, gp = gelu_both(u)
            r.g[:, part] = g.astype(BF16)
            r.gpl[:, part] = gp.astype(BF16)

        loop(2, half)

        @pl.when(i < 6)
        def _():
            ring.last(i + 6)

    loop(8, raise_up, 4)

    def lower(kc):
        for j in range(2):
            ring.arrived(8 + 2 * kc + j)
        part = slice(kc * W, (kc + 1) * W)
        r.n2[:, part] = r.f[:, part].astype(F32) + r.lb[4:5, part]

        def quarter(x):
            pieces = [r.ws[cc, 8 + 2 * kc + j, x, y] for y in range(4) for cc in range(2) for j in range(2)]
            r.n2[:, part] += dot(r.g[:, col(x, D)], jnp.concatenate(pieces, axis=0))

        loop(4, quarter)

    lower(0)
    lower(1)

    def norm_two(rows):
        n, rstd = norm(r.n2[rows, :])
        r.n2[rows, :] = n
        r.rstl[1, rows, :] = jnp.broadcast_to(rstd, (64, 128))
        r.lo[rows, :] = (n * r.lb[7:8, :] + r.lb[5:6, :]).astype(BF16)

    blocks(norm_two)

    row = lax.broadcasted_iota(jnp.int32, (8, D), 0)
    z0 = jnp.zeros((8, D), F32)
    dy0 = jnp.zeros((8, D), F32)
    for s in range(3):
        z0 = jnp.where(row == s, r.n2[128 * s : 128 * s + 1, :] * r.lb[7:8, :] + r.lb[5:6, :], z0)
        dy0 = jnp.where(row == s, r.cot[128 * s : 128 * s + 16, :].astype(F32)[0:1, :], dy0)
    cross.reshard_end()
    cross.start(z0, dy0)
    kept = [
        (r.ws, r.ws_o), (r.qkvv, r.qkv_o), (r.mix, r.mix_o), (r.n1, r.n1_o), (r.n2, r.n2_o), (r.f, r.f_o),
        (r.g, r.g_o), (r.gpl, r.gp_o), (r.rstl, r.rst_o), (r.aw, r.aw_o),
    ]
    for i, (src, dst) in enumerate(kept):
        pltpu.make_async_copy(src, dst, r.keep.at[i]).start()
    cross.attention()
    cross.first_norm()
    cross.mlp()
    cross.second_norm()
    cross.mlp_back()
    cross.first_norm_back()
    cross.attention_back()
    y = cross.output_rows()
    row16 = lax.broadcasted_iota(jnp.int32, (16, D), 0)
    for s in range(3):
        old = r.lo[128 * s : 128 * s + 16, :].astype(F32)
        r.lo[128 * s : 128 * s + 16, :] = jnp.where(row16 == 0, y[s : s + 1, :], old).astype(BF16)
    cross.grads()
    r.dx[...] = cross.finish()
    cross.drain()
    ring.drain()
    for i, (src, dst) in enumerate(swaps):
        take(src, r.sib_s.at[i])
    take(r.smg.at[pl.ds(0, 31)], r.sm_s)
    for i, (src, dst) in enumerate(kept):
        take(dst, r.keep.at[i])


B_IN = list(dict(tok=0, cot=0, ws_o=0, qkv_o=0, mix_o=0, n1_o=0, n2_o=0, f_o=0, g_o=0, gp_o=0, rst_o=0, aw_o=0, lb=0, dx=0, pu=0, pq=0, po=0, gdn=0, small=0, dc=0, doc=0))
B_OUT = dict(
    tg=((ROWS, D), F32),
    fa=((16, 24, W), BF16),
    fd=((8, 24, W), BF16),
    cf=((8, 2, 24, W), BF16),
    uf=((8, 4, 24, 128), BF16),
    osm=((12, 8, D), F32),
)
B_SCR = dict(
    qkv=VM((3, ROWS, D), BF16),
    mix=VM((ROWS, D), BF16),
    aw=VM((3, 6, 256, 128), BF16),
    gup=VM((32, 24, 128), BF16),
    gqkv=VM((6, 24, W), BF16),
    go=VM((2, 24, D), BF16),
    n1=VM((ROWS, D), F32),
    n2=VM((ROWS, D), F32),
    f=VM((ROWS, D), BF16),
    g=VM((ROWS, FF), BF16),
    gp=VM((ROWS, FF), BF16),
    rst=VM((2, ROWS, 128), F32),
    dd=VM((ROWS, D), BF16),
    de=VM((ROWS, D), BF16),
    dqkv=VM((3, ROWS, D), BF16),
    wdb=VM((2, 2, 4, 48, D), BF16),
    wub=VM((2, 4, 4, 48, W), BF16),
    wo=VM((2, 4, 4, 48, W), BF16),
    wq=VM((2, 3, 4, 4, 48, W), BF16),
    gb=VM((2, 12, 4, 4, 48, W), BF16),
    r0=VM((12, 4, 4, 48, W), BF16),
    f2=VM((12, 4, 48, W), BF16),
    a2=VM((12, 4, 48, W), BF16),
    b2=VM((12, 4, 48, W), BF16),
    t1=VM((12, 4, 48, W), BF16),
    f1=VM((12, 48, W), BF16),
    a1=VM((12, 48, W), BF16),
    b1=VM((12, 48, W), BF16),
    z0=VM((3, 8, 24, W), BF16),
    zr=VM((3, 8, 24, W), BF16),
    zs=VM((3, 24, W), BF16),
    c0=VM((16, 24, W), BF16),
    cr=VM((8, 2, 24, W), BF16),
    cs=VM((2, 24, W), BF16),
    ur=VM((8, 4, 24, 128), BF16),
    us=VM((4, 24, 128), BF16),
    sf=VM((96, D), F32),
    s0=VM((12, 8, D), BF16),
    sg=VM((32, 8, D), BF16),
    s1=VM((8, D), F32),
    sz=VM((31, 8, D), F32),
    s2=VM((8, D), F32),
    dcl=VM((1, FF), F32),
    mr=DMA((12, 7)),
    ms=DMA((12, 7)),
    xr=DMA((8,)),
    xs=DMA((8,)),
    zsr=DMA((3, 2)),
    zss=DMA((3, 2)),
    keep=DMA((9,)),
    ks=DMA((3,)),
    kr=DMA((3,)),
    wds=DMA((2, 8)),
    wus=DMA((2,)),
    wos=DMA((2,)),
    wqs=DMA((2,)),
)


class Reduce(Plane):
    def __init__(self, r):
        super().__init__()
        self.r = r
        self.z = lax.axis_index("grp")

    @staticmethod
    def unit(i):
        return jnp.where(i < 4, 8 + i, jnp.where(i < 8, i, jnp.where(i == 8, 3, i - 9)))

    def peers(self, fn):
        loop(7, lambda i: fn((self.z + 1 + i) % 8))

    def to_sibling(self, k):
        r = self.r
        rcopy(r.gb.at[1, k], r.r0.at[k], r.ms.at[k, 0], r.mr.at[k, 0], self.other).start()

    def msg(self, k, part, q):
        return self.r.gb.at[0, k, :, q] if part == 0 else self.r.gb.at[0, k, q]

    def step_a(self, k):
        r, ahead = self.r, self.ahead(k)
        take(r.r0.at[k], r.mr.at[k, 0])

        def add(i):
            px, py = i // 4, i % 4
            r.gb[0, k, px, py] = (r.gb[0, k, px, py].astype(F32) + r.r0[k, px, py].astype(F32)).astype(BF16)

        loop(16, add)

        def go(part):
            q = self.pos(part, 2)
            far, back = self.msg(k, part, (q + 2) % 4), self.msg(k, part, (q + 4 - ahead) % 4)
            rcopy(far, r.f2.at[k], r.ms.at[k, 1], r.mr.at[k, 1], self.ring(part, 2, ahead)).start()
            rcopy(back, r.b2.at[k], r.ms.at[k, 2], r.mr.at[k, 2], self.ring(part, 2, 4 - ahead)).start()

        self.by_part(k, go)

    def step_b(self, k):
        r, ahead = self.r, self.ahead(k)
        take(r.f2.at[k], r.mr.at[k, 1])

        def go(part):
            block = self.msg(k, part, (self.pos(part, 2) + ahead) % 4)

            def add(i):
                block[i] = (block[i].astype(F32) + r.f2[k, i].astype(F32)).astype(BF16)

            loop(4, add)
            rcopy(block, r.a2.at[k], r.ms.at[k, 3], r.mr.at[k, 3], self.ring(part, 2, ahead)).start()

        self.by_part(k, go)

    def step_c(self, k):
        r, ahead = self.r, self.ahead(k)
        take(r.a2.at[k], r.mr.at[k, 3])
        take(r.b2.at[k], r.mr.at[k, 2])

        def go(part):
            block = self.msg(k, part, self.pos(part, 2))

            def add(i):
                r.t1[k, i] = (block[i].astype(F32) + r.a2[k, i].astype(F32) + r.b2[k, i].astype(F32)).astype(BF16)

            loop(4, add)
            q = self.pos(part, 1)
            far, back = r.t1.at[k, (q + 2) % 4], r.t1.at[k, (q + 4 - ahead) % 4]
            rcopy(far, r.f1.at[k], r.ms.at[k, 4], r.mr.at[k, 4], self.ring(part, 1, ahead)).start()
            rcopy(back, r.b1.at[k], r.ms.at[k, 5], r.mr.at[k, 5], self.ring(part, 1, 4 - ahead)).start()

        self.by_part(k, go)

    def step_d(self, k):
        r, ahead = self.r, self.ahead(k)
        take(r.f1.at[k], r.mr.at[k, 4])

        def go(part):
            n = (self.pos(part, 1) + ahead) % 4
            r.t1[k, n] = (r.t1[k, n].astype(F32) + r.f1[k].astype(F32)).astype(BF16)
            rcopy(r.t1.at[k, n], r.a1.at[k], r.ms.at[k, 6], r.mr.at[k, 6], self.ring(part, 1, ahead)).start()

        self.by_part(k, go)

    def step_e(self, i):
        r = self.r
        k = self.unit(i)
        take(r.a1.at[k], r.mr.at[k, 6])
        take(r.b1.at[k], r.mr.at[k, 5])

        def go(part):
            t = r.t1[k, self.pos(part, 1)].astype(F32) + r.a1[k].astype(F32) + r.b1[k].astype(F32)
            r.z0[i // 4, pl.ds(2 * (i % 4), 2)] = t.reshape(2, 24, W).astype(BF16)

        self.by_part(k, go)

    def z_send(self, g):
        r, z, me = self.r, self.z, self.me
        self.peers(lambda zz: zcopy(r.z0.at[g, zz], r.zr.at[g, z], r.zss.at[g, 0], r.zsr.at[g, 0], zz, me).start())
        pltpu.make_async_copy(r.z0.at[g, z], r.zr.at[g, z], r.zsr.at[g, 0]).start()

    def z_sum(self, g):
        r, z, me, c = self.r, self.z, self.me, self.c
        take(r.zr.at[g], r.zsr.at[g, 0])
        r.zs[g] = jnp.sum(r.zr[g].astype(F32), axis=0).astype(BF16)
        m, h = z // 2, z % 2

        def out(dst, sem, seg):
            def one(zz):
                here = (zz == z) & (seg == me)

                @pl.when(here)
                def _():
                    pltpu.make_async_copy(r.zs.at[g], dst, sem).start()

                @pl.when(jnp.logical_not(here))
                def _():
                    zcopy(r.zs.at[g], dst, r.zss.at[g, 1], sem, zz, seg).start()

            loop(8, one)

        if g == 0:
            out(r.fd.at[z], r.zsr.at[0, 1], me)
        elif g == 1:
            out(r.fa.at[8 + 2 * m + c], r.zsr.at[1, 1], me - c + h)
        else:
            out(r.fa.at[2 * ((m + 3) % 4) + c], r.zsr.at[2, 1], me - c + h)

    def drain(self):
        r, z, c = self.r, self.z, self.c

        def one(k):
            take(r.r0.at[k], r.ms.at[k, 0])
            for n in range(1, 4):
                take(r.f2.at[k], r.ms.at[k, n])
            for n in range(4, 7):
                take(r.f1.at[k], r.ms.at[k, n])

        loop(12, one)
        for g in range(3):
            take(r.zr.at[g, pl.ds(0, 7)], r.zss.at[g, 0])
            stays = (z % 2 == c) if g > 0 else (z >= 0)

            @pl.when(stays)
            def _():
                take(r.zr.at[g, pl.ds(0, 7)], r.zss.at[g, 1])

            @pl.when(jnp.logical_not(stays))
            def _():
                take(r.zr.at[g], r.zss.at[g, 1])


def backward_kernel(*refs):
    r = fields(B_IN + list(B_OUT) + list(B_SCR), refs)
    red = Reduce(r)
    me, c, z = red.me, red.c, red.z
    is_owner = (c == 0) & (me < 24)
    cross = CrossGrads(r, r)
    loads = [
        (r.n2_o, r.n2), (r.rst_o, r.rst), (r.g_o, r.g), (r.gp_o, r.gp), (r.f_o, r.f), (r.n1_o, r.n1),
        (r.mix_o, r.mix), (r.qkv_o, r.qkv), (r.aw_o, r.aw),
    ]
    for i, (src, dst) in enumerate(loads):
        pltpu.make_async_copy(src, dst, r.keep.at[i]).start()

    def have(i):
        take(loads[i][1], r.keep.at[i])

    bar = pltpu.get_barrier_semaphore()
    loop(31, lambda i: pl.semaphore_signal(bar, inc=1, device_id={"grp": z, "seg": (me + 1 + i) % 32}, device_id_type=MESH))

    def greet_z(zz):
        for seg in (me, red.other):
            pl.semaphore_signal(bar, inc=1, device_id={"grp": zz, "seg": seg}, device_id_type=MESH)

    red.peers(greet_z)

    def down_block(b, start):
        for cc in range(2):
            for j in range(4):
                cp = pltpu.make_async_copy(
                    r.ws_o.at[cc, 8 + j, b // 2, pl.ds(2 * (b % 2), 2)],
                    r.wdb.at[b % 2, :, 2 * cc + j % 2, :, pl.ds((j // 2) * W, W)],
                    r.wds.at[b % 2, 4 * cc + j],
                )
                cp.start() if start else cp.wait()

    def up_block(b, start):
        cp = pltpu.make_async_copy(r.ws_o.at[b % 2, 4 + b // 2], r.wub.at[b % 2], r.wus.at[b % 2])
        cp.start() if start else cp.wait()

    down_block(0, True)
    up_block(0, True)
    for cc in range(2):
        pltpu.make_async_copy(r.ws_o.at[cc, 3], r.wo.at[cc], r.wos.at[cc]).start()
        pltpu.make_async_copy(r.ws_o.at[cc, pl.ds(0, 3)], r.wq.at[cc], r.wqs.at[cc]).start()

    def blocks(fn):
        loop(ROWS // 64, lambda i: fn(pl.ds(pl.multiple_of(i * 64, 64), 64)))

    sf = r.sf
    sf[...] = jnp.zeros((96, D), F32)
    have(0)
    have(1)
    row = lax.broadcasted_iota(jnp.int32, (64, D), 0)

    def norm_two(i):
        rows = pl.ds(pl.multiple_of(i * 64, 64), 64)
        first = r.dx[pl.ds(i // 2, 1), :]
        dy = jnp.where((row == 0) & (i % 2 == 0), first, r.cot[rows, :].astype(F32))
        n = r.n2[rows, :]
        dr2 = norm_back(dy, n, r.rst[1, rows, 0:1], r.lb[7:8, :])
        dd = dr2.astype(BF16)
        r.n2[rows, :] = dr2
        r.dd[rows, :] = dd
        sf[5:6, :] += sum0(dy)
        sf[7:8, :] += sum0(dy * n)
        sf[4:5, :] += sum0(dd.astype(F32))

    loop(6, norm_two)
    have(2)

    def down_grad(b):
        v = dot_at(r.g[:, col(b)], r.dd[...]).astype(BF16).reshape(2, 2, 2, 48, D)
        for chip in range(2):
            for cc in range(2):
                for j in range(4):
                    r.gb[(cc + c) % 2, 8 + j, b // 2, 2 * (b % 2) + chip] = v[chip, cc, j % 2, :, (j // 2) * W : (j // 2 + 1) * W]

    loop(8, down_grad)
    pl.semaphore_wait(bar, 45)
    loop(12, red.to_sibling, 8)

    cross.scatter()

    def tick(t):
        def run(lag, fn):
            @pl.when((t >= lag) & (t < lag + 12))
            def _():
                fn(t - lag)

        run(0, lambda i: red.step_a(red.unit(i)))
        run(2, lambda i: red.step_b(red.unit(i)))
        run(4, lambda i: red.step_c(red.unit(i)))
        run(5, lambda i: red.step_d(red.unit(i)))
        run(6, red.step_e)

    have(3)
    have(4)

    def middle(b):
        @pl.when(b < 7)
        def _():
            down_block(b + 1, True)
            up_block(b + 1, True)

        part = col(b)
        down_block(b, False)
        dg = dot_bt(r.dd[...], r.wdb[b % 2].reshape(W, D))
        du = (dg * r.gp[:, part].astype(F32)).astype(BF16)
        r.dcl[:, part] = sum0(du.astype(F32))
        up_block(b, False)
        r.n2[...] += dot_bt(du, r.wub[b % 2].reshape(D, W))
        r.gb[(b + c) % 2, 4 + b // 2] = dot_at(r.f[...], du).astype(BF16).reshape(4, 4, 48, W)

        @pl.when(b % 2 == 1)
        def _():
            red.to_sibling(4 + b // 2)
            tick(b // 2)

        @pl.when(b == 4)
        def _():
            cross.planes(red)

    loop(8, middle)
    have(5)

    def norm_one(rows):
        df, n = r.n2[rows, :], r.n1[rows, :]
        dr1 = norm_back(df, n, r.rst[0, rows, 0:1], r.lb[6:7, :])
        de = dr1.astype(BF16)
        r.n2[rows, :] = dr1
        r.de[rows, :] = de
        sf[3:4, :] += sum0(df)
        sf[6:7, :] += sum0(df * n)
        sf[2:3, :] += sum0(de.astype(F32))

    blocks(norm_one)
    have(6)
    for cc in range(2):
        r.gb[(cc + c) % 2, 3] = dot_at(r.mix[...], r.de[:, cc * W : (cc + 1) * W]).astype(BF16).reshape(4, 4, 48, W)
    red.to_sibling(3)
    for cc in range(2):
        take(r.wo.at[cc], r.wos.at[cc])
        part = dot_bt(r.de[:, cc * W : (cc + 1) * W], r.wo[cc].reshape(D, W))
        if cc == 0:
            r.n1[...] = part
        else:
            r.dd[...] = (r.n1[...] + part).astype(BF16)
    tick(4)
    have(7)
    have(8)

    def attend_back(s):
        rows = pl.ds(pl.multiple_of(s * 128, 128), 128)
        for p in range(6):
            part = slice(128 * p, 128 * (p + 1))
            q, k, v = r.qkv[0, rows, part], r.qkv[1, rows, part], r.qkv[2, rows, part]
            do = two_heads(r.dd[rows, part])
            w = r.aw[s, p]
            ds = softmax_back(w.astype(F32), dot_bt(do, v)).astype(BF16)
            r.dqkv[0, rows, part] = (side_by_side(dot(ds, k)) * 0.125).astype(BF16)
            r.dqkv[1, rows, part] = (dot_at(ds, two_heads(q)) * 0.125).astype(BF16)
            r.dqkv[2, rows, part] = dot_at(w, do).astype(BF16)
        tick(5 + s)

    loop(3, attend_back)
    cross.planes_sum(red)

    sf[0:1, :] = sum0(r.dqkv[0].astype(F32))
    sf[1:2, :] = sum0(r.dqkv[2].astype(F32))
    sf[8:16, :] = r.small[...]
    for i in range(4):
        sf[16 + i : 17 + i, :] = r.dcl[:, D * i : D * (i + 1)]
    own = jnp.concatenate([r.dc[0:1, :], jnp.zeros((1, D - 128), F32)], axis=1)
    own = pltpu.roll(own, 96 * (me % 8), 1)
    sf[pl.ds(20 + me // 8, 1), :] = own
    line = lax.broadcasted_iota(jnp.int32, (64, D), 0)
    for s in range(3):
        _, place = slot_layout(r.doc, (64, D), jnp.full((64, D), me * 3 + s, jnp.int32))
        sf[24:88, :] += jnp.where(line == place, r.dx[s : s + 1, :], 0.0)
    r.s0[...] = sf[...].reshape(12, 8, D).astype(BF16)
    xs, xr = r.xs, r.xr
    loop(12, lambda k: send_to(me, owner_seg(k), r.s0.at[k], r.sg.at[me], xs.at[0], xr.at[0]))

    def qkv_grad(i):
        for cc in range(2):
            part = slice(cc * W, (cc + 1) * W)
            r.gb[(cc + c) % 2, i] = dot_at(r.tok[...], r.dqkv[i, :, part]).astype(BF16).reshape(4, 4, 48, W)
        red.to_sibling(i)
        tick(8 + i)

    loop(3, qkv_grad)
    red.z_send(0)

    @pl.when(is_owner)
    def _():
        take(r.sg, xr.at[0])
        r.s1[...] = jnp.sum(r.sg[...].astype(F32), axis=0)
        red.peers(lambda zz: zcopy(r.s1, r.sz.at[z], xs.at[3], xr.at[3], zz, me).start())
        pltpu.make_async_copy(r.s1, r.sz.at[z], xr.at[3]).start()

    tick(11)
    for cc in range(2):
        take(r.wq.at[cc], r.wqs.at[cc])
    r.tg[...] = r.n2[...]

    def token_grad(i):
        acc = dot_bt(r.dqkv[i, :, 0:W], r.wq[0, i].reshape(D, W))
        r.tg[...] += acc + dot_bt(r.dqkv[i, :, W : 2 * W], r.wq[1, i].reshape(D, W))

    token_grad(0)
    tick(12)
    token_grad(1)
    red.z_sum(0)
    tick(13)
    red.z_send(1)
    token_grad(2)
    tick(14)

    @pl.when(is_owner)
    def _():
        take(r.sz.at[pl.ds(0, 8)], xr.at[3])
        r.s2[...] = jnp.sum(r.sz[0:8], axis=0)
        loop(32, lambda t: send_to(me, t, r.s2, r.osm.at[me // 2], xs.at[6], xr.at[6]))

    tick(15)
    red.z_sum(1)
    tick(16)
    tick(17)
    red.z_send(2)
    red.z_sum(2)
    for g, ref in ((0, r.fd), (1, r.fa.at[pl.ds(8, 8)]), (2, r.fa.at[pl.ds(0, 8)])):
        take(ref, r.zsr.at[g, 1])
    take(r.osm, xr.at[6])
    cross.end()
    red.drain()

    @pl.when(is_owner)
    def _():
        take(r.sg.at[pl.ds(0, 11)], xs.at[0])
        take(r.sz.at[pl.ds(0, 7)], xs.at[3])
        take(r.sz, xs.at[6])

    @pl.when(jnp.logical_not(is_owner))
    def _():
        take(r.sg.at[pl.ds(0, 12)], xs.at[0])


FORMAT_IN = list(dict(lo=0, tg=0, fa=0, fd=0, cf=0, uf=0, osm=0))
FORMAT_OUT = dict(
    lo_o=((ROWS, D), BF16),
    tg_o=((ROWS, D), F32),
    oq=((24, 3 * D), F32),
    oo=((24, D), F32),
    ou=((24, FF), F32),
    od=((96, D), F32),
    ob=((6, 24), F32),
    ouv=((1, 96), F32),
    og=((2, 24), F32),
    xoq=((24, 3 * D), F32),
    xoo=((24, D), F32),
    xou=((24, FF), F32),
    xod=((96, D), F32),
    xob=((6, 24), F32),
    xouv=((1, 96), F32),
    xog=((2, 24), F32),
    opos=((2, D), F32),
)


def format_kernel(*refs):
    r = fields(FORMAT_IN + list(FORMAT_OUT), refs)
    me = lax.axis_index("seg")
    r.lo_o[...] = r.lo[...]
    r.tg_o[...] = r.tg[...]
    for p in range(6):
        for j in range(3):
            r.xoq[:, D * j + 128 * p : D * j + 128 * (p + 1)] = r.cf[p // 2, p % 2, :, 128 * j : 128 * (j + 1)].astype(F32)
    for i in range(2):
        r.xoo[:, W * i : W * (i + 1)] = r.cf[3, i].astype(F32)
        for n in range(4):
            m = 8 + 4 * i + n
            r.xod[24 * n : 24 * (n + 1), W * i : W * (i + 1)] = r.cf[m // 2, m % 2].astype(F32)
    for t in range(32):
        r.xou[:, 96 * t : 96 * t + 96] = r.uf[t // 4, t % 4].astype(F32)[:, 0:96]
    for n in range(8):
        j, h = n // 2, n % 2
        top = (j % 2) * 48 + 24 * h
        r.od[top : top + 24, (j // 2) * W : (j // 2 + 1) * W] = r.fd[n].astype(F32)
    for u in range(8, 16):
        r.ou[:, W * (u - 8) : W * (u - 7)] = r.fa[u].astype(F32)
    ours = pltpu.roll(r.osm[0:2].reshape(16, D), (D - 24 * me) % D, 1)
    r.ob[...] = ours[0:6, 0:24]
    r.og[...] = ours[6:8, 0:24]
    r.xob[...] = ours[8:14, 0:24]
    r.xog[...] = ours[14:16, 0:24]
    ups = pltpu.roll(r.osm[2], (D - 96 * (me % 8)) % D, 1)
    line = lax.broadcasted_iota(jnp.int32, (8, D), 0)
    r.ouv[...] = sum0(jnp.where(line == me // 8, ups, 0.0))[:, 0:96]
    r.xouv[...] = sum0(jnp.where(line == 4 + me // 8, ups, 0.0))[:, 0:96]
    r.opos[...] = pltpu.roll(r.osm[3 + me // 4], (8 - 2 * (me % 4)) % 8, 0)[0:2]
    for u in range(8):
        if u < 6:
            r.oq[:, W * u : W * (u + 1)] = r.fa[u].astype(F32)
        else:
            r.oo[:, W * (u - 6) : W * (u - 5)] = r.fa[u].astype(F32)


def call(kernel, name, ins, outs, hbm_in, hbm_out, scratch, cid, args):
    vm, hbm = pl.BlockSpec(memory_space=pltpu.VMEM), pl.BlockSpec(memory_space=pl.ANY)
    smem = pl.BlockSpec(memory_space=pltpu.SMEM)
    return pl.pallas_call(
        kernel,
        out_shape=tuple(jax.ShapeDtypeStruct(s, t) for s, t in outs.values()),
        in_specs=[smem if n == "doc" else hbm if n in hbm_in else vm for n in ins],
        out_specs=tuple(hbm if n in hbm_out else vm for n in outs),
        scratch_shapes=list(scratch.values()),
        compiler_params=pltpu.CompilerParams(
            collective_id=cid, has_side_effects=cid is not None, vmem_limit_bytes=62 << 20
        ),
        name=name,
    )(*args)


def shards(tokens, doc, qkv, out, up, down, bias, upbias, gains, cqkv, cout, cup, cdown, cbias, cupbias, cgains, pos, cot):
    fwd = call(
        forward_kernel, "forward", F_IN, F_OUT, (), F_HBM, F_SCR, 0,
        (tokens, cot, qkv, out, up, down, bias, upbias.reshape(1, 96), gains, cqkv, cout, cup, cdown, cbias,
         cupbias.reshape(1, 96), cgains, pos, doc),
    )
    saved = dict(zip(F_OUT, fwd), tok=tokens, cot=cot, doc=doc)
    back = call(
        backward_kernel, "backward", B_IN, B_OUT, F_HBM, (), B_SCR, 1, [saved[n] for n in B_IN]
    )
    saved.update(zip(B_OUT, back))
    out = call(
        format_kernel, "format", FORMAT_IN, FORMAT_OUT, (), (), {}, None, [saved[n] for n in FORMAT_IN]
    )
    out = dict(zip(FORMAT_OUT, out))
    out["ouv"], out["xouv"] = out["ouv"].reshape(96), out["xouv"].reshape(96)
    return tuple(out.values())


def solution(mesh):
    both, seg, cols, flat = P(("grp", "seg"), None), P("seg", None), P(None, "seg"), P("seg")
    weights = (seg, seg, seg, seg, cols, flat, cols)
    in_specs = (both, P("grp", None)) + weights + weights + (seg, both)
    out_specs = (both, both) + weights + weights + (seg,)
    return jax.shard_map(shards, mesh=mesh, in_specs=in_specs, out_specs=out_specs, check_vma=False)
```

time: 1600 us -> 232 us (0.14)
  waiting for transfers between devices: 941 us -> 0 us
  blocking collectives: 383 us -> 0 us
  Pallas kernels: 0 us -> 231 us
  matrix products: 118 us -> 0 us
  local copies, waits for them, and re-layouts: 76.6 us -> 0 us
  other arithmetic: 49.8 us -> 0 us
  between operations: 18.9 us -> 0.83 us
    reduce_scatter x7 -> x0, waiting for transfers between devices: 530 us -> none  [the longest x1 95.1 us: shards(): lax.psum_scatter(local_grads[2].astype(jnp.bfloat16), 'seg', scatter_dime...]
    unnamed x2 -> x0, blocking collectives: 242 us -> none
    pallas_call x0 -> x3, Pallas kernels: none -> 231 us  [call(): pl.pallas_call(kernel, out_shape=tuple((jax.ShapeDtypeStruct(s, t) for s,...]
    unnamed x23 -> x0, waiting for transfers between devices: 205 us -> none
    all_gather x6 -> x0, blocking collectives: 141 us -> none  [the longest x1 25.8 us: shards(): lax.all_gather(local_bias, 'seg', axis=1, tiled=True)]
    psum x2 -> x0, waiting for transfers between devices: 137 us -> none  [the longest x1 69.4 us: shards(): lax.psum(local_share[0].astype(jnp.bfloat16), 'grp').astype(jnp.float32)]
    dot_general x39 -> x0, matrix products: 118 us -> none  [the longest x2 19.8 us: tail_ahead(): jnp.dot(first_norm, w_up, preferred_element_type=jnp.float32) + up_bias]
    all_gather x8 -> x0, waiting for transfers between devices: 69.9 us -> none  [the longest x1 50.1 us: shards(): lax.all_gather(cross_down, 'seg', axis=0, tiled=True)]
  transfers between devices with their start and end apart: 20 -> 0, of which waited for: 12 -> 0; matrix products, arithmetic and copies ran while one was open for 12% -> 0% of each run, Pallas kernels for 0% -> 0%
where the time goes in v1:
time: 232 us; the launch traced here: 231 us
  Pallas kernels  231 us (100%)
    pallas_call x3, Pallas kernels, call(): pl.pallas_call(kernel, out_shape=tuple((jax.ShapeDtypeStruct(s, t) for s,...  231 us

profile of v1, /device:TPU:1, one launch (start us, length us, event | category | flops | bytes accessed | tf_op | source)
XLA Modules:
  0.0 231.5 jit_solution(6671987538770792543)
XLA Ops:
  0.7 127.1 %forward.1 = (bf16[384,768]{1,0:T(8,128)(2,1)}, bf16[2,12,4,4,48,384]{5,4,3,2,1,0:T(8,128)(2,1)}, bf16[3,384,768]{2,1,0:T(8,128)(2,1)}, bf16[384,768]{1,0:T(8,12...) custom-call(bf16[384,768]{1,0:T(8,128)(2,1)} %refs_0_.3, ...), custom_call_target="tpu_custom_call" | custom-call | tf_op jit(solution)/shard_map/forward/pallas_call | solution.py:1497
  127.8 99.8 %backward.1 = (f32[384,768]{1,0:T(8,128)}, bf16[16,24,384]{2,1,0:T(8,128)(2,1)}, bf16[8,24,384]{2,1,0:T(8,128)(2,1)}, bf16[8,2,24,384]{3,2,1,0:T(8,128)(2,1)}, b...) custom-call(bf16[384,768]{1,0:T(8,128)(2,1)} %refs_0_.3, bf16[384,768]{1,0:T(8,128)(2,1)} %refs_1_.3, ...), custom_call_target="tpu_custom_call" | custom-call | tf_op jit(solution)/shard_map/backward/pallas_call | solution.py:1497
  227.6 3.7 %format.1 = (bf16[384,768]{1,0:T(8,128)(2,1)}, f32[384,768]{1,0:T(8,128)}, f32[24,2304]{1,0:T(8,128)}, f32[24,768]{1,0:T(8,128)}, f32[24,3072]{1,0:T(8,128)}, /*...) custom-call(bf16[384,768]{1,0:T(8,128)(2,1)} %get-tuple-element.59.r, ...), custom_call_target="tpu_custom_call" | custom-call | tf_op jit(solution)/shard_map/format/pallas_call | solution.py:1497

commit v2 on v1

v2 whole, which is shorter than its diff:
```python
import functools
import math
import types

import jax
import jax.numpy as jnp
from jax import lax
from jax.experimental import pallas as pl
from jax.experimental.pallas import tpu as pltpu
from jax.sharding import PartitionSpec as P

D = 768
FF = 3072
ROWS = 384
SEG_LEN = 128
W = 384
F32, BF16 = jnp.float32, jnp.bfloat16
MESH = pl.DeviceIdType.MESH
DMA = pltpu.SemaphoreType.DMA
RSQ2 = 1.0 / math.sqrt(2.0)
RS2PI = 1.0 / math.sqrt(2.0 * math.pi)
VM = pltpu.VMEM


def dot(a, b):
    return lax.dot_general(a, b, (((1,), (0,)), ((), ())), preferred_element_type=F32)


def dot_bt(a, b):
    return lax.dot_general(a, b, (((1,), (1,)), ((), ())), preferred_element_type=F32)


def dot_at(a, b):
    return lax.dot_general(a, b, (((0,), (0,)), ((), ())), preferred_element_type=F32)


def rcopy(src, dst, ssem, rsem, seg):
    return pltpu.make_async_remote_copy(
        src_ref=src, dst_ref=dst, send_sem=ssem, recv_sem=rsem, device_id={"seg": seg}, device_id_type=MESH
    )


def zcopy(src, dst, ssem, rsem, z, seg):
    return pltpu.make_async_remote_copy(
        src_ref=src, dst_ref=dst, send_sem=ssem, recv_sem=rsem, device_id={"grp": z, "seg": seg}, device_id_type=MESH
    )


def take(ref, sem):
    pltpu.make_async_copy(ref, ref, sem).wait()


def send_to(me, target, src, dst, ssem, rsem):
    @pl.when(target != me)
    def _():
        rcopy(src, dst, ssem, rsem, target).start()

    @pl.when(target == me)
    def _():
        pltpu.make_async_copy(src, dst, rsem).start()


def loop(n, fn, first=0):
    def body(i, _):
        fn(i)
        return 0

    lax.fori_loop(first, n, body, 0)


def col(u, width=W):
    return pl.ds(pl.multiple_of(u * width, 128), width)


def norm(v):
    center = v - jnp.mean(v, axis=-1, keepdims=True)
    rstd = lax.rsqrt(jnp.mean(center * center, axis=-1, keepdims=True) + 1e-05)
    return center * rstd, rstd


def norm_back(grad, n, rstd, gain):
    dn = grad * gain
    return rstd * (dn - jnp.mean(dn, axis=-1, keepdims=True) - n * jnp.mean(dn * n, axis=-1, keepdims=True))


def gelu_both(u):
    e = jnp.exp(-0.5 * u * u)
    t = 1.0 / (1.0 + (0.3275911 * RSQ2) * jnp.abs(u))
    poly = t * (0.127414796 + t * (-0.142248368 + t * (0.7107068705 + t * (-0.7265760135 + t * 0.5307027145))))
    tail = poly * e
    cdf = jnp.where(u < 0.0, tail, 1.0 - tail)
    return u * cdf, cdf + u * (RS2PI * e)


def two_heads(v):
    lane = lax.broadcasted_iota(jnp.int32, v.shape, 1)
    none = jnp.zeros_like(v)
    return jnp.concatenate([jnp.where(lane < 64, v, none), jnp.where(lane >= 64, v, none)], axis=0)


def side_by_side(v):
    n = v.shape[0] // 2
    lane = lax.broadcasted_iota(jnp.int32, (n, 128), 1)
    return jnp.where(lane < 64, v[:n], v[n:])


def softmax(s):
    e = jnp.exp(s - jnp.max(s, axis=-1, keepdims=True))
    return e / jnp.sum(e, axis=-1, keepdims=True)


def softmax_back(w, dw):
    return w * (dw - jnp.sum(w * dw, axis=-1, keepdims=True))


def rows8(value):
    return value.reshape(value.shape[0] // 8, 8, value.shape[1])


def flat8(value):
    v = value.astype(F32)
    return v.reshape(v.shape[0] * v.shape[1], v.shape[2])


def sum0(v):
    return jnp.sum(v, axis=0, keepdims=True)


def owner_seg(k):
    return 2 * k


def pair_seg(p):
    return 4 * p + 1


def pair_first(p):
    return 5 * (p % 3) + 16 * (p // 3)


def fields(spec, refs):
    return types.SimpleNamespace(**dict(zip(spec, refs)))


CROSS = dict(
    pup=VM((32, 24, 128), BF16),
    xup=VM((32, 24, 128), BF16),
    xqkv=VM((32, 3, 24, 128), BF16),
    xout=VM((6, 24, D), BF16),
    wup=VM((D, 128), BF16),
    wqkv=VM((D, 384), BF16),
    wout=VM((128, D), BF16),
    wout_f=VM((144, D), F32),
    wdn=VM((128, D), BF16),
    msg=VM((8, D), BF16),
    x1=VM((32, 8, D), BF16),
    own=VM((8, 8, D), F32),
    rst=VM((8, 128), F32),
    xall=VM((96, D), BF16),
    q=VM((3, 96, 128), BF16),
    o=VM((96, 128), BF16),
    af=VM((192, 96), F32),
    p2=VM((12, 8, D), BF16),
    g2=VM((6, 8, D), BF16),
    p3=VM((8, D), BF16),
    g3=VM((12, 8, D), BF16),
    p4=VM((12, 8, D), BF16),
    g46=VM((64, 8, D), BF16),
    p5=VM((2, 8, D), BF16),
    g5=VM((12, 2, 8, D), BF16),
    p6=VM((12, 8, D), BF16),
    p7=VM((8, D), BF16),
    g7=VM((12, 8, D), BF16),
    p7f=VM((8, D), F32),
    g7f=VM((2, 8, D), F32),
    p8=VM((12, 8, D), BF16),
    g8=VM((6, 2, 8, D), BF16),
    gp=VM((96, 128), F32),
    gact=VM((96, 128), BF16),
    fall=VM((96, D), BF16),
    dd=VM((96, D), BF16),
    du=VM((96, 128), BF16),
    dq=VM((96, 384), BF16),
    de=VM((96, D), BF16),
    cs=DMA((12,)),
    cr=DMA((12,)),
    c7=DMA,
)


def slot_layout(doc, shape, slots):
    pos = (slots % 3) * 32 + slots // 3
    number = jnp.zeros(shape, jnp.int32)
    begin = jnp.zeros(shape, jnp.int32)
    end = jnp.int32(0)
    for d in range(6):
        begin = jnp.where(pos >= end, end, begin)
        number = jnp.where(pos >= end, d, number)
        end = end + doc[0, d]
    return number, pos - begin


class Cross:
    def __init__(self, r, a):
        self.r, self.a = r, a
        self.me = lax.axis_index("seg")
        self.is_owner = (self.me % 2 == 0) & (self.me < 24)
        self.k = self.me // 2
        self.is_pair = (self.me % 4 == 1) & (self.me < 24)
        self.p = self.me // 4

    def sem(self, e):
        return self.r.xcs.at[e], self.r.xcr.at[e]

    def seams(self):
        m = self.me % 16
        seam = (m == 5) | (m == 10)
        p0 = 3 * (self.me // 16) + jnp.where(m > 10, 2, jnp.where(m > 5, 1, 0))
        return seam, p0

    def reshard(self):
        r, a, me = self.r, self.a, self.me
        s0, r0 = self.sem(0)
        s1, r1 = self.sem(1)
        s2, r2 = self.sem(2)
        r.pup[...] = jnp.zeros((32, 24, 128), BF16)
        up = a.cup[...].astype(F32)
        for t in range(32):
            r.pup[t, :, 0:96] = up[:, 96 * t : 96 * t + 96].astype(BF16)
        loop(32, lambda t: send_to(me, t, r.pup.at[t], r.xup.at[me], s0, r0))

        def to_pair(p):
            for j in range(3):
                part = pl.ds(pl.multiple_of(D * j + 128 * p, 128), 128)
                send_to(me, pair_seg(p), a.cqkv.at[:, part], r.xqkv.at[me, j], s1, r1)
            first = pair_first(p)

            @pl.when((me >= first) & (me < first + 6))
            def _():
                send_to(me, pair_seg(p), a.cout, r.xout.at[me - first], s2, r2)

        loop(6, to_pair)
        r.wdn[0:96, :] = a.cdown[...]
        r.wdn[96:128, :] = jnp.zeros((32, D), BF16)

    def reshard_end(self):
        r = self.r
        take(r.xup, r.xcr.at[0])
        self.reshard_sent()
        r.wup[...] = r.xup[...].astype(F32).reshape(D, 128).astype(BF16)

        @pl.when(self.is_pair)
        def _():
            take(r.xqkv, r.xcr.at[1])
            for j in range(3):
                r.wqkv[:, 128 * j : 128 * (j + 1)] = r.xqkv[:, j].astype(F32).reshape(D, 128).astype(BF16)
            take(r.xout, r.xcr.at[2])
            r.wout_f[...] = r.xout[...].astype(F32).reshape(144, D)
            off = pl.multiple_of(8 * (self.p % 3), 8)
            r.wout[...] = r.wout_f[pl.ds(off, 128), :].astype(BF16)

    def reshard_sent(self):
        r, me = self.r, self.me
        take(r.xup.at[pl.ds(0, 31)], r.xcs.at[0])

        @pl.when(self.is_pair)
        def _():
            take(r.xqkv.at[pl.ds(0, 5)], r.xcs.at[1])

        @pl.when(jnp.logical_not(self.is_pair))
        def _():
            take(r.xqkv.at[pl.ds(0, 6)], r.xcs.at[1])

        seam, p0 = self.seams()
        hits = jnp.where(me == pair_seg(p0), 1, 0) + jnp.where(seam & (me == pair_seg(p0 + 1)), 1, 0)
        count = jnp.where(seam, 2, 1) - hits
        for n in (1, 2):

            @pl.when(count == n)
            def _():
                take(r.xout.at[pl.ds(0, n)], r.xcs.at[2])

    def start(self, z0, dy0):
        r, a, me = self.r, self.a, self.me
        row = lax.broadcasted_iota(jnp.int32, (8, 512), 0)
        lane = lax.broadcasted_iota(jnp.int32, (8, 512), 1)
        _, place = slot_layout(a.doc, (8, 512), jnp.minimum(me * 3 + row, 95))
        table = a.smg[...].astype(F32).reshape(512, W)[:, 256:384].astype(BF16)
        parts = []
        for i in range(6):
            hot = (lane == (place // 2) * 16 + (place % 2) * 6 + i) & (row < 3)
            parts.append(dot(hot.astype(BF16), table))
        cross_in = z0 + jnp.concatenate(parts, axis=1)
        rowd = lax.broadcasted_iota(jnp.int32, (8, D), 0)
        both = jnp.where(rowd < 3, cross_in, pltpu.roll(dy0, 3, 0))
        r.msg[...] = jnp.where(rowd < 6, both, 0.0).astype(BF16)
        ss, rs = self.sem(3)
        loop(6, lambda p: send_to(me, pair_seg(p), r.msg, r.x1.at[me], ss, rs))
        loop(12, lambda k: send_to(me, owner_seg(k), r.msg, r.x1.at[me], ss, rs))

    def pick(self, n, first, base):
        row = lax.broadcasted_iota(jnp.int32, (n, 256), 0) + first
        lane = lax.broadcasted_iota(jnp.int32, (n, 256), 1)
        return (lane == (row // 3) * 8 + row % 3 + base).astype(BF16)

    def attention(self):
        r, a, me = self.r, self.a, self.me
        ss, rs = self.sem(4)

        @pl.when(self.is_pair)
        def _():
            take(r.x1, r.xcr.at[3])
            msgs = flat8(r.x1[...]).astype(BF16)
            xall = dot(self.pick(96, 0, 0), msgs).astype(BF16)
            r.xall[...] = xall
            part = col(self.p, 128)
            joined = dot(xall, r.wqkv[...])
            q = (joined[:, 0:128] + a.cb[0:1, part]).astype(BF16)
            k = joined[:, 128:256].astype(BF16)
            v = (joined[:, 256:384] + a.cb[1:2, part]).astype(BF16)
            r.q[0], r.q[1], r.q[2] = q, k, v
            line = lax.broadcasted_iota(jnp.int32, (192, 96), 0)
            doc_r, _ = slot_layout(a.doc, (192, 96), jnp.where(line < 96, line, line - 96))
            doc_c, _ = slot_layout(a.doc, (192, 96), lax.broadcasted_iota(jnp.int32, (192, 96), 1))
            w = softmax(jnp.where(doc_r == doc_c, dot_bt(two_heads(q), k) * 0.125, -1e30))
            r.af[...] = w
            o = side_by_side(dot(w.astype(BF16), v)).astype(BF16)
            r.o[...] = o
            r.p2[...] = rows8(dot(o, r.wout[...])).astype(BF16)
            loop(12, lambda k: send_to(me, owner_seg(k), r.p2.at[k], r.g2.at[self.p], ss, rs))

    def first_norm(self):
        r, a, me = self.r, self.a, self.me
        ss, rs = self.sem(5)

        @pl.when(self.is_owner)
        def _():
            take(r.x1, r.xcr.at[3])
            msgs = flat8(r.x1[...]).astype(BF16)
            x = dot(self.pick(8, 8 * self.k, 0), msgs)
            r.own[1] = dot(self.pick(8, 8 * self.k, 3), msgs)
            take(r.g2, r.xcr.at[4])
            total = jnp.sum(r.g2[...].astype(F32), axis=0)
            n, rstd = norm(x + (total + a.cb[2:3, :]))
            r.own[2] = n
            r.xrst[...] = jnp.broadcast_to(rstd, (8, 128))
            r.p3[...] = (n * a.cb[6:7, :] + a.cb[3:4, :]).astype(BF16)
            loop(32, lambda t: send_to(me, t, r.p3, r.g3.at[self.k], ss, rs))

    def mlp(self):
        r, a, me = self.r, self.a, self.me
        ss, rs = self.sem(6)
        take(r.g3, r.xcr.at[5])
        f = flat8(r.g3[...]).astype(BF16)
        r.fall[...] = f
        g, gp = gelu_both(dot(f, r.wup[...]) + a.cub[0:1, :])
        r.gp[...] = gp
        g = g.astype(BF16)
        r.gact[...] = g
        r.p4[...] = rows8(dot(g, r.wdn[...])).astype(BF16)
        loop(12, lambda k: send_to(me, owner_seg(k), r.p4.at[k], r.g46.at[me], ss, rs))

    def second_norm(self):
        r, a, me = self.r, self.a, self.me
        ss, rs = self.sem(7)

        @pl.when(self.is_owner)
        def _():
            take(r.g46.at[pl.ds(0, 32)], r.xcr.at[6])
            total = jnp.sum(r.g46[0:32].astype(F32), axis=0)
            n, rstd = norm(r.p3[...].astype(F32) + (total + a.cb[4:5, :]))
            y = n * a.cb[7:8, :] + a.cb[5:6, :]
            dr2 = norm_back(r.own[1], n, rstd, a.cb[7:8, :])
            r.own[3] = n
            r.own[4] = dr2
            r.p5[0] = dr2.astype(BF16)
            r.p5[1] = y.astype(BF16)
            loop(32, lambda t: send_to(me, t, r.p5, r.g5.at[self.k], ss, rs))

    def mlp_back(self):
        r, me = self.r, self.me
        ss, rs = self.sem(8)
        take(r.g5, r.xcr.at[7])
        dd = flat8(r.g5[:, 0]).astype(BF16)
        r.xdd[...] = dd
        du = (dot_bt(dd, r.wdn[...]) * r.gp[...]).astype(BF16)
        r.du[...] = du
        r.p6[...] = rows8(dot_bt(du, r.wup[...])).astype(BF16)
        loop(12, lambda k: send_to(me, owner_seg(k), r.p6.at[k], r.g46.at[32 + me], ss, rs))

    def window(self, seg):
        return jnp.minimum((3 * seg) // 8, 10)

    def first_norm_back(self):
        r, a, me = self.r, self.a, self.me
        ss, rs = self.sem(9)
        fr = r.xcr.at[10]

        @pl.when(self.is_owner)
        def _():
            take(r.g46.at[pl.ds(32, 32)], r.xcr.at[8])
            df = jnp.sum(r.g46[32:64].astype(F32), axis=0) + r.own[4]
            r.own[5] = df
            dr1 = norm_back(df, r.own[2], r.xrst[:, 0:1], a.cb[6:7, :])
            r.p7[...] = dr1.astype(BF16)
            loop(6, lambda p: send_to(me, pair_seg(p), r.p7, r.g7.at[self.k], ss, rs))
            r.p7f[...] = dr1

            def one(t):
                w = self.window(t)

                @pl.when((w == self.k) | (w + 1 == self.k))
                def _():
                    send_to(me, t, r.p7f, r.g7f.at[self.k - w], r.c7, fr)

            loop(32, one)

    def attention_back(self):
        r, me = self.r, self.me
        ss, rs = self.sem(11)

        @pl.when(self.is_pair)
        def _():
            take(r.g7, r.xcr.at[9])
            de = flat8(r.g7[...]).astype(BF16)
            r.xde[...] = de
            do = dot_bt(de, r.wout[...]).astype(BF16)
            q, k, v = r.q[0], r.q[1], r.q[2]
            do2, w = two_heads(do), r.af[...]
            ds = softmax_back(w, dot_bt(do2, v)).astype(BF16)
            r.dq[:, 0:128] = (side_by_side(dot(ds, k)) * 0.125).astype(BF16)
            r.dq[:, 128:256] = (dot_at(ds, two_heads(q)) * 0.125).astype(BF16)
            r.dq[:, 256:384] = dot_at(w.astype(BF16), do2).astype(BF16)
            r.p8[...] = rows8(dot_bt(r.dq[...], r.wqkv[...])).astype(BF16)
            loop(32, lambda t: send_to(me, t, r.p8.at[pl.ds(self.window(t), 2)], r.g8.at[self.p], ss, rs))

    def finish(self):
        r = self.r
        take(r.g7f, r.xcr.at[10])
        take(r.g8, r.xcr.at[11])
        total = r.g7f[...] + jnp.sum(r.g8[...].astype(F32), axis=0)
        shift = 3 * self.me - 8 * self.window(self.me)
        return pltpu.roll(total.reshape(16, D), 16 - shift, 0)[0:8]

    def output_rows(self):
        w = self.window(self.me)
        y = self.r.g5[pl.ds(w, 2), 1].astype(F32).reshape(16, D)
        return pltpu.roll(y, 16 - (3 * self.me - 8 * w), 0)[0:8]

    def grads(self):
        r, a = self.r, self.a
        a.pu[...] = dot_at(r.fall[...], r.du[...]).reshape(32, 24, 128).astype(BF16)
        a.gdn[...] = dot_at(r.gact[...], r.xdd[...])[0:96].astype(BF16)

        @pl.when(self.is_pair)
        def _():
            for j in range(3):
                part = dot_at(r.xall[...], r.dq[:, 128 * j : 128 * (j + 1)])
                a.pq[:, j] = part.reshape(32, 24, 128).astype(BF16)
            r.po_f[...] = jnp.zeros((144, D), F32)
            off = pl.multiple_of(8 * (self.p % 3), 8)
            r.po_f[pl.ds(off, 128), :] = dot_at(r.o[...], r.xde[...])
            a.po[...] = r.po_f[...].reshape(6, 24, D).astype(BF16)

        a.small[...] = jnp.zeros((8, D), F32)

        @pl.when(self.is_owner)
        def _():
            dr1, df, dr2, dy = r.p7[...].astype(F32), r.own[5], r.own[4], r.own[1]
            dd = r.p5[0].astype(F32)
            for row, v in ((2, dr1), (3, df), (4, dd), (5, dy), (6, df * r.own[2]), (7, dy * r.own[3])):
                a.small[row : row + 1, :] = sum0(v)

        @pl.when(self.is_pair)
        def _():
            part = col(self.p, 128)
            a.small[0:1, part] = sum0(r.dq[:, 0:128].astype(F32))
            a.small[1:2, part] = sum0(r.dq[:, 256:384].astype(F32))

        a.dc[...] = jnp.broadcast_to(sum0(r.du[...].astype(F32)), (8, 128))

    def drain(self):
        r, me = self.r, self.me
        cs = r.xcs

        def some(e, ref, count, fewer):
            @pl.when(fewer)
            def _():
                take(ref.at[pl.ds(0, count - 1)], cs.at[e])

            @pl.when(jnp.logical_not(fewer))
            def _():
                take(ref.at[pl.ds(0, count)], cs.at[e])

        some(3, r.g46, 18, self.is_pair | self.is_owner)
        some(6, r.g46, 12, self.is_owner)
        some(8, r.g46, 12, self.is_owner)

        @pl.when(self.is_pair)
        def _():
            take(r.g46.at[pl.ds(0, 12)], cs.at[4])
            take(r.g46.at[pl.ds(0, 62)], cs.at[11])

        @pl.when(self.is_owner)
        def _():
            take(r.g46.at[pl.ds(0, 31)], cs.at[5])
            take(r.g46.at[pl.ds(0, 62)], cs.at[7])
            take(r.g46.at[pl.ds(0, 6)], cs.at[9])

            count = jnp.int32(0)
            for t in range(32):
                w = min(3 * t // 8, 10)
                count += jnp.where(((self.k == w) | (self.k == w + 1)) & (me != t), 1, 0)
            for n in range(1, 10):

                @pl.when(count == n)
                def _():
                    take(r.g46.at[pl.ds(0, 2 * n)], r.c7)


class CrossGrads(Cross):
    def scatter(self):
        r, a, me = self.r, self.a, self.me
        loop(32, lambda t: send_to(me, t, a.pu.at[t], r.gup.at[me], r.ks.at[0], r.kr.at[0]))

        @pl.when(self.is_pair)
        def _():
            loop(32, lambda t: send_to(me, t, a.pq.at[t], r.gqkv.at[self.p], r.ks.at[1], r.kr.at[1]))
            loop(
                6,
                lambda i: send_to(
                    me, pair_first(self.p) + i, a.po.at[i], r.go.at[self.p % 2], r.ks.at[2], r.kr.at[2]
                ),
            )

    def planes(self, red):
        r, a, me, z = self.r, self.a, self.me, red.z
        take(r.gup, r.kr.at[0])
        take(r.gqkv, r.kr.at[1])
        for i in range(6):
            for j in range(3):
                r.c0[i, :, 128 * j : 128 * (j + 1)] = r.gqkv[i, j]
        seam, p0 = self.seams()

        @pl.when(seam)
        def _():
            take(r.go, r.kr.at[2])
            both = (r.go[0].astype(F32) + r.go[1].astype(F32)).astype(BF16)
            for i in range(2):
                r.c0[6 + i] = both[:, W * i : W * (i + 1)]

        @pl.when(jnp.logical_not(seam))
        def _():
            take(r.go.at[0], r.kr.at[2])
            for i in range(2):
                r.c0[6 + i] = r.go[p0 % 2, :, W * i : W * (i + 1)]

        gdn = a.gdn[...].astype(F32).reshape(4, 24, D)
        for i in range(2):
            for n in range(4):
                r.c0[8 + 4 * i + n] = gdn[n, :, W * i : W * (i + 1)].astype(BF16)

        def out(zz):
            zcopy(r.c0.at[pl.ds(2 * zz, 2)], r.cr.at[z], r.xs.at[1], r.xr.at[1], zz, me).start()
            zcopy(r.gup.at[pl.ds(4 * zz, 4)], r.ur.at[z], r.xs.at[2], r.xr.at[2], zz, me).start()

        red.peers(out)
        pltpu.make_async_copy(r.c0.at[pl.ds(2 * z, 2)], r.cr.at[z], r.xr.at[1]).start()
        pltpu.make_async_copy(r.gup.at[pl.ds(4 * z, 4)], r.ur.at[z], r.xr.at[2]).start()

    def planes_sum(self, red):
        r, me, z = self.r, self.me, red.z
        take(r.cr, r.xr.at[1])
        r.cs[...] = jnp.sum(r.cr[...].astype(F32), axis=0).astype(BF16)
        take(r.ur, r.xr.at[2])
        r.us[...] = jnp.sum(r.ur[...].astype(F32), axis=0).astype(BF16)

        def back(zz):
            zcopy(r.cs, r.cf.at[z], r.xs.at[4], r.xr.at[4], zz, me).start()
            zcopy(r.us, r.uf.at[z], r.xs.at[5], r.xr.at[5], zz, me).start()

        red.peers(back)
        pltpu.make_async_copy(r.cs, r.cf.at[z], r.xr.at[4]).start()
        pltpu.make_async_copy(r.us, r.uf.at[z], r.xr.at[5]).start()

    def end(self):
        r, me = self.r, self.me
        take(r.cf, r.xr.at[4])
        take(r.uf, r.xr.at[5])
        take(r.gup.at[pl.ds(0, 31)], r.ks.at[0])

        @pl.when(self.is_pair)
        def _():
            take(r.pq.at[pl.ds(0, 31)], r.ks.at[1])
            first = pair_first(self.p)
            inside = (me >= first) & (me < first + 6)

            @pl.when(inside)
            def _():
                take(r.po.at[pl.ds(0, 5)], r.ks.at[2])

            @pl.when(jnp.logical_not(inside))
            def _():
                take(r.po, r.ks.at[2])

        for n, buf in ((1, r.cr), (2, r.ur), (4, r.cr), (5, r.ur)):
            take(buf.at[pl.ds(0, 7)], r.xs.at[n])


class Plane:
    def __init__(self):
        self.me = lax.axis_index("seg")
        self.x, self.y, self.c = self.me // 8, (self.me // 2) % 4, self.me % 2
        self.other = self.me + 1 - 2 * self.c

    def seg(self, on_x, step):
        if on_x:
            return (((self.x + step) % 4) * 4 + self.y) * 2 + self.c
        return (self.x * 4 + (self.y + step) % 4) * 2 + self.c

    def ring(self, part, which, step):
        return self.seg((part == 0) == (which == 1), step)

    def pos(self, part, which):
        return self.x if (part == 0) == (which == 1) else self.y

    def by_part(self, k, fn):
        for part in range(2):
            pl.when(k % 2 == part)(functools.partial(fn, part))

    @staticmethod
    def ahead(k):
        return 1 + 2 * ((k // 2) % 2)


class Gather(Plane):
    def __init__(self, r):
        super().__init__()
        self.r = r

    def v1(self, k, part, off):
        mine = self.r.ws.at[self.c, k]
        return mine.at[(self.x + off) % 4, self.y] if part == 0 else mine.at[self.x, (self.y + off) % 4]

    def v2(self, k, part, off):
        mine = self.r.ws.at[self.c, k]
        return mine.at[:, (self.y + off) % 4] if part == 0 else mine.at[(self.x + off) % 4]

    def first(self, k):
        r = self.r

        def go(part):
            own = self.v1(k, part, 0)
            src = r.stage.at[k]
            pltpu.make_async_copy(src, own, r.own_sem.at[k]).start()
            rcopy(src, own, r.s1, r.r1.at[k, 0], self.ring(part, 1, 1)).start()
            rcopy(src, own, r.s1, r.r1.at[k, 1], self.ring(part, 1, 3)).start()

        self.by_part(k, go)

    def first_on(self, k):
        r, ahead = self.r, self.ahead(k)

        def go(part):
            block = self.v1(k, part, 4 - ahead)
            take(block, r.r1.at[k, ahead // 2])
            rcopy(block, block, r.s1, r.r1.at[k, 1 - ahead // 2], self.ring(part, 1, ahead)).start()

        self.by_part(k, go)

    def second(self, k):
        r, ahead = self.r, self.ahead(k)

        def go(part):
            take(r.ws.at[0, 0, 0, pl.ds(0, 2)], r.r1.at[k, 1 - ahead // 2])
            own = self.v1(k, part, 0)
            take(own, r.own_sem.at[k])
            row = self.v2(k, part, 0)
            rcopy(row, row, r.s2, r.r2.at[k, 0], self.ring(part, 2, 1)).start()
            rcopy(row, row, r.s2, r.r2.at[k, 1], self.ring(part, 2, 3)).start()
            rcopy(row, row, r.s3, r.r3.at[k], self.other).start()

        self.by_part(k, go)

    def second_on(self, k):
        r, ahead = self.r, self.ahead(k)

        def go(part):
            row = self.v2(k, part, 4 - ahead)
            take(row, r.r2.at[k, ahead // 2])
            rcopy(row, row, r.s2, r.r2.at[k, 2], self.ring(part, 2, ahead)).start()
            rcopy(row, row, r.s3, r.r3.at[k], self.other).start()
            row = self.v2(k, part, ahead)
            take(row, r.r2.at[k, 1 - ahead // 2])
            rcopy(row, row, r.s3, r.r3.at[k], self.other).start()

        self.by_part(k, go)

    def last(self, k):
        r = self.r

        def go(part):
            row = self.v2(k, part, 2)
            take(row, r.r2.at[k, 2])
            rcopy(row, row, r.s3, r.r3.at[k], self.other).start()

        self.by_part(k, go)

    def arrived(self, k):
        r = self.r
        take(r.ws.at[1 - self.c, k], r.r3.at[k])

    def drain(self):
        r = self.r

        take(r.ws.at[0, pl.ds(0, 9), 0], r.s1)
        take(r.ws.at[0, pl.ds(0, 9)], r.s2)
        take(r.ws.at[0], r.s3)


class Reduce(Plane):
    def __init__(self, r, pieces):
        super().__init__()
        self.r, self.pieces = r, pieces
        self.z = lax.axis_index("grp")

    def peers(self, fn):
        loop(7, lambda i: fn((self.z + 1 + i) % 8))

    def to_sibling(self, k):
        r = self.r
        rcopy(r.gb.at[1, k], r.r0.at[k], r.ms.at[0], r.mr.at[k, 0], self.other).start()

    def msg(self, k, part, q):
        return self.r.gb.at[0, k, :, q] if part == 0 else self.r.gb.at[0, k, q]

    def step_a(self, k):
        r, ahead = self.r, self.ahead(k)
        take(r.r0.at[k], r.mr.at[k, 0])

        def add(i):
            px, py = i // 4, i % 4
            r.gb[0, k, px, py] = (r.gb[0, k, px, py].astype(F32) + r.r0[k, px, py].astype(F32)).astype(BF16)

        loop(16, add)

        def go(part):
            q = self.pos(part, 2)
            far, back = self.msg(k, part, (q + 2) % 4), self.msg(k, part, (q + 4 - ahead) % 4)
            rcopy(far, r.f2.at[k], r.ms.at[1], r.mr.at[k, 1], self.ring(part, 2, ahead)).start()
            rcopy(back, r.b2.at[k], r.ms.at[1], r.mr.at[k, 2], self.ring(part, 2, 4 - ahead)).start()

        self.by_part(k, go)

    def step_b(self, k):
        r, ahead = self.r, self.ahead(k)
        take(r.f2.at[k], r.mr.at[k, 1])

        def go(part):
            block = self.msg(k, part, (self.pos(part, 2) + ahead) % 4)

            def add(i):
                block[i] = (block[i].astype(F32) + r.f2[k, i].astype(F32)).astype(BF16)

            loop(4, add)
            rcopy(block, r.a2.at[k], r.ms.at[1], r.mr.at[k, 2], self.ring(part, 2, ahead)).start()

        self.by_part(k, go)

    def step_c(self, k):
        r, ahead = self.r, self.ahead(k)
        take(r.r0.at[0, pl.ds(0, 2)], r.mr.at[k, 2])

        def go(part):
            block = self.msg(k, part, self.pos(part, 2))

            def add(i):
                r.t1[k, i] = (block[i].astype(F32) + r.a2[k, i].astype(F32) + r.b2[k, i].astype(F32)).astype(BF16)

            loop(4, add)
            q = self.pos(part, 1)
            far, back = r.t1.at[k, (q + 2) % 4], r.t1.at[k, (q + 4 - ahead) % 4]
            rcopy(far, r.f1.at[k], r.ms.at[2], r.mr.at[k, 3], self.ring(part, 1, ahead)).start()
            rcopy(back, r.b1.at[k], r.ms.at[2], r.mr.at[k, 4], self.ring(part, 1, 4 - ahead)).start()

        self.by_part(k, go)

    def step_d(self, k):
        r, ahead = self.r, self.ahead(k)
        take(r.f1.at[k], r.mr.at[k, 3])

        def go(part):
            n = (self.pos(part, 1) + ahead) % 4
            r.t1[k, n] = (r.t1[k, n].astype(F32) + r.f1[k].astype(F32)).astype(BF16)
            rcopy(r.t1.at[k, n], r.a1.at[k], r.ms.at[2], r.mr.at[k, 4], self.ring(part, 1, ahead)).start()

        self.by_part(k, go)

    def step_e(self, k):
        r = self.r
        take(r.r0.at[0, 0, pl.ds(0, 2)], r.mr.at[k, 4])

        def go(part):
            t = r.t1[k, self.pos(part, 1)].astype(F32) + r.a1[k].astype(F32) + r.b1[k].astype(F32)
            self.pieces[k // 4, pl.ds(2 * (k % 4), 2)] = t.reshape(2, 24, W).astype(BF16)

        self.by_part(k, go)

    def tick(self, t, slots):
        for lag, step in ((0, self.step_a), (3, self.step_b), (6, self.step_c), (8, self.step_d), (10, self.step_e)):

            @pl.when((t >= lag) & (t < lag + slots))
            def _():
                step(t - lag)

    def sent(self, slots):
        r = self.r
        some = pl.ds(0, slots * 3 // 4)
        take(r.r0, r.ms.at[0])
        take(r.r0.at[some], r.ms.at[1])
        take(r.r0.at[some, 0], r.ms.at[2])

    def z_send(self, g):
        r, z, me = self.r, self.z, self.me
        self.peers(lambda zz: zcopy(r.zp.at[g, zz], r.zr.at[g, z], r.zss.at[g, 0], r.zsr.at[g, 0], zz, me).start())
        pltpu.make_async_copy(r.zp.at[g, z], r.zr.at[g, z], r.zsr.at[g, 0]).start()

    def z_sum(self, g):
        r, z, me, c = self.r, self.z, self.me, self.c
        take(r.zr.at[g], r.zsr.at[g, 0])
        r.zs[g] = jnp.sum(r.zr[g].astype(F32), axis=0).astype(BF16)
        m, h = z // 2, z % 2

        def out(dst, sem, seg):
            def one(zz):
                here = (zz == z) & (seg == me)

                @pl.when(here)
                def _():
                    pltpu.make_async_copy(r.zs.at[g], dst, sem).start()

                @pl.when(jnp.logical_not(here))
                def _():
                    zcopy(r.zs.at[g], dst, r.zss.at[g, 1], sem, zz, seg).start()

            loop(8, one)

        if g == 0:
            out(r.fd.at[z], r.zsr.at[0, 1], me)
        elif g == 1:
            out(r.fa.at[8 + 2 * m + c], r.zsr.at[1, 1], me - c + h)
        else:
            out(r.fa.at[2 * ((m + 3) % 4) + c], r.zsr.at[2, 1], me - c + h)

    def z_sent(self):
        r, z, c = self.r, self.z, self.c
        for g in range(3):
            take(r.zr.at[g, pl.ds(0, 7)], r.zss.at[g, 0])
            stays = (z % 2 == c) if g > 0 else (z >= 0)

            @pl.when(stays)
            def _():
                take(r.zr.at[g, pl.ds(0, 7)], r.zss.at[g, 1])

            @pl.when(jnp.logical_not(stays))
            def _():
                take(r.zr.at[g], r.zss.at[g, 1])


F_IN = list(dict(tok=0, cot=0, qkv=0, out=0, up=0, down=0, bias=0, upbias=0, gains=0, cqkv=0, cout=0, cup=0, cdown=0, cbias=0, cupbias=0, cgains=0, pos=0, doc=0))
F_OUT = dict(
    lo_h=((ROWS, D), BF16),
    tg_h=((ROWS, D), F32),
    fa=((16, 24, W), BF16),
    fd=((8, 24, W), BF16),
    cf=((8, 2, 24, W), BF16),
    uf=((8, 4, 24, 128), BF16),
    osm=((12, 8, D), BF16),
)


def reduce_scratch(n):
    unit, line = (4, 4, 48, W), (n, 4, 48, W)
    return dict(
        gb=VM((2, n) + unit, BF16),
        r0=VM((n,) + unit, BF16),
        f2=VM(line, BF16),
        a2=VM(line, BF16),
        b2=VM(line, BF16),
        t1=VM(line, BF16),
        f1=VM((n, 48, W), BF16),
        a1=VM((n, 48, W), BF16),
        b1=VM((n, 48, W), BF16),
        mr=DMA((n, 5)),
        ms=DMA((3,)),
    )


F_SCR = dict(
    ws=VM((2, 12, 4, 4, 48, W), BF16),
    stage=VM((12, 48, W), BF16),
    sibq=VM((24, 3 * D), BF16),
    sibo=VM((24, D), BF16),
    sibu=VM((24, FF), BF16),
    smf=VM((16, W), F32),
    sm=VM((16, W), BF16),
    smg=VM((32, 16, W), BF16),
    both=VM((16, D), F32),
    lb=VM((8, D), F32),
    lub=VM((1, FF), F32),
    cub=VM((8, 128), F32),
    cb=VM((8, D), F32),
    qkvv=VM((3, ROWS, D), BF16),
    mix=VM((ROWS, D), BF16),
    aw=VM((3, 6, 256, 128), BF16),
    n1=VM((ROWS, D), F32),
    f=VM((ROWS, D), BF16),
    g=VM((ROWS, FF), BF16),
    gpl=VM((ROWS, FF), BF16),
    rst=VM((ROWS, 128), F32),
    dd=VM((ROWS, D), BF16),
    hf=VM((8, D), BF16),
    hg=VM((8, FF), BF16),
    hgp=VM((8, FF), F32),
    hn=VM((2, 8, D), F32),
    hrst=VM((2, 8, 128), F32),
    hgs=VM((32, 8, 128), BF16),
    hfp=VM((8, W), BF16),
    hdp=VM((8, W), BF16),
    hdd=VM((8, D), BF16),
    hdf=VM((8, D), F32),
    hs=DMA((3,)),
    hr=DMA((3,)),
    sib_s=DMA((3,)),
    sib_r=DMA((3,)),
    sm_s=DMA,
    sm_r=DMA,
    own_sem=DMA((12,)),
    s1=DMA,
    r1=DMA((12, 2)),
    s2=DMA,
    r2=DMA((12, 3)),
    s3=DMA,
    r3=DMA((12,)),
    lo=VM((ROWS, D), BF16),
    tg=VM((ROWS, D), F32),
    done=DMA((2,)),
    sloc=VM((8, D), F32),
    dcl=VM((1, FF), F32),
    dx=VM((8, D), F32),
    hfa=VM((32, 8, W), BF16),
    hda=VM((32, 8, W), BF16),
    hgr=VM((32, 8, 128), BF16),
    gdn=VM((96, D), BF16),
    small=VM((8, D), F32),
    dc=VM((8, 128), F32),
    gup=VM((32, 24, 128), BF16),
    gqkv=VM((6, 3, 24, 128), BF16),
    go=VM((2, 24, D), BF16),
    cu=VM((2, 16, 24, 128), BF16),
    zc=VM((24, W), F32),
    zp=VM((3, 8, 24, W), BF16),
    zr=VM((3, 8, 24, W), BF16),
    zs=VM((3, 24, W), BF16),
    c0=VM((16, 24, W), BF16),
    cr=VM((8, 2, 24, W), BF16),
    cs=VM((2, 24, W), BF16),
    ur=VM((8, 4, 24, 128), BF16),
    us=VM((4, 24, 128), BF16),
    sf=VM((96, D), F32),
    s0=VM((12, 8, D), BF16),
    sm1=VM((8, D), BF16),
    sm2=VM((8, D), BF16),
    xr=DMA((8,)),
    xs=DMA((8,)),
    zsr=DMA((3, 2)),
    zss=DMA((3, 2)),
    ks=DMA((4,)),
    kr=DMA((4,)),
    free=pltpu.SemaphoreType.REGULAR,
    mr2=DMA((4, 5)),
    ms2=DMA((3,)),
    **reduce_scratch(8),
    **{("x" + n if n in ("rst", "dd", "de", "cs", "cr") else n): v for n, v in CROSS.items()},
)


def layer_kernel(*refs):
    r = fields(F_IN + list(F_OUT) + list(F_SCR), refs)
    ring = Gather(r)
    cross = CrossGrads(r, r)
    again = types.SimpleNamespace(
        gb=r.ws.at[:, pl.ds(4, 4)],
        r0=r.ws.at[0, pl.ds(8, 4)],
        f2=r.ws.at[1, 8],
        a2=r.ws.at[1, 9],
        b2=r.ws.at[1, 10],
        t1=r.ws.at[1, 11],
        f1=r.stage.at[pl.ds(0, 4)],
        a1=r.stage.at[pl.ds(4, 4)],
        b1=r.stage.at[pl.ds(8, 4)],
        mr=r.mr2,
        ms=r.ms2,
    )
    red, red2 = Reduce(r, r.zp.at[pl.ds(0, 2)]), Reduce(again, r.zp.at[pl.ds(2, 1)])
    me, c, z = ring.me, ring.c, red.z
    is_owner = (c == 0) & (me < 24)
    r.n2, r.de, r.do = r.tg, r.f, r.dd
    r.pcu, r.po_f, r.pu, r.pq, r.po = r.xup, r.wout_f, r.pup, r.xqkv, r.xout
    r.sz, r.sg = r.g46.at[pl.ds(0, 32)], r.g46.at[pl.ds(32, 32)]
    bar = pltpu.get_barrier_semaphore()
    loop(31, lambda i: pl.semaphore_signal(bar, inc=1, device_id={"seg": (me + 1 + i) % 32}, device_id_type=MESH))

    def greet(zz):
        for seg in (me, red.other):
            pl.semaphore_signal(bar, inc=1, device_id={"grp": zz, "seg": seg}, device_id_type=MESH)

    red.peers(greet)
    r.smf[...] = jnp.zeros((16, W), F32)
    r.smf[0:6, 0:24] = r.bias[...].astype(F32)
    r.smf[6:8, 0:24] = r.gains[...].astype(F32)
    r.smf[8:14, 0:24] = r.cbias[...].astype(F32)
    r.smf[14:16, 0:24] = r.cgains[...].astype(F32)
    r.smf[0:1, 128:224] = r.upbias[...].astype(F32)
    table = r.pos[...].astype(F32)
    for t in range(2):
        for i in range(6):
            r.smf[6 * t + i : 6 * t + i + 1, 256:384] = table[t : t + 1, 128 * i : 128 * (i + 1)]
    r.sm[...] = r.smf[...].astype(BF16)
    r.cub[...] = jnp.zeros((8, 128), F32)
    r.cub[0:1, 0:96] = r.cupbias[...].astype(F32)
    pl.semaphore_wait(bar, 45)

    swaps = [(r.qkv, r.sibq), (r.out, r.sibo), (r.up, r.sibu)]
    for i, (src, dst) in enumerate(swaps):
        rcopy(src, dst, r.sib_s.at[i], r.sib_r.at[i], ring.other).start()
    for j in range(4):
        r.stage[8 + j] = r.down[(j % 2) * 48 : (j % 2) * 48 + 48, (j // 2) * W : (j // 2 + 1) * W]

    def compose(k, src, sib, block):
        own = src[:, col(block)].astype(F32)
        oth = sib[:, col(block)].astype(F32)
        lo, hi = jnp.where(c == 0, own, oth), jnp.where(c == 0, oth, own)
        r.stage[k] = jnp.concatenate([lo, hi], axis=0).astype(BF16)
        ring.first(k)

    def arrive(i):
        take(swaps[i][1], r.sib_r.at[i])

    arrive(0)
    loop(3, lambda k: compose(k, r.qkv, r.sibq, 2 * k + c))
    arrive(1)
    compose(3, r.out, r.sibo, c)
    arrive(2)
    loop(8, lambda k: compose(k, r.up, r.sibu, 2 * (k - 4) + c), 4)
    loop(12, ring.first, 8)
    loop(32, lambda t: send_to(me, t, r.sm, r.smg.at[me], r.sm_s, r.sm_r))
    loop(12, ring.first_on)
    loop(6, ring.second)
    cross.reshard()

    take(r.smg, r.sm_r)
    for t in range(32):
        block = r.smg[t].astype(F32)
        r.both[:, 24 * t : 24 * t + 24] = block[:, 0:24]
        r.lub[:, 96 * t : 96 * t + 96] = block[0:1, 128:224]
    r.lb[...] = r.both[0:8, :]
    r.cb[...] = r.both[8:16, :]

    def tick(k):
        ring.second_on(k)

        @pl.when(k < 6)
        def _():
            ring.second(k + 6)

        @pl.when(k >= 3)
        def _():
            ring.last(k - 3)

    def weight(cc, k):
        return r.ws[cc, k].reshape(D, W)

    loop(5, tick)

    def project(k):
        tick(k)
        i = k - 5
        ring.arrived(i)
        shift = jnp.where(i == 0, r.lb[0:1, :], jnp.where(i == 2, r.lb[1:2, :], 0.0))
        for cc in range(2):
            part = slice(cc * W, (cc + 1) * W)
            r.qkvv[i, :, part] = (dot(r.tok[...], weight(cc, i)) + shift[:, part]).astype(BF16)

    loop(8, project, 5)

    def attend(k):
        tick(k)
        s = k - 8
        rows = pl.ds(pl.multiple_of(s * 128, 128), 128)
        for p in range(6):
            part = slice(128 * p, 128 * (p + 1))
            w = softmax(dot_bt(two_heads(r.qkvv[0, rows, part]), r.qkvv[1, rows, part]) * 0.125).astype(BF16)
            r.aw[s, p] = w
            r.mix[rows, part] = side_by_side(dot(w, r.qkvv[2, rows, part])).astype(BF16)

    loop(11, attend, 8)
    tick(11)
    ring.arrived(3)
    for cc in range(2):
        part = slice(cc * W, (cc + 1) * W)
        r.n1[:, part] = dot(r.mix[...], weight(cc, 3)) + (r.tok[:, part].astype(F32) + r.lb[2:3, part])
    ring.last(9)

    row8 = lax.broadcasted_iota(jnp.int32, (8, D), 0)
    r.sloc[...] = jnp.zeros((8, D), F32)

    def heads(ref):
        out = jnp.zeros((8, D), F32)
        for s in range(3):
            top = ref[128 * s : 128 * s + 16, :].astype(F32)[0:1, :]
            out = jnp.where(row8 == s, top, out)
        return out

    def head_norm(i, value):
        n, rstd = norm(value)
        r.hn[i] = n
        r.hrst[i] = jnp.broadcast_to(rstd, (8, 128))
        return n

    hf = head_norm(0, heads(r.n1)) * r.lb[6:7, :] + r.lb[3:4, :]
    r.hf[...] = jnp.where(row8 < 3, hf, 0.0).astype(BF16)

    def head_up(i):
        ring.arrived(i)
        for cc in range(2):
            part = col(2 * (i - 4) + cc)
            g, gp = gelu_both(dot(r.hf[...], weight(cc, i)) + r.lub[0:1, part])
            keep = lax.broadcasted_iota(jnp.int32, (8, W), 0) < 3
            r.hg[:, part] = jnp.where(keep, g, 0.0).astype(BF16)
            r.hgp[:, part] = gp

        @pl.when(i < 6)
        def _():
            ring.last(i + 6)

    loop(8, head_up, 4)

    def down_rows(x, kc):
        pieces = [r.ws[cc, 8 + 2 * kc + j, x, y] for y in range(4) for cc in range(2) for j in range(2)]
        return jnp.concatenate(pieces, axis=0)

    halves = []
    for kc in range(2):
        for j in range(2):
            ring.arrived(8 + 2 * kc + j)
        part = slice(kc * W, (kc + 1) * W)
        acc = r.hf[:, part].astype(F32) + r.lb[4:5, part]
        for x in range(4):
            acc += dot(r.hg[:, D * x : D * (x + 1)], down_rows(x, kc))
        halves.append(acc)
    z0 = head_norm(1, jnp.concatenate(halves, axis=1)) * r.lb[7:8, :] + r.lb[5:6, :]
    cross.reshard_end()
    cross.start(z0, heads(r.cot))

    def blocks(fn):
        loop(ROWS // 64, lambda i: fn(pl.ds(pl.multiple_of(i * 64, 64), 64)))

    def norm_one(rows):
        n, rstd = norm(r.n1[rows, :])
        r.n1[rows, :] = n
        r.rst[rows, :] = jnp.broadcast_to(rstd, (64, 128))
        r.f[rows, :] = (n * r.lb[6:7, :] + r.lb[3:4, :]).astype(BF16)

    def raise_up(i):
        def half(cc):
            part = col(2 * (i - 4) + cc)
            g, gp = gelu_both(dot(r.f[...], weight(cc, i)) + r.lub[0:1, part])
            r.g[:, part] = g.astype(BF16)
            r.gpl[:, part] = gp.astype(BF16)

        loop(2, half)

    def lower(kc):
        part = slice(kc * W, (kc + 1) * W)
        r.n2[:, part] = r.f[:, part].astype(F32) + r.lb[4:5, part]

        def quarter(x):
            r.n2[:, part] += dot(r.g[:, col(x, D)], down_rows(x, kc))

        loop(4, quarter)

    row64 = lax.broadcasted_iota(jnp.int32, (64, D), 0)

    def norm_two(i):
        rows = pl.ds(pl.multiple_of(i * 64, 64), 64)
        n, rstd = norm(r.n2[rows, :])
        r.lo[rows, :] = (n * r.lb[7:8, :] + r.lb[5:6, :]).astype(BF16)
        dy = jnp.where((row64 == 0) & (i % 2 == 0), 0.0, r.cot[rows, :].astype(F32))
        dr2 = norm_back(dy, n, rstd, r.lb[7:8, :])
        dd = dr2.astype(BF16)
        r.n2[rows, :] = dr2
        r.dd[rows, :] = dd
        r.sloc[5:6, :] += sum0(dy)
        r.sloc[7:8, :] += sum0(dy * n)
        r.sloc[4:5, :] += sum0(dd.astype(F32))

    def down_grad(b):
        v = dot_at(r.g[:, col(b)], r.dd[...]).astype(BF16).reshape(2, 2, 2, 48, D)
        for chip in range(2):
            for cc in range(2):
                for j in range(4):
                    v4 = v[chip, cc, j % 2, :, (j // 2) * W : (j // 2 + 1) * W]
                    r.gb[(cc + c) % 2, j, b // 2, 2 * (b % 2) + chip] = v4

    def down_block(b, kc):
        chips = [(b // 2, 2 * (b % 2) + chip) for chip in range(2)]
        pieces = [r.ws[cc, 8 + 2 * kc + j, x, y] for x, y in chips for cc in range(2) for j in range(2)]
        return jnp.concatenate(pieces, axis=0)

    def middle(b):
        part = col(b)
        dg = dot_bt(r.dd[:, 0:W], down_block(b, 0)) + dot_bt(r.dd[:, W:D], down_block(b, 1))
        du = (dg * r.gpl[:, part].astype(F32)).astype(BF16)
        r.dcl[:, part] = sum0(du.astype(F32))
        r.n2[...] += dot_bt(du, r.ws[b % 2, 4 + b // 2].reshape(D, W))
        r.gb[(b + c) % 2, 4 + b // 2] = dot_at(r.f[...], du).astype(BF16).reshape(4, 4, 48, W)

        @pl.when(b % 2 == 1)
        def _():
            red.to_sibling(4 + b // 2)

    def norm_one_back(rows):
        df, n = r.n2[rows, :], r.n1[rows, :]
        dr1 = norm_back(df, n, r.rst[rows, 0:1], r.lb[6:7, :])
        de = dr1.astype(BF16)
        r.n2[rows, :] = dr1
        r.de[rows, :] = de
        r.sloc[3:4, :] += sum0(df)
        r.sloc[6:7, :] += sum0(df * n)
        r.sloc[2:3, :] += sum0(de.astype(F32))

    def out_back(de):
        return dot_bt(de[:, 0:W], weight(0, 3)) + dot_bt(de[:, W:D], weight(1, 3))

    def tick(t):
        red.tick(t, 8)

    blocks(norm_one)
    raise_up(4)
    cross.attention()
    loop(8, raise_up, 5)
    cross.first_norm()
    def pack(value):
        n = value.shape[1] // 2
        row = lax.broadcasted_iota(jnp.int32, (8, n), 0)
        both = jnp.where(row < 3, value[:, :n], pltpu.roll(value[:, n:], 3, 0))
        return jnp.where(row < 6, both, 0.0)

    r.hgs[...] = jnp.zeros((32, 8, 128), BF16)
    hidden, slope = r.hg[...].astype(F32), r.hgp[...]
    for t in range(32):
        part = slice(96 * t, 96 * t + 96)
        both = jnp.concatenate([hidden[:, part], slope[:, part]], axis=1)
        r.hgs[t, :, 0:96] = pack(both).astype(BF16)
    r.hfp[...] = pack(r.hf[...].astype(F32)).astype(BF16)
    loop(32, lambda t: send_to(me, t, r.hgs.at[t], r.hgr.at[me], r.hs.at[0], r.hr.at[0]))
    loop(32, lambda t: send_to(me, t, r.hfp, r.hfa.at[me], r.hs.at[1], r.hr.at[1]))
    lower(0)
    lower(1)
    cross.mlp()
    loop(6, norm_two)
    loop(4, down_grad)
    cross.second_norm()
    loop(8, down_grad, 4)
    loop(4, red.to_sibling)
    middle(0)
    tick(0)
    cross.mlp_back()
    middle(1)
    tick(1)
    middle(2)
    tick(2)
    middle(3)
    tick(3)
    cross.first_norm_back()
    middle(4)
    tick(4)
    middle(5)
    middle(6)
    tick(5)
    middle(7)
    cross.attention_back()
    tick(6)
    blocks(norm_one_back)
    r.do[...] = out_back(r.de[...]).astype(BF16)
    tick(7)
    cross.grads()
    cross.scatter()
    tick(8)
    r.dx[...] = jnp.where(row8 < 3, cross.finish(), 0.0)

    dy0, hn2 = r.dx[...], r.hn[1]
    dr2 = norm_back(dy0, hn2, r.hrst[1, :, 0:1], r.lb[7:8, :])
    r.hdd[...] = dr2.astype(BF16)
    r.hdf[...] = dr2
    r.hdp[...] = pack(dr2).astype(BF16)
    loop(32, lambda t: send_to(me, t, r.hdp, r.hda.at[me], r.hs.at[2], r.hr.at[2]))
    r.sloc[5:6, :] += sum0(dy0)
    r.sloc[7:8, :] += sum0(dy0 * hn2)
    r.sloc[4:5, :] += sum0(r.hdd[...].astype(F32))

    def head_middle(i):
        for cc in range(2):
            b = 2 * i + cc
            part = col(b)
            dg = dot_bt(r.hdd[:, 0:W], down_block(b, 0)) + dot_bt(r.hdd[:, W:D], down_block(b, 1))
            du = (dg * r.hgp[:, part]).astype(BF16)
            r.dcl[:, part] += sum0(du.astype(F32))
            r.hdf[...] += dot_bt(du, weight(cc, 4 + i))

    head_middle(0)
    head_middle(1)
    tick(9)
    head_middle(2)
    head_middle(3)
    ring.drain()
    for t in (ring.other, ring.seg(True, 1), ring.seg(True, 3), ring.seg(False, 1), ring.seg(False, 3)):
        pl.semaphore_signal(r.free, inc=1, device_id={"seg": t}, device_id_type=MESH)
    df, hn1 = r.hdf[...], r.hn[0]
    dr1 = norm_back(df, hn1, r.hrst[0, :, 0:1], r.lb[6:7, :])
    de = dr1.astype(BF16)
    r.sloc[3:4, :] += sum0(df)
    r.sloc[6:7, :] += sum0(df * hn1)
    r.sloc[2:3, :] += sum0(de.astype(F32))
    do = out_back(de)
    y = cross.output_rows()
    row16 = lax.broadcasted_iota(jnp.int32, (16, D), 0)

    def put(ref, s, value):
        rows = slice(128 * s, 128 * s + 16)
        ref[rows, :] = jnp.where(row16 == 0, value[s : s + 1, :], ref[rows, :].astype(F32)).astype(ref.dtype)

    for s in range(3):
        put(r.lo, s, y)
        put(r.n2, s, dr1)
        put(r.de, s, de.astype(F32))
        put(r.do, s, do)
    pltpu.make_async_copy(r.lo, r.lo_h, r.done.at[0]).start()

    def attend_back(s):
        rows = pl.ds(pl.multiple_of(s * 128, 128), 128)
        for p in range(6):
            part = slice(128 * p, 128 * (p + 1))
            q, k, v = r.qkvv[0, rows, part], r.qkvv[1, rows, part], r.qkvv[2, rows, part]
            do = two_heads(r.do[rows, part])
            w = r.aw[s, p]
            ds = softmax_back(w.astype(F32), dot_bt(do, v)).astype(BF16)
            r.qkvv[0, rows, part] = (side_by_side(dot(ds, k)) * 0.125).astype(BF16)
            r.qkvv[1, rows, part] = (dot_at(ds, two_heads(q)) * 0.125).astype(BF16)
            r.qkvv[2, rows, part] = dot_at(w, do).astype(BF16)

    attend_back(0)
    attend_back(1)
    cross.planes(red)
    attend_back(2)
    tick(10)

    def qkv_grad(i):
        for cc in range(2):
            part = slice(cc * W, (cc + 1) * W)
            again.gb[(cc + c) % 2, i + 1] = dot_at(r.tok[...], r.qkvv[i, :, part]).astype(BF16).reshape(4, 4, 48, W)

    pl.semaphore_wait(r.free, 5)

    def qkv_out(i):
        qkv_grad(i)
        red2.to_sibling(i + 1)

    loop(3, qkv_out)
    tick(11)
    for cc in range(2):
        again.gb[(cc + c) % 2, 0] = dot_at(r.mix[...], r.de[:, cc * W : (cc + 1) * W]).astype(BF16).reshape(4, 4, 48, W)
    red2.to_sibling(0)

    def second_round(step):
        loop(4, step, 1)
        step(0)

    sf = r.sf
    sf[...] = jnp.zeros((96, D), F32)
    sf[0:8, :] = r.sloc[...]
    sf[0:1, :] = sum0(r.qkvv[0].astype(F32))
    sf[1:2, :] = sum0(r.qkvv[2].astype(F32))
    sf[8:16, :] = r.small[...]
    for i in range(4):
        sf[16 + i : 17 + i, :] = r.dcl[:, D * i : D * (i + 1)]
    own = jnp.concatenate([r.dc[0:1, :], jnp.zeros((1, D - 128), F32)], axis=1)
    own = pltpu.roll(own, 96 * (me % 8), 1)
    sf[pl.ds(20 + me // 8, 1), :] = own
    line = lax.broadcasted_iota(jnp.int32, (64, D), 0)
    for s in range(3):
        _, place = slot_layout(r.doc, (64, D), jnp.full((64, D), me * 3 + s, jnp.int32))
        sf[24:88, :] += jnp.where(line == place, r.dx[s : s + 1, :], 0.0)
    r.s0[...] = sf[...].reshape(12, 8, D).astype(BF16)
    xs, xr = r.xs, r.xr
    loop(12, lambda k: send_to(me, owner_seg(k), r.s0.at[k], r.sg.at[me], xs.at[0], xr.at[0]))

    tick(12)
    second_round(red2.step_a)
    take(r.hgr, r.hr.at[0])
    take(r.hfa, r.hr.at[1])
    take(r.hda, r.hr.at[2])
    dda, hfa, both = flat8(r.hda[...]).astype(BF16), flat8(r.hfa[...]).astype(BF16), flat8(r.hgr[...])
    line = lax.broadcasted_iota(jnp.int32, (256, 128), 0) % 8

    def low(v):
        return jnp.where(line[:, : v.shape[1]] < 3, v, 0.0)

    left, right = dot_bt(dda, r.down[:, 0:W]), dot_bt(dda, r.down[:, W:D])
    du = low((left + pltpu.roll(right, 253, 0)) * pltpu.roll(both, 253, 0)[:, 0:96])
    share_up = [dot_at(hfa, v.astype(BF16)) for v in (du, pltpu.roll(du, 3, 0))]
    r.pcu[:, :, 0:96] = jnp.concatenate(share_up, axis=0).reshape(32, 24, 96).astype(BF16)
    core = (me // 4) % 2

    def share(t):
        send_to(me, t - t % 2 + core, r.pcu.at[t], r.cu.at[t % 2, (me // 8) * 4 + me % 4], r.ks.at[3], r.kr.at[3])

    loop(32, share)
    tick(13)
    hidden = low(both)
    down_share = [dot_at(v.astype(BF16), dda)[0:96] for v in (hidden, pltpu.roll(hidden, 3, 0))]
    for n in range(8):
        j, h = n // 2, n % 2
        top = (j % 2) * 48 + 24 * h
        piece = down_share[j // 2][top : top + 24]
        r.zp[0, n] = (r.zp[0, n].astype(F32) + piece).astype(BF16)
    red.z_send(0)
    tick(14)
    cross.planes_sum(red)
    second_round(red2.step_b)
    tick(15)

    @pl.when(is_owner)
    def _():
        take(r.sg, xr.at[0])
        r.sm1[...] = jnp.sum(r.sg[...].astype(F32), axis=0).astype(BF16)
        red.peers(lambda zz: zcopy(r.sm1, r.sz.at[z], xs.at[3], xr.at[3], zz, me).start())
        pltpu.make_async_copy(r.sm1, r.sz.at[z], xr.at[3]).start()

    tick(16)
    tick(17)
    second_round(red2.step_c)

    take(r.cu, r.kr.at[3])
    for n in range(8):
        m, h = n // 2, n % 2
        for q in range(4):
            r.zc[:, 96 * q : 96 * q + 96] = r.cu[h, 4 * m + q].astype(F32)[:, 0:96]
        r.zp[1, n] = (r.zp[1, n].astype(F32) + r.zc[...]).astype(BF16)
    red.z_send(1)
    red.z_sum(0)
    second_round(red2.step_d)

    def token_grad(i):
        acc = dot_bt(r.qkvv[i, :, 0:W], weight(0, i))
        r.tg[...] += acc + dot_bt(r.qkvv[i, :, W : 2 * W], weight(1, i))

    token_grad(0)
    second_round(red2.step_e)
    red.z_send(2)
    token_grad(1)

    @pl.when(is_owner)
    def _():
        take(r.sz.at[pl.ds(0, 8)], xr.at[3])
        r.sm2[...] = jnp.sum(r.sz[0:8].astype(F32), axis=0).astype(BF16)
        loop(32, lambda t: send_to(me, t, r.sm2, r.osm.at[me // 2], xs.at[6], xr.at[6]))

    red.z_sum(1)
    token_grad(2)
    pltpu.make_async_copy(r.tg, r.tg_h, r.done.at[1]).start()
    red.z_sum(2)
    for g, ref in ((0, r.fd), (1, r.fa.at[pl.ds(8, 8)]), (2, r.fa.at[pl.ds(0, 8)])):
        take(ref, r.zsr.at[g, 1])
    take(r.osm, xr.at[6])

    take(r.lo, r.done.at[0])
    take(r.tg, r.done.at[1])

    cross.end()
    cross.drain()
    red2.sent(4)
    red.sent(8)
    red.z_sent()
    for i, (src, dst) in enumerate(swaps):
        take(src, r.sib_s.at[i])
    take(r.smg.at[pl.ds(0, 31)], r.sm_s)
    take(r.hgr.at[pl.ds(0, 31)], r.hs.at[0])
    take(r.hfa.at[pl.ds(0, 31)], r.hs.at[1])
    take(r.hda.at[pl.ds(0, 31)], r.hs.at[2])

    @pl.when(core == c)
    def _():
        take(r.pcu.at[pl.ds(0, 30)], r.ks.at[3])

    @pl.when(core != c)
    def _():
        take(r.pcu, r.ks.at[3])

    @pl.when(is_owner)
    def _():
        take(r.sg.at[pl.ds(0, 11)], xs.at[0])
        take(r.sz.at[pl.ds(0, 7)], xs.at[3])
        take(r.sz.at[pl.ds(0, 31)], xs.at[6])

    @pl.when(jnp.logical_not(is_owner))
    def _():
        take(r.sg.at[pl.ds(0, 12)], xs.at[0])


FORMAT_OUT = dict(
    lo_o=((ROWS, D), BF16),
    tg_o=((ROWS, D), F32),
    oq=((24, 3 * D), F32),
    oo=((24, D), F32),
    ou=((24, FF), F32),
    od=((96, D), F32),
    ob=((6, 24), F32),
    ouv=((1, 96), F32),
    og=((2, 24), F32),
    xoq=((24, 3 * D), F32),
    xoo=((24, D), F32),
    xou=((24, FF), F32),
    xod=((96, D), F32),
    xob=((6, 24), F32),
    xouv=((1, 96), F32),
    xog=((2, 24), F32),
    opos=((2, D), F32),
)


def format_kernel(*refs):
    r = fields(list(F_OUT) + list(FORMAT_OUT), refs)
    me = lax.axis_index("seg")
    r.lo_o[...] = r.lo_h[...]
    r.tg_o[...] = r.tg_h[...]
    for p in range(6):
        for j in range(3):
            r.xoq[:, D * j + 128 * p : D * j + 128 * (p + 1)] = r.cf[p // 2, p % 2, :, 128 * j : 128 * (j + 1)].astype(F32)
    for i in range(2):
        r.xoo[:, W * i : W * (i + 1)] = r.cf[3, i].astype(F32)
        for n in range(4):
            m = 8 + 4 * i + n
            r.xod[24 * n : 24 * (n + 1), W * i : W * (i + 1)] = r.cf[m // 2, m % 2].astype(F32)
    for t in range(32):
        r.xou[:, 96 * t : 96 * t + 96] = r.uf[t // 4, t % 4].astype(F32)[:, 0:96]
    for n in range(8):
        j, h = n // 2, n % 2
        top = (j % 2) * 48 + 24 * h
        r.od[top : top + 24, (j // 2) * W : (j // 2 + 1) * W] = r.fd[n].astype(F32)
    for u in range(8, 16):
        r.ou[:, W * (u - 8) : W * (u - 7)] = r.fa[u].astype(F32)
    ours = pltpu.roll(r.osm[0:2].astype(F32).reshape(16, D), (D - 24 * me) % D, 1)
    r.ob[...] = ours[0:6, 0:24]
    r.og[...] = ours[6:8, 0:24]
    r.xob[...] = ours[8:14, 0:24]
    r.xog[...] = ours[14:16, 0:24]
    ups = pltpu.roll(r.osm[2].astype(F32), (D - 96 * (me % 8)) % D, 1)
    line = lax.broadcasted_iota(jnp.int32, (8, D), 0)
    r.ouv[...] = sum0(jnp.where(line == me // 8, ups, 0.0))[:, 0:96]
    r.xouv[...] = sum0(jnp.where(line == 4 + me // 8, ups, 0.0))[:, 0:96]
    r.opos[...] = pltpu.roll(r.osm[3 + me // 4].astype(F32), (8 - 2 * (me % 4)) % 8, 0)[0:2]
    for u in range(8):
        if u < 6:
            r.oq[:, W * u : W * (u + 1)] = r.fa[u].astype(F32)
        else:
            r.oo[:, W * (u - 6) : W * (u - 5)] = r.fa[u].astype(F32)


def call(kernel, name, ins, outs, scratch, cid, args):
    vm, smem = pl.BlockSpec(memory_space=pltpu.VMEM), pl.BlockSpec(memory_space=pltpu.SMEM)
    hbm = pl.BlockSpec(memory_space=pl.ANY)
    return pl.pallas_call(
        kernel,
        out_shape=tuple(jax.ShapeDtypeStruct(s, t) for s, t in outs.values()),
        in_specs=[smem if n == "doc" else vm for n in ins],
        out_specs=tuple(hbm if n in ("lo_h", "tg_h") else vm for n in outs),
        scratch_shapes=list(scratch.values()),
        compiler_params=pltpu.CompilerParams(
            collective_id=cid, has_side_effects=cid is not None, vmem_limit_bytes=63 << 20
        ),
        name=name,
    )(*args)


def shards(tokens, doc, qkv, out, up, down, bias, upbias, gains, cqkv, cout, cup, cdown, cbias, cupbias, cgains, pos, cot):
    made = call(
        layer_kernel, "layer", F_IN, F_OUT, F_SCR, 0,
        (tokens, cot, qkv, out, up, down, bias, upbias.reshape(1, 96), gains, cqkv, cout, cup, cdown, cbias,
         cupbias.reshape(1, 96), cgains, pos, doc),
    )
    out = dict(zip(FORMAT_OUT, call(format_kernel, "format", list(F_OUT), FORMAT_OUT, {}, None, made)))
    out["ouv"], out["xouv"] = out["ouv"].reshape(96), out["xouv"].reshape(96)
    return tuple(out.values())


def solution(mesh):
    both, seg, cols, flat = P(("grp", "seg"), None), P("seg", None), P(None, "seg"), P("seg")
    weights = (seg, seg, seg, seg, cols, flat, cols)
    in_specs = (both, P("grp", None)) + weights + weights + (seg, both)
    out_specs = (both, both) + weights + weights + (seg,)
    return jax.shard_map(shards, mesh=mesh, in_specs=in_specs, out_specs=out_specs, check_vma=False)
```

time: 232 us -> 191 us (0.82)
  Pallas kernels: 231 us -> 189 us
    pallas_call x3 -> x2, Pallas kernels: 231 us -> 189 us  [call(): pl.pallas_call(kernel, out_shape=tuple((jax.ShapeDtypeStruct(s, t) for s,...]
where the time goes in v2:
time: 191 us; the launch traced here: 190 us
  Pallas kernels  189 us (99%)
    pallas_call x2, Pallas kernels, call(): pl.pallas_call(kernel, out_shape=tuple((jax.ShapeDtypeStruct(s, t) for s,...  189 us

profile of v2, /device:TPU:1, one launch (start us, length us, event | category | flops | bytes accessed | tf_op | source)
XLA Modules:
  0.0 189.6 jit_solution(10749090437272133315)
XLA Ops:
  0.7 185.1 %layer.1 = (bf16[384,768]{1,0:T(8,128)(2,1)}, f32[384,768]{1,0:T(8,128)}, bf16[16,24,384]{2,1,0:T(8,128)(2,1)}, bf16[8,24,384]{2,1,0:T(8,128)(2,1)}, bf16[8,2,24...) custom-call(bf16[384,768]{1,0:T(8,128)(2,1)} %refs_0_.1, ...), custom_call_target="tpu_custom_call" | custom-call | tf_op jit(solution)/shard_map/layer/pallas_call | solution.py:1584
  185.8 3.7 %format.1 = (bf16[384,768]{1,0:T(8,128)(2,1)}, f32[384,768]{1,0:T(8,128)}, f32[24,2304]{1,0:T(8,128)}, f32[24,768]{1,0:T(8,128)}, f32[24,3072]{1,0:T(8,128)}, /*...) custom-call(bf16[384,768]{1,0:T(8,128)(2,1)} %get-tuple-element.41.r, ...), custom_call_target="tpu_custom_call" | custom-call | tf_op jit(solution)/shard_map/format/pallas_call | solution.py:1584

commit v3 on v2

--- a/solution.py
+++ b/solution.py
@@ -167,14 +167,16 @@
     p4=VM((12, 8, D), BF16),
     g46=VM((64, 8, D), BF16),
     p5=VM((2, 8, D), BF16),
-    g5=VM((12, 2, 8, D), BF16),
+    g5=VM((12, 8, D), BF16),
+    g5y=VM((2, 8, D), BF16),
+    y_r=DMA,
     p6=VM((12, 8, D), BF16),
     p7=VM((8, D), BF16),
     g7=VM((12, 8, D), BF16),
     p7f=VM((8, D), F32),
     g7f=VM((2, 8, D), F32),
-    p8=VM((12, 8, D), BF16),
-    g8=VM((6, 2, 8, D), BF16),
+    p8=VM((32, 8, W), BF16),
+    g8=VM((6, 8, W), BF16),
     gp=VM((96, 128), F32),
     gact=VM((96, 128), BF16),
     fall=VM((96, D), BF16),
@@ -285,7 +287,7 @@
         row = lax.broadcasted_iota(jnp.int32, (8, 512), 0)
         lane = lax.broadcasted_iota(jnp.int32, (8, 512), 1)
         _, place = slot_layout(a.doc, (8, 512), jnp.minimum(me * 3 + row, 95))
-        table = a.smg[...].astype(F32).reshape(512, W)[:, 256:384].astype(BF16)
+        table = a.smg[...].astype(F32).reshape(512, 256)[:, 128:256].astype(BF16)
         parts = []
         for i in range(6):
             hot = (lane == (place // 2) * 16 + (place % 2) * 6 + i) & (row < 3)
@@ -375,13 +377,14 @@
             r.own[4] = dr2
             r.p5[0] = dr2.astype(BF16)
             r.p5[1] = y.astype(BF16)
-            loop(32, lambda t: send_to(me, t, r.p5, r.g5.at[self.k], ss, rs))
+            loop(32, lambda t: send_to(me, t, r.p5.at[0], r.g5.at[self.k], ss, rs))
+            self.to_slots(lambda t, i: send_to(me, t, r.p5.at[1], r.g5y.at[i], r.c7, r.y_r))
 
     def mlp_back(self):
         r, me = self.r, self.me
         ss, rs = self.sem(8)
         take(r.g5, r.xcr.at[7])
-        dd = flat8(r.g5[:, 0]).astype(BF16)
+        dd = flat8(r.g5[...]).astype(BF16)
         r.xdd[...] = dd
         du = (dot_bt(dd, r.wdn[...]) * r.gp[...]).astype(BF16)
         r.du[...] = du
@@ -406,14 +409,17 @@
             loop(6, lambda p: send_to(me, pair_seg(p), r.p7, r.g7.at[self.k], ss, rs))
             r.p7f[...] = dr1
 
-            def one(t):
-                w = self.window(t)
-
-                @pl.when((w == self.k) | (w + 1 == self.k))
-                def _():
-                    send_to(me, t, r.p7f, r.g7f.at[self.k - w], r.c7, fr)
-
-            loop(32, one)
+            self.to_slots(lambda t, i: send_to(me, t, r.p7f, r.g7f.at[i], r.c7, fr))
+
+    def to_slots(self, fn):
+        def one(t):
+            w = self.window(t)
+
+            @pl.when((w == self.k) | (w + 1 == self.k))
+            def _():
+                fn(t, self.k - w)
+
+        loop(32, one)
 
     def attention_back(self):
         r, me = self.r, self.me
@@ -431,21 +437,27 @@
             r.dq[:, 0:128] = (side_by_side(dot(ds, k)) * 0.125).astype(BF16)
             r.dq[:, 128:256] = (dot_at(ds, two_heads(q)) * 0.125).astype(BF16)
             r.dq[:, 256:384] = dot_at(w.astype(BF16), do2).astype(BF16)
-            r.p8[...] = rows8(dot_bt(r.dq[...], r.wqkv[...])).astype(BF16)
-            loop(32, lambda t: send_to(me, t, r.p8.at[pl.ds(self.window(t), 2)], r.g8.at[self.p], ss, rs))
+            dx = dot_bt(r.dq[...], r.wqkv[...]).astype(BF16)
+            line = lax.broadcasted_iota(jnp.int32, (256, 96), 0)
+            place = (line // 8) * 3 + line % 8 - lax.broadcasted_iota(jnp.int32, (256, 96), 1)
+            left = ((line % 8 < 3) & (place == 0)).astype(BF16)
+            right = ((line % 8 >= 3) & (line % 8 < 6) & (place == 3)).astype(BF16)
+            r.p8[...] = rows8(dot(left, dx[:, 0:W]) + dot(right, dx[:, W:D])).astype(BF16)
+            loop(32, lambda t: send_to(me, t, r.p8.at[t], r.g8.at[self.p], ss, rs))
 
     def finish(self):
         r = self.r
         take(r.g7f, r.xcr.at[10])
         take(r.g8, r.xcr.at[11])
-        total = r.g7f[...] + jnp.sum(r.g8[...].astype(F32), axis=0)
+        total = jnp.sum(r.g8[...].astype(F32), axis=0)
         shift = 3 * self.me - 8 * self.window(self.me)
-        return pltpu.roll(total.reshape(16, D), 16 - shift, 0)[0:8]
+        rest = pltpu.roll(r.g7f[...].reshape(16, D), 16 - shift, 0)[0:8]
+        return rest + jnp.concatenate([total, pltpu.roll(total, 5, 0)], axis=1)
 
     def output_rows(self):
-        w = self.window(self.me)
-        y = self.r.g5[pl.ds(w, 2), 1].astype(F32).reshape(16, D)
-        return pltpu.roll(y, 16 - (3 * self.me - 8 * w), 0)[0:8]
+        take(self.r.g5y, self.r.y_r)
+        y = self.r.g5y[...].astype(F32).reshape(16, D)
+        return pltpu.roll(y, 16 - (3 * self.me - 8 * self.window(self.me)), 0)[0:8]
 
     def grads(self):
         r, a = self.r, self.a
@@ -499,12 +511,12 @@
         @pl.when(self.is_pair)
         def _():
             take(r.g46.at[pl.ds(0, 12)], cs.at[4])
-            take(r.g46.at[pl.ds(0, 62)], cs.at[11])
+            take(r.p8.at[pl.ds(0, 31)], cs.at[11])
 
         @pl.when(self.is_owner)
         def _():
             take(r.g46.at[pl.ds(0, 31)], cs.at[5])
-            take(r.g46.at[pl.ds(0, 62)], cs.at[7])
+            take(r.g46.at[pl.ds(0, 31)], cs.at[7])
             take(r.g46.at[pl.ds(0, 6)], cs.at[9])
 
             count = jnp.int32(0)
@@ -515,7 +527,7 @@
 
                 @pl.when(count == n)
                 def _():
-                    take(r.g46.at[pl.ds(0, 2 * n)], r.c7)
+                    take(r.g46.at[pl.ds(0, 3 * n)], r.c7)
 
 
 class CrossGrads(Cross):
@@ -637,6 +649,25 @@
     def __init__(self, r):
         super().__init__()
         self.r = r
+        self.z = lax.axis_index("grp")
+        self.mine, self.others = 4 + 2 * (self.z % 2), 6 - 2 * (self.z % 2)
+
+    def unit(self, i):
+        return jnp.where(i < 3, i, jnp.where(i < 5, self.mine + i - 3, jnp.where(i == 5, 3, i + 2)))
+
+    def to_plane(self, k, row):
+        @pl.when((k >= 4) & (k < 8))
+        def _():
+            z = (self.z + 1 + 6 * (k % 2)) % 8
+            zcopy(row, row, self.r.up_s, self.r.up_r.at[k - 4], z, self.me).start()
+
+    def from_planes(self):
+        r = self.r
+        for j in range(2):
+            k = self.others + j
+            unit = r.ws.at[self.c, k]
+            take(unit, r.up_r.at[k - 4])
+            rcopy(unit, unit, r.s3, r.r3.at[k], self.other).start()
 
     def v1(self, k, part, off):
         mine = self.r.ws.at[self.c, k]
@@ -656,7 +687,9 @@
             rcopy(src, own, r.s1, r.r1.at[k, 0], self.ring(part, 1, 1)).start()
             rcopy(src, own, r.s1, r.r1.at[k, 1], self.ring(part, 1, 3)).start()
 
-        self.by_part(k, go)
+        @pl.when((k < 4) | (k >= 8) | (k // 2 == self.mine // 2))
+        def _():
+            self.by_part(k, go)
 
     def first_on(self, k):
         r, ahead = self.r, self.ahead(k)
@@ -679,6 +712,7 @@
             rcopy(row, row, r.s2, r.r2.at[k, 0], self.ring(part, 2, 1)).start()
             rcopy(row, row, r.s2, r.r2.at[k, 1], self.ring(part, 2, 3)).start()
             rcopy(row, row, r.s3, r.r3.at[k], self.other).start()
+            self.to_plane(k, row)
 
         self.by_part(k, go)
 
@@ -690,9 +724,11 @@
             take(row, r.r2.at[k, ahead // 2])
             rcopy(row, row, r.s2, r.r2.at[k, 2], self.ring(part, 2, ahead)).start()
             rcopy(row, row, r.s3, r.r3.at[k], self.other).start()
+            self.to_plane(k, row)
             row = self.v2(k, part, ahead)
             take(row, r.r2.at[k, 1 - ahead // 2])
             rcopy(row, row, r.s3, r.r3.at[k], self.other).start()
+            self.to_plane(k, row)
 
         self.by_part(k, go)
 
@@ -703,6 +739,7 @@
             row = self.v2(k, part, 2)
             take(row, r.r2.at[k, 2])
             rcopy(row, row, r.s3, r.r3.at[k], self.other).start()
+            self.to_plane(k, row)
 
         self.by_part(k, go)
 
@@ -713,8 +750,9 @@
     def drain(self):
         r = self.r
 
-        take(r.ws.at[0, pl.ds(0, 9), 0], r.s1)
-        take(r.ws.at[0, pl.ds(0, 9)], r.s2)
+        take(r.ws.at[0, pl.ds(0, 10), 0, pl.ds(0, 3)], r.s1)
+        take(r.ws.at[0, pl.ds(0, 10), pl.ds(0, 3)], r.s2)
+        take(r.ws.at[0, pl.ds(0, 2)], r.up_s)
         take(r.ws.at[0], r.s3)
 
 
@@ -768,7 +806,7 @@
         self.by_part(k, go)
 
     def step_c(self, k):
-        r, ahead = self.r, self.ahead(k)
+        r = self.r
         take(r.r0.at[0, pl.ds(0, 2)], r.mr.at[k, 2])
 
         def go(part):
@@ -779,39 +817,22 @@
 
             loop(4, add)
             q = self.pos(part, 1)
-            far, back = r.t1.at[k, (q + 2) % 4], r.t1.at[k, (q + 4 - ahead) % 4]
-            rcopy(far, r.f1.at[k], r.ms.at[2], r.mr.at[k, 3], self.ring(part, 1, ahead)).start()
-            rcopy(back, r.b1.at[k], r.ms.at[2], r.mr.at[k, 4], self.ring(part, 1, 4 - ahead)).start()
+            for step, dst in ((1, r.a1), (2, r.f1), (3, r.b1)):
+                block = r.t1.at[k, (q + step) % 4]
+                rcopy(block, dst.at[k], r.ms.at[2], r.mr.at[k, 3], self.ring(part, 1, step)).start()
 
         self.by_part(k, go)
 
     def step_d(self, k):
-        r, ahead = self.r, self.ahead(k)
-        take(r.f1.at[k], r.mr.at[k, 3])
+        r = self.r
+        take(r.r0.at[0, 0, pl.ds(0, 3)], r.mr.at[k, 3])
 
         def go(part):
-            n = (self.pos(part, 1) + ahead) % 4
-            r.t1[k, n] = (r.t1[k, n].astype(F32) + r.f1[k].astype(F32)).astype(BF16)
-            rcopy(r.t1.at[k, n], r.a1.at[k], r.ms.at[2], r.mr.at[k, 4], self.ring(part, 1, ahead)).start()
+            t = r.t1[k, self.pos(part, 1)].astype(F32) + r.f1[k].astype(F32)
+            t += r.a1[k].astype(F32) + r.b1[k].astype(F32)
+            self.pieces[k // 4, pl.ds(2 * (k % 4), 2)] = t.reshape(2, 24, W).astype(BF16)
 
         self.by_part(k, go)
-
-    def step_e(self, k):
-        r = self.r
-        take(r.r0.at[0, 0, pl.ds(0, 2)], r.mr.at[k, 4])
-
-        def go(part):
-            t = r.t1[k, self.pos(part, 1)].astype(F32) + r.a1[k].astype(F32) + r.b1[k].astype(F32)
-            self.pieces[k // 4, pl.ds(2 * (k % 4), 2)] = t.reshape(2, 24, W).astype(BF16)
-
-        self.by_part(k, go)
-
-    def tick(self, t, slots):
-        for lag, step in ((0, self.step_a), (3, self.step_b), (6, self.step_c), (8, self.step_d), (10, self.step_e)):
-
-            @pl.when((t >= lag) & (t < lag + slots))
-            def _():
-                step(t - lag)
 
     def sent(self, slots):
         r = self.r
@@ -891,7 +912,7 @@
         f1=VM((n, 48, W), BF16),
         a1=VM((n, 48, W), BF16),
         b1=VM((n, 48, W), BF16),
-        mr=DMA((n, 5)),
+        mr=DMA((n, 4)),
         ms=DMA((3,)),
     )
 
@@ -902,9 +923,9 @@
     sibq=VM((24, 3 * D), BF16),
     sibo=VM((24, D), BF16),
     sibu=VM((24, FF), BF16),
-    smf=VM((16, W), F32),
-    sm=VM((16, W), BF16),
-    smg=VM((32, 16, W), BF16),
+    smf=VM((16, 256), F32),
+    sm=VM((16, 256), BF16),
+    smg=VM((16, 2, 16, 256), BF16),
     both=VM((16, D), F32),
     lb=VM((8, D), F32),
     lub=VM((1, FF), F32),
@@ -933,8 +954,8 @@
     hr=DMA((3,)),
     sib_s=DMA((3,)),
     sib_r=DMA((3,)),
-    sm_s=DMA,
-    sm_r=DMA,
+    sm_s=DMA((2,)),
+    sm_r=DMA((2,)),
     own_sem=DMA((12,)),
     s1=DMA,
     r1=DMA((12, 2)),
@@ -942,14 +963,15 @@
     r2=DMA((12, 3)),
     s3=DMA,
     r3=DMA((12,)),
+    up_s=DMA,
+    up_r=DMA((4,)),
     lo=VM((ROWS, D), BF16),
     tg=VM((ROWS, D), F32),
     done=DMA((2,)),
     sloc=VM((8, D), F32),
     dcl=VM((1, FF), F32),
     dx=VM((8, D), F32),
-    hfa=VM((32, 8, W), BF16),
-    hda=VM((32, 8, W), BF16),
+    hfd=VM((2, 16, 2, 8, W), BF16),
     hgr=VM((32, 8, 128), BF16),
     gdn=VM((96, D), BF16),
     small=VM((8, D), F32),
@@ -978,7 +1000,7 @@
     ks=DMA((4,)),
     kr=DMA((4,)),
     free=pltpu.SemaphoreType.REGULAR,
-    mr2=DMA((4, 5)),
+    mr2=DMA((4, 4)),
     ms2=DMA((3,)),
     **reduce_scratch(8),
     **{("x" + n if n in ("rst", "dd", "de", "cs", "cr") else n): v for n, v in CROSS.items()},
@@ -1016,16 +1038,16 @@
             pl.semaphore_signal(bar, inc=1, device_id={"grp": zz, "seg": seg}, device_id_type=MESH)
 
     red.peers(greet)
-    r.smf[...] = jnp.zeros((16, W), F32)
+    r.smf[...] = jnp.zeros((16, 256), F32)
     r.smf[0:6, 0:24] = r.bias[...].astype(F32)
     r.smf[6:8, 0:24] = r.gains[...].astype(F32)
     r.smf[8:14, 0:24] = r.cbias[...].astype(F32)
     r.smf[14:16, 0:24] = r.cgains[...].astype(F32)
-    r.smf[0:1, 128:224] = r.upbias[...].astype(F32)
+    r.smf[0:1, 32:128] = r.upbias[...].astype(F32)
     table = r.pos[...].astype(F32)
     for t in range(2):
         for i in range(6):
-            r.smf[6 * t + i : 6 * t + i + 1, 256:384] = table[t : t + 1, 128 * i : 128 * (i + 1)]
+            r.smf[6 * t + i : 6 * t + i + 1, 128:256] = table[t : t + 1, 128 * i : 128 * (i + 1)]
     r.sm[...] = r.smf[...].astype(BF16)
     r.cub[...] = jnp.zeros((8, 128), F32)
     r.cub[0:1, 0:96] = r.cupbias[...].astype(F32)
@@ -1054,49 +1076,51 @@
     arrive(2)
     loop(8, lambda k: compose(k, r.up, r.sibu, 2 * (k - 4) + c), 4)
     loop(12, ring.first, 8)
-    loop(32, lambda t: send_to(me, t, r.sm, r.smg.at[me], r.sm_s, r.sm_r))
-    loop(12, ring.first_on)
-    loop(6, ring.second)
-    cross.reshard()
-
-    take(r.smg, r.sm_r)
+    loop(16, lambda t: send_to(me, 2 * t + c, r.sm, r.smg.at[me // 2, c], r.sm_s.at[0], r.sm_r.at[0]))
+    loop(10, lambda i: ring.first_on(ring.unit(i)))
+    loop(6, lambda i: ring.second(ring.unit(i)))
+    take(r.smg.at[:, 0], r.sm_r.at[0])
+    rcopy(r.smg.at[:, c], r.smg.at[:, c], r.sm_s.at[1], r.sm_r.at[1], ring.other).start()
+
+    def tick(i):
+        ring.second_on(ring.unit(i))
+
+        @pl.when(i < 4)
+        def _():
+            ring.second(ring.unit(i + 6))
+
+        @pl.when(i >= 3)
+        def _():
+            ring.last(ring.unit(i - 3))
+
+    def weight(cc, k):
+        return r.ws[cc, k].reshape(D, W)
+
+    loop(3, tick)
+    take(r.smg.at[:, 0], r.sm_r.at[1])
     for t in range(32):
-        block = r.smg[t].astype(F32)
+        block = r.smg[t // 2, t % 2].astype(F32)
         r.both[:, 24 * t : 24 * t + 24] = block[:, 0:24]
-        r.lub[:, 96 * t : 96 * t + 96] = block[0:1, 128:224]
+        r.lub[:, 96 * t : 96 * t + 96] = block[0:1, 32:128]
     r.lb[...] = r.both[0:8, :]
     r.cb[...] = r.both[8:16, :]
-
-    def tick(k):
-        ring.second_on(k)
-
-        @pl.when(k < 6)
-        def _():
-            ring.second(k + 6)
-
-        @pl.when(k >= 3)
-        def _():
-            ring.last(k - 3)
-
-    def weight(cc, k):
-        return r.ws[cc, k].reshape(D, W)
-
-    loop(5, tick)
+    tick(3)
 
     def project(k):
         tick(k)
-        i = k - 5
+        i = k - 4
         ring.arrived(i)
         shift = jnp.where(i == 0, r.lb[0:1, :], jnp.where(i == 2, r.lb[1:2, :], 0.0))
         for cc in range(2):
             part = slice(cc * W, (cc + 1) * W)
             r.qkvv[i, :, part] = (dot(r.tok[...], weight(cc, i)) + shift[:, part]).astype(BF16)
 
-    loop(8, project, 5)
+    loop(7, project, 4)
+    cross.reshard()
 
     def attend(k):
         tick(k)
-        s = k - 8
+        s = k - 7
         rows = pl.ds(pl.multiple_of(s * 128, 128), 128)
         for p in range(6):
             part = slice(128 * p, 128 * (p + 1))
@@ -1104,14 +1128,11 @@
             r.aw[s, p] = w
             r.mix[rows, part] = side_by_side(dot(w, r.qkvv[2, rows, part])).astype(BF16)
 
-    loop(11, attend, 8)
-    tick(11)
+    loop(10, attend, 7)
     ring.arrived(3)
     for cc in range(2):
         part = slice(cc * W, (cc + 1) * W)
         r.n1[:, part] = dot(r.mix[...], weight(cc, 3)) + (r.tok[:, part].astype(F32) + r.lb[2:3, part])
-    ring.last(9)
-
     row8 = lax.broadcasted_iota(jnp.int32, (8, D), 0)
     r.sloc[...] = jnp.zeros((8, D), F32)
 
@@ -1140,11 +1161,14 @@
             r.hg[:, part] = jnp.where(keep, g, 0.0).astype(BF16)
             r.hgp[:, part] = gp
 
-        @pl.when(i < 6)
-        def _():
-            ring.last(i + 6)
-
-    loop(8, head_up, 4)
+    head_up(ring.mine)
+    head_up(ring.mine + 1)
+    ring.last(ring.unit(7))
+    ring.from_planes()
+    ring.last(ring.unit(8))
+    ring.last(ring.unit(9))
+    head_up(ring.others)
+    head_up(ring.others + 1)
 
     def down_rows(x, kc):
         pieces = [r.ws[cc, 8 + 2 * kc + j, x, y] for y in range(4) for cc in range(2) for j in range(2)]
@@ -1243,14 +1267,10 @@
     def out_back(de):
         return dot_bt(de[:, 0:W], weight(0, 3)) + dot_bt(de[:, W:D], weight(1, 3))
 
-    def tick(t):
-        red.tick(t, 8)
-
     blocks(norm_one)
-    raise_up(4)
+    loop(6, raise_up, 4)
     cross.attention()
-    loop(8, raise_up, 5)
-    cross.first_norm()
+    loop(8, raise_up, 6)
     def pack(value):
         n = value.shape[1] // 2
         row = lax.broadcasted_iota(jnp.int32, (8, n), 0)
@@ -1264,8 +1284,7 @@
         both = jnp.concatenate([hidden[:, part], slope[:, part]], axis=1)
         r.hgs[t, :, 0:96] = pack(both).astype(BF16)
     r.hfp[...] = pack(r.hf[...].astype(F32)).astype(BF16)
-    loop(32, lambda t: send_to(me, t, r.hgs.at[t], r.hgr.at[me], r.hs.at[0], r.hr.at[0]))
-    loop(32, lambda t: send_to(me, t, r.hfp, r.hfa.at[me], r.hs.at[1], r.hr.at[1]))
+    cross.first_norm()
     lower(0)
     lower(1)
     cross.mlp()
@@ -1274,30 +1293,20 @@
     cross.second_norm()
     loop(8, down_grad, 4)
     loop(4, red.to_sibling)
-    middle(0)
-    tick(0)
+    loop(2, middle)
     cross.mlp_back()
-    middle(1)
-    tick(1)
     middle(2)
-    tick(2)
-    middle(3)
-    tick(3)
+    loop(4, red.step_a)
+    loop(5, middle, 3)
     cross.first_norm_back()
-    middle(4)
-    tick(4)
-    middle(5)
-    middle(6)
-    tick(5)
-    middle(7)
+    loop(8, middle, 5)
     cross.attention_back()
-    tick(6)
+    loop(4, red.step_b)
     blocks(norm_one_back)
     r.do[...] = out_back(r.de[...]).astype(BF16)
-    tick(7)
+    loop(6, red.step_a, 4)
     cross.grads()
     cross.scatter()
-    tick(8)
     r.dx[...] = jnp.where(row8 < 3, cross.finish(), 0.0)
 
     dy0, hn2 = r.dx[...], r.hn[1]
@@ -1305,7 +1314,10 @@
     r.hdd[...] = dr2.astype(BF16)
     r.hdf[...] = dr2
     r.hdp[...] = pack(dr2).astype(BF16)
-    loop(32, lambda t: send_to(me, t, r.hdp, r.hda.at[me], r.hs.at[2], r.hr.at[2]))
+    loop(16, lambda t: send_to(me, 2 * t + c, r.hdp, r.hfd.at[1, me // 2, c], r.hs.at[1], r.hr.at[1]))
+    loop(32, lambda t: send_to(me, t, r.hgs.at[t], r.hgr.at[me], r.hs.at[0], r.hr.at[0]))
+    loop(16, lambda t: send_to(me, 2 * t + c, r.hfp, r.hfd.at[0, me // 2, c], r.hs.at[1], r.hr.at[1]))
+    loop(8, red.step_a, 6)
     r.sloc[5:6, :] += sum0(dy0)
     r.sloc[7:8, :] += sum0(dy0 * hn2)
     r.sloc[4:5, :] += sum0(r.hdd[...].astype(F32))
@@ -1319,11 +1331,7 @@
             r.dcl[:, part] += sum0(du.astype(F32))
             r.hdf[...] += dot_bt(du, weight(cc, 4 + i))
 
-    head_middle(0)
-    head_middle(1)
-    tick(9)
-    head_middle(2)
-    head_middle(3)
+    loop(4, head_middle)
     ring.drain()
     for t in (ring.other, ring.seg(True, 1), ring.seg(True, 3), ring.seg(False, 1), ring.seg(False, 3)):
         pl.semaphore_signal(r.free, inc=1, device_id={"seg": t}, device_id_type=MESH)
@@ -1361,31 +1369,33 @@
             r.qkvv[2, rows, part] = dot_at(w, do).astype(BF16)
 
     attend_back(0)
+    loop(6, red.step_b, 4)
+    pl.semaphore_wait(r.free, 5)
+    for cc in range(2):
+        again.gb[(cc + c) % 2, 0] = dot_at(r.mix[...], r.de[:, cc * W : (cc + 1) * W]).astype(BF16).reshape(4, 4, 48, W)
+    red2.to_sibling(0)
     attend_back(1)
     cross.planes(red)
     attend_back(2)
-    tick(10)
+    loop(8, red.step_b, 6)
 
     def qkv_grad(i):
         for cc in range(2):
             part = slice(cc * W, (cc + 1) * W)
             again.gb[(cc + c) % 2, i + 1] = dot_at(r.tok[...], r.qkvv[i, :, part]).astype(BF16).reshape(4, 4, 48, W)
 
-    pl.semaphore_wait(r.free, 5)
-
     def qkv_out(i):
         qkv_grad(i)
         red2.to_sibling(i + 1)
 
     loop(3, qkv_out)
-    tick(11)
-    for cc in range(2):
-        again.gb[(cc + c) % 2, 0] = dot_at(r.mix[...], r.de[:, cc * W : (cc + 1) * W]).astype(BF16).reshape(4, 4, 48, W)
-    red2.to_sibling(0)
+    take(r.hfd.at[:, :, 0], r.hr.at[1])
+    rcopy(r.hfd.at[:, :, c], r.hfd.at[:, :, c], r.hs.at[2], r.hr.at[2], ring.other).start()
+    loop(4, red.step_c)
+    red2.step_a(0)
 
     def second_round(step):
-        loop(4, step, 1)
-        step(0)
+        loop(4, step)
 
     sf = r.sf
     sf[...] = jnp.zeros((96, D), F32)
@@ -1406,12 +1416,12 @@
     xs, xr = r.xs, r.xr
     loop(12, lambda k: send_to(me, owner_seg(k), r.s0.at[k], r.sg.at[me], xs.at[0], xr.at[0]))
 
-    tick(12)
-    second_round(red2.step_a)
+    loop(4, red2.step_a, 1)
+    loop(8, red.step_c, 4)
     take(r.hgr, r.hr.at[0])
-    take(r.hfa, r.hr.at[1])
-    take(r.hda, r.hr.at[2])
-    dda, hfa, both = flat8(r.hda[...]).astype(BF16), flat8(r.hfa[...]).astype(BF16), flat8(r.hgr[...])
+    take(r.hfd.at[:, :, 0], r.hr.at[2])
+    hfa, dda = [r.hfd[i].astype(F32).reshape(256, W).astype(BF16) for i in range(2)]
+    both = flat8(r.hgr[...])
     line = lax.broadcasted_iota(jnp.int32, (256, 128), 0) % 8
 
     def low(v):
@@ -1427,7 +1437,7 @@
         send_to(me, t - t % 2 + core, r.pcu.at[t], r.cu.at[t % 2, (me // 8) * 4 + me % 4], r.ks.at[3], r.kr.at[3])
 
     loop(32, share)
-    tick(13)
+    loop(4, red.step_d)
     hidden = low(both)
     down_share = [dot_at(v.astype(BF16), dda)[0:96] for v in (hidden, pltpu.roll(hidden, 3, 0))]
     for n in range(8):
@@ -1436,10 +1446,9 @@
         piece = down_share[j // 2][top : top + 24]
         r.zp[0, n] = (r.zp[0, n].astype(F32) + piece).astype(BF16)
     red.z_send(0)
-    tick(14)
     cross.planes_sum(red)
     second_round(red2.step_b)
-    tick(15)
+    loop(8, red.step_d, 4)
 
     @pl.when(is_owner)
     def _():
@@ -1447,10 +1456,6 @@
         r.sm1[...] = jnp.sum(r.sg[...].astype(F32), axis=0).astype(BF16)
         red.peers(lambda zz: zcopy(r.sm1, r.sz.at[z], xs.at[3], xr.at[3], zz, me).start())
         pltpu.make_async_copy(r.sm1, r.sz.at[z], xr.at[3]).start()
-
-    tick(16)
-    tick(17)
-    second_round(red2.step_c)
 
     take(r.cu, r.kr.at[3])
     for n in range(8):
@@ -1459,15 +1464,15 @@
             r.zc[:, 96 * q : 96 * q + 96] = r.cu[h, 4 * m + q].astype(F32)[:, 0:96]
         r.zp[1, n] = (r.zp[1, n].astype(F32) + r.zc[...]).astype(BF16)
     red.z_send(1)
+    second_round(red2.step_c)
     red.z_sum(0)
-    second_round(red2.step_d)
 
     def token_grad(i):
         acc = dot_bt(r.qkvv[i, :, 0:W], weight(0, i))
         r.tg[...] += acc + dot_bt(r.qkvv[i, :, W : 2 * W], weight(1, i))
 
     token_grad(0)
-    second_round(red2.step_e)
+    second_round(red2.step_d)
     red.z_send(2)
     token_grad(1)
 
@@ -1495,10 +1500,11 @@
     red.z_sent()
     for i, (src, dst) in enumerate(swaps):
         take(src, r.sib_s.at[i])
-    take(r.smg.at[pl.ds(0, 31)], r.sm_s)
+    take(r.smg.at[pl.ds(0, 15), 0], r.sm_s.at[0])
+    take(r.smg.at[:, 0], r.sm_s.at[1])
     take(r.hgr.at[pl.ds(0, 31)], r.hs.at[0])
-    take(r.hfa.at[pl.ds(0, 31)], r.hs.at[1])
-    take(r.hda.at[pl.ds(0, 31)], r.hs.at[2])
+    take(r.hfd.at[:, pl.ds(0, 15), 0], r.hs.at[1])
+    take(r.hfd.at[:, :, 0], r.hs.at[2])
 
     @pl.when(core == c)
     def _():

time: 191 us -> 178 us (0.932)
  Pallas kernels: 189 us -> 177 us
    pallas_call x2, Pallas kernels: 189 us -> 177 us  [call(): pl.pallas_call(kernel, out_shape=tuple((jax.ShapeDtypeStruct(s, t) for s,...]
where the time goes in v3:
time: 178 us
  Pallas kernels  177 us (99%)
    pallas_call x2, Pallas kernels, call(): pl.pallas_call(kernel, out_shape=tuple((jax.ShapeDtypeStruct(s, t) for s,...  177 us

profile of v3, /device:TPU:1, one launch (start us, length us, event | category | flops | bytes accessed | tf_op | source)
XLA Modules:
  0.0 177.9 jit_solution(6798264398208689658)
XLA Ops:
  0.7 173.4 %layer.1 = (bf16[384,768]{1,0:T(8,128)(2,1)}, f32[384,768]{1,0:T(8,128)}, bf16[16,24,384]{2,1,0:T(8,128)(2,1)}, bf16[8,24,384]{2,1,0:T(8,128)(2,1)}, bf16[8,2,24...) custom-call(bf16[384,768]{1,0:T(8,128)(2,1)} %refs_0_.1, ...), custom_call_target="tpu_custom_call" | custom-call | tf_op jit(solution)/shard_map/layer/pallas_call | solution.py:1590
  174.1 3.7 %format.1 = (bf16[384,768]{1,0:T(8,128)(2,1)}, f32[384,768]{1,0:T(8,128)}, f32[24,2304]{1,0:T(8,128)}, f32[24,768]{1,0:T(8,128)}, f32[24,3072]{1,0:T(8,128)}, /*...) custom-call(bf16[384,768]{1,0:T(8,128)(2,1)} %get-tuple-element.41.r, ...), custom_call_target="tpu_custom_call" | custom-call | tf_op jit(solution)/shard_map/format/pallas_call | solution.py:1590

commit v4 on v3

--- a/solution.py
+++ b/solution.py
@@ -1389,10 +1389,10 @@
         red2.to_sibling(i + 1)
 
     loop(3, qkv_out)
+    loop(4, red2.step_a)
     take(r.hfd.at[:, :, 0], r.hr.at[1])
     rcopy(r.hfd.at[:, :, c], r.hfd.at[:, :, c], r.hs.at[2], r.hr.at[2], ring.other).start()
     loop(4, red.step_c)
-    red2.step_a(0)
 
     def second_round(step):
         loop(4, step)
@@ -1416,7 +1416,6 @@
     xs, xr = r.xs, r.xr
     loop(12, lambda k: send_to(me, owner_seg(k), r.s0.at[k], r.sg.at[me], xs.at[0], xr.at[0]))
 
-    loop(4, red2.step_a, 1)
     loop(8, red.step_c, 4)
     take(r.hgr, r.hr.at[0])
     take(r.hfd.at[:, :, 0], r.hr.at[2])

time: 178 us -> 188 us (1.056); the launches traced: 178 us -> 185 us
  Pallas kernels: 177 us -> 184 us
    pallas_call x2, Pallas kernels: 177 us -> 184 us  [call(): pl.pallas_call(kernel, out_shape=tuple((jax.ShapeDtypeStruct(s, t) for s,...]
where the time goes in v4:
time: 188 us; the launch traced here: 185 us
  Pallas kernels  184 us (98%)
    pallas_call x2, Pallas kernels, call(): pl.pallas_call(kernel, out_shape=tuple((jax.ShapeDtypeStruct(s, t) for s,...  184 us

profile of v4, /device:TPU:1, one launch (start us, length us, event | category | flops | bytes accessed | tf_op | source)
XLA Modules:
  0.0 184.5 jit_solution(245037562998393930)
XLA Ops:
  0.7 180.0 %layer.1 = (bf16[384,768]{1,0:T(8,128)(2,1)}, f32[384,768]{1,0:T(8,128)}, bf16[16,24,384]{2,1,0:T(8,128)(2,1)}, bf16[8,24,384]{2,1,0:T(8,128)(2,1)}, bf16[8,2,24...) custom-call(bf16[384,768]{1,0:T(8,128)(2,1)} %refs_0_.1, ...), custom_call_target="tpu_custom_call" | custom-call | tf_op jit(solution)/shard_map/layer/pallas_call | solution.py:1589
  180.7 3.7 %format.1 = (bf16[384,768]{1,0:T(8,128)(2,1)}, f32[384,768]{1,0:T(8,128)}, f32[24,2304]{1,0:T(8,128)}, f32[24,768]{1,0:T(8,128)}, f32[24,3072]{1,0:T(8,128)}, /*...) custom-call(bf16[384,768]{1,0:T(8,128)(2,1)} %get-tuple-element.41.r, ...), custom_call_target="tpu_custom_call" | custom-call | tf_op jit(solution)/shard_map/format/pallas_call | solution.py:1589
